TPU v7x, 32 devices: a whole 2x2x4 slice. The times are simulated.
32 devices in a mesh: pipe: 4 (over x, core), ctx: 2 (over y), dp: 4 (over z).
Axes of the slice: x: 2, y: 2, z: 4, core: 2. Of those that a mesh axis runs over, the one named last changes fastest.
Arguments:
- section_held: bfloat16 [4, 4, 512, 1024], P('pipe', 'dp', 'ctx'), may hold values from -6 to 6
- segments: int32 [4, 4, 512], P('pipe', 'dp'), may hold values from 0 to 3, never falling along the last dimension, each value on 1 to 256 neighbouring positions
- norm_gain: float32 [4, 1024], P('pipe'), may hold values from 0.1 to 1.9
- w_qkv: bfloat16 [4, 1024, 1536], P('pipe')
- w_out: bfloat16 [4, 512, 1024], P('pipe'), may hold values from -1 to 1
- grad_parts: float32 [4, 2, 4, 524288], P('pipe', 'ctx', 'dp'), may hold values from -2 to 2
- master: float32 [4, 524288], P('pipe', ('ctx', 'dp')), may hold values from -0.25 to 0.25
- moment: float32 [4, 524288], P('pipe', ('ctx', 'dp')), may hold values from -4 to 4
- second: float32 [4, 524288], P('pipe', ('ctx', 'dp')), may hold values from 0.1 to 1
Outputs:
- section_next: bfloat16 [4, 4, 512, 1024], P('pipe', 'dp', 'ctx')
- new_master: float32 [4, 524288], P('pipe', ('ctx', 'dp'))
- new_moment: float32 [4, 524288], P('pipe', ('ctx', 'dp'))
- new_second: float32 [4, 524288], P('pipe', ('ctx', 'dp'))
Inputs may be any that keep to these rules, and one draw needn't show every extreme that they name: `segments`: within each sequence the ids never fall and each segment holds 1 to 256 tokens.
All inputs are finite; a program needn't handle non-finite values.
Results may differ from a plain program's by a relative error of at most 0.006.
Values may be sent and summed in bfloat16 or wider, within the bound.
No kernel may reach another device: no remote copies, remote signals or barrier semaphores. Data moves between devices by JAX's collectives and lax.ppermute only.
A program may use at most 64 MiB of HBM per device.

v0:
```python
import jax
import jax.numpy as jnp
from jax import lax
from jax.sharding import PartitionSpec as P

H = 4
DH = 128


eps_norm = 1e-06
rate = 0.001
beta_one = 0.9
beta_two = 0.999
adam_eps = 1e-08
decay = 0.1
fix_one = 0.9999734386011124
fix_two = 0.09520785288629038


def shifted(value, axis, by):
    count = lax.axis_size(axis)
    return lax.ppermute(value, axis, [(i, (i + by) % count) for i in range(count)])


def on_device(section_held, segments, norm_gain, w_qkv, w_out, grad_parts, master, moment, second):
    incoming = shifted(section_held, "pipe", 1)
    inputs = incoming[0, 0]
    row_count = inputs.shape[0]
    head_cols = H * DH
    values = inputs.astype(jnp.float32)
    meansq = jnp.mean(values * values, axis=-1, keepdims=True)
    normed = (values * lax.rsqrt(meansq + eps_norm) * norm_gain[0]).astype(jnp.bfloat16)
    projected = jnp.dot(normed, w_qkv[0], preferred_element_type=jnp.float32)
    queries = projected[:, :head_cols].astype(jnp.bfloat16).reshape(row_count, H, DH)
    key_rows = projected[:, head_cols : 2 * head_cols].astype(jnp.bfloat16)
    value_rows = projected[:, 2 * head_cols :].astype(jnp.bfloat16)
    seg_all = segments[0, 0]
    my_start = lax.axis_index("ctx") * row_count
    query_seg = lax.dynamic_slice_in_dim(seg_all, my_start, row_count)
    query_pos = my_start + jnp.arange(row_count, dtype=jnp.int32)
    score_scale = DH ** (-0.5)
    running = jnp.full((H, row_count), -1e30, jnp.float32)
    key_part = lax.all_gather(key_rows, "ctx", axis=0, tiled=True)
    value_part = lax.all_gather(value_rows, "ctx", axis=0, tiled=True)
    key_count = key_part.shape[0]
    key_heads = key_part.reshape(key_count, H, DH)
    value_heads = value_part.reshape(key_count, H, DH)
    scores = (
        jnp.einsum("qhd,khd->hqk", queries, key_heads, preferred_element_type=jnp.float32)
        * score_scale
    )
    key_pos = jnp.arange(key_count, dtype=jnp.int32)
    allowed = (key_pos[None, :] <= query_pos[:, None]) & (seg_all[None, :] == query_seg[:, None])
    scores = jnp.where(allowed[None], scores, -1e30)
    newest = jnp.maximum(running, jnp.max(scores, axis=-1))
    weights = jnp.where(allowed[None], jnp.exp(scores - newest[:, :, None]), 0.0)
    totals = jnp.sum(weights, axis=-1)
    weighted = jnp.einsum(
        "hqk,khd->hqd",
        weights.astype(jnp.bfloat16),
        value_heads,
        preferred_element_type=jnp.float32,
    )
    running, totals, weighted = (newest, totals, weighted)
    attended = (
        jnp.transpose(weighted / totals[:, :, None], (1, 0, 2))
        .reshape(row_count, head_cols)
        .astype(jnp.bfloat16)
    )
    section_next = (
        (jnp.dot(attended, w_out[0], preferred_element_type=jnp.float32) + values)
        .astype(jnp.bfloat16)
        .reshape(section_held.shape)
    )
    flat_grad = grad_parts.reshape(-1)
    grad_sum = lax.psum_scatter(flat_grad, ("ctx", "dp"), scatter_dimension=0, tiled=True)
    master_row = master[0]
    new_moment = beta_one * moment[0] + (1.0 - beta_one) * grad_sum
    new_second = beta_two * second[0] + (1.0 - beta_two) * grad_sum * grad_sum
    update = new_moment / fix_one / (jnp.sqrt(new_second / fix_two) + adam_eps) + decay * master_row
    new_master = master_row - rate * update
    return (
        section_next,
        new_master.reshape(master.shape),
        new_moment.reshape(moment.shape),
        new_second.reshape(second.shape),
    )


def solution(mesh):
    in_specs = (
        P("pipe", "dp", "ctx", None),
        P("pipe", "dp", None),
        P("pipe", None),
        P("pipe", None, None),
        P("pipe", None, None),
        P("pipe", "ctx", "dp", None),
        P("pipe", ("ctx", "dp")),
        P("pipe", ("ctx", "dp")),
        P("pipe", ("ctx", "dp")),
    )
    out_specs = (
        P("pipe", "dp", "ctx", None),
        P("pipe", ("ctx", "dp")),
        P("pipe", ("ctx", "dp")),
        P("pipe", ("ctx", "dp")),
    )
    return jax.shard_map(
        on_device, mesh=mesh, in_specs=in_specs, out_specs=out_specs, check_vma=False
    )
```

profile of v0, /device:TPU:0, one launch (start us, length us, event | category | flops | bytes accessed | tf_op | source)
XLA Modules:
  0.0 126.0 jit_solution(17509623936549251759)
XLA Ops:
  7.2 0.0 copy-start
  7.2 0.0 copy-start.7
  7.2 0.0 copy-start.4
  7.2 0.0 copy-start.5
  7.2 0.0 copy-start.6
  7.2 0.0 all-reduce.3.cloned.1.call-start
  7.3 0.5 collective-permute-start
  7.8 0.2 all-reduce.3.cloned.1.call-update
  8.0 0.3 copy-done.4
  8.3 1.0 broadcast_multiply_fusion.1
  9.3 1.9 %broadcast_multiply_fusion = f32[1,65536]{1,0:T(1,128)} fusion(f32[1,65536]{1,0:T(1,128)} %param.17), kind=kLoop, calls=%fused_computation.40 | loop fusion | flops 65536 | bytes 524288 | tf_op jit(solution)/shard_map/mul | solution.py:79
  11.2 0.0 copy-done.7
  11.2 0.6 dynamic-slice.1
  12.4 0.0 copy-done.5
  12.5 0.2 fusion.29
  12.7 4.2 %collective-permute-done = bf16[1,1,256,1024]{3,2,1,0:T(8,128)(2,1)} collective-permute-done((bf16[1,1,256,1024]{3,2,1,0:T(8,128)(2,1)}, bf16[1,1,256,1024]{3,2,1,0:T(8,128)(2,1)}, u32[]{:S(2)}, u32[]{:S(2)}) %collective-permute-start) | collective-permute-done | bytes 524320 | tf_op jit(solution)/shard_map/ppermute | solution.py:22
  16.9 1.2 fusion.13
  18.1 0.0 copy-done
  18.1 0.0 copy-done.6
  18.1 2.1 %fusion.2 = bf16[256,1536]{1,0:T(8,128)(2,1)S(1)} fusion(bf16[1,1024,1536]{2,1,0:T(8,128)(2,1)S(1)} %copy-done, bf16[1,1,256,1024]{3,2,1,0:T(8,128)(2,1)} %collective-permute-done, f32[1024]{0:T(1024)S(1)} %bitcast.75, f32[256]{0:T(256)S(1)} %add_rsqrt_fusion), kind=kOutput, calls=%fused_computation.2 | convolution fusion | flops 806748160 | bytes 4461568 | tf_op jit(solution)/shard_map/dot_general | solution.py:33
  20.2 0.8 slice_bitcast_fusion
  21.0 14.1 %all_gather.7 = bf16[512,512]{1,0:T(8,128)(2,1)} all-gather(bf16[256,512]{1,0:T(8,128)(2,1)S(1)} %get-tuple-element.8), channel_id=1, replica_groups=mesh['pipe'=4,'ctx'=2,'dp'=4] {'ctx'}, dimensions={0}, use_global_device_ids=true | all-gather | bytes 786432 | tf_op jit(solution)/shard_map/all_gather | solution.py:44
  35.1 2.1 %copy.19 = bf16[512,512]{0,1:T(8,128)(2,1)} copy(bf16[512,512]{1,0:T(8,128)(2,1)} %all_gather.7) | data formatting | bytes 1048576 | tf_op jit(solution)/shard_map/reshape | solution.py:47
  37.2 8.6 %all_gather.6 = bf16[512,512]{1,0:T(8,128)(2,1)S(1)} all-gather(bf16[256,512]{1,0:T(8,128)(2,1)S(1)} %get-tuple-element.9), channel_id=1, replica_groups=mesh['pipe'=4,'ctx'=2,'dp'=4] {'ctx'}, dimensions={0}, use_global_device_ids=true | all-gather | bytes 786432 | tf_op jit(solution)/shard_map/all_gather | solution.py:43
  45.7 0.0 copy-start.3
  45.7 1.6 %fusion.5 = (f32[4,256]{1,0:T(4,128)S(1)}, f32[4,256,512]{2,1,0:T(8,128)S(1)}) fusion(pred[256,512]{1,0:T(8,128)(4,1)S(1)} %fusion.29, bf16[32,4,8,128]{3,2,1,0:T(8,128)(2,1)} %get-tuple-element.7, bf16[512,512]{1,0:T(8,128)(2,1)S(1)} %all_gather.6), kind=kOutput, calls=%fused_computation.5 | convolution fusion | flops 135789568 | bytes 3018752 | tf_op jit(solution)/shard_map/qhd,khd->hqk/dot_general | solution.py:49
  47.3 0.8 fusion.6
  48.2 0.0 copy-done.3
  48.2 0.0 copy-start.1
  48.2 0.8 fusion.12
  49.0 0.0 copy-start.2
  49.0 0.4 copy-done.1
  49.4 2.3 %fusion.10 = bf16[1,1,256,1024]{3,2,1,0:T(8,128)(2,1)} fusion(bf16[1,1,256,1024]{3,2,1,0:T(8,128)(2,1)} %collective-permute-done, bf16[256,512]{0,1:T(8,128)(2,1)S(1)} %bitcast.67, bf16[1,512,1024]{2,1,0:T(8,128)(2,1)S(1)} %copy-done.1), kind=kOutput, calls=%fused_computation.13 | convolution fusion | flops 269221888 | bytes 2359296 | tf_op jit(solution)/shard_map/dot_general | solution.py:71
  51.7 65.3 %all-reduce.3.cloned.1.call-done = f32[524288]{0:T(1024)} async-done(((f32[524288]{0:T(1024)}), f32[524288]{0:T(1024)}) %all-reduce.3.cloned.1.call-update) | async-done | bytes 2097168
  117.0 0.0 copy-done.2
  117.0 2.1 %multiply_subtract_fusion = (f32[65536]{0:T(1024)}, f32[65536]{0:T(1024)}, f32[65536]{0:T(1024)}) fusion(f32[65536]{0:T(1024)} %bitcast.68, f32[65536]{0:T(1024)S(1)} %bitcast.64, f32[524288]{0:T(1024)} %all-reduce.3.cloned.1.call-done, u32[]{:T(128)S(6)} %multiply.9, f32[65536]{0:T(1024)} %bitcast.65), kind=kLoop, calls=%fused_computation.38 | loop fusion | flops 851968 | bytes 1835012 | tf_op jit(solution)/shard_map/sub | solution.py:81
  (4 shorter events, 0.0 us)
Async XLA Ops:
  7.2 11.0 %copy-start = (bf16[1,1024,1536]{2,1,0:T(8,128)(2,1)S(1)}, bf16[1,1024,1536]{2,1,0:T(8,128)(2,1)}, u32[]{:S(2)}) copy-start(bf16[1,1024,1536]{2,1,0:T(8,128)(2,1)} %param.12) | copy-start | bytes 9437188
  7.2 4.0 %copy-start.7 = (u32[32]{0:T(128)S(1)}, u32[32]{0:T(128)}, u32[]{:S(2)}) copy-start(u32[32]{0:T(128)} %constant.54) | copy-start | bytes 388
  7.2 1.1 copy-start.4
  7.2 5.2 %copy-start.5 = (s32[1,1,512]{2,1,0:T(1,128)S(1)}, s32[1,1,512]{2,1,0:T(1,128)}, u32[]{:S(2)}) copy-start(s32[1,1,512]{2,1,0:T(1,128)} %param.10) | copy-start | bytes 6148
  7.2 10.9 %copy-start.6 = (f32[1,1024]{1,0:T(1,128)S(1)}, f32[1,1024]{1,0:T(1,128)}, u32[]{:S(2)}) copy-start(f32[1,1024]{1,0:T(1,128)} %param.11) | copy-start | bytes 12292
  7.2 109.8 %all-reduce.3.cloned.1.call-start = ((), (), s32[]{:S(2)}) async-start(), calls=%async_computation | async-start | bytes 4194304
  7.3 9.6 %collective-permute-start = (bf16[1,1,256,1024]{3,2,1,0:T(8,128)(2,1)}, bf16[1,1,256,1024]{3,2,1,0:T(8,128)(2,1)}, u32[]{:S(2)}, u32[]{:S(2)}) collective-permute-start(bf16[1,1,256,1024]{3,2,1,0:T(8,128)(2,1)} %param.9), channel_id=1, source_target_pairs={{0,8},{8,16},{16,24},{24,0},{1,9},{9,17},{17,25},{25,1},{2,10},{10... | collective-permute-start | bytes 1572872 | tf_op jit(solution)/shard_map/ppermute | solution.py:22
  45.7 2.4 %copy-start.3 = (bf16[512,512]{0,1:T(8,128)(2,1)S(1)}, bf16[512,512]{0,1:T(8,128)(2,1)}, u32[]{:S(2)}) copy-start(bf16[512,512]{0,1:T(8,128)(2,1)} %copy.19) | copy-start | bytes 1572868
  48.2 1.2 copy-start.1
  49.0 68.0 %copy-start.2 = (f32[1,65536]{1,0:T(1,128)S(1)}, f32[1,65536]{1,0:T(1,128)}, u32[]{:S(2)}) copy-start(f32[1,65536]{1,0:T(1,128)} %broadcast_multiply_fusion.1) | copy-start | bytes 786436
Sparse Core Ops, SparseCore 0:
  11.7 105.3 all-reduce.2
where the time goes:
time: 126 us
  waiting for transfers between devices  69.7 us (55%)
  blocking collectives  22.7 us (18%)
  between operations  14.8 us (12%)
  other arithmetic  7.22 us (6%)
  matrix products  6.79 us (5%)
  local copies, waits for them, and re-layouts  4.18 us (3%)
    unnamed x2, waiting for transfers between devices  65.5 us
    all_gather x1, blocking collectives, on_device(): value_part = lax.all_gather(value_rows, 'ctx', axis=0, tiled=True)  14.1 us
    all_gather x1, blocking collectives, on_device(): key_part = lax.all_gather(key_rows, 'ctx', axis=0, tiled=True)  8.56 us
    ppermute x1, waiting for transfers between devices, shifted(): lax.ppermute(value, axis, [(i, (i + by) % count) for i in range(count)])  4.22 us
  transfers between devices with their start and end apart: 2, of which 2 were waited for; matrix products, arithmetic and copies ran while one was open for 12% of the time, Pallas kernels for 0%

commit v1 on v0

v1 whole, which is shorter than its diff:
```python
import jax
import jax.numpy as jnp
from jax import lax
from jax.sharding import PartitionSpec as P

H = 4
DH = 128


eps_norm = 1e-06
rate = 0.001
beta_one = 0.9
beta_two = 0.999
adam_eps = 1e-08
decay = 0.1
fix_one = 0.9999734386011124
fix_two = 0.09520785288629038
lane = 128
cuts = 2


def bits_of(count):
    return count.bit_length() - 1


def flipped(value, flips):
    axes = tuple(flips)
    sizes = [lax.axis_size(axis) for axis in axes]
    pairs = []
    if len(axes) == 1:
        pairs = [(i, i ^ flips[axes[0]]) for i in range(sizes[0])]
        return lax.ppermute(value, axes[0], pairs)
    for i in range(sizes[0]):
        for j in range(sizes[1]):
            pairs.append((i * sizes[1] + j, (i ^ flips[axes[0]]) * sizes[1] + (j ^ flips[axes[1]])))
    return lax.ppermute(value, axes, pairs)


def halve(value, axis, bit, dim):
    mine = (lax.axis_index(axis) >> bit) & 1
    sent = lax.dynamic_index_in_dim(value, 1 - mine, dim, keepdims=False).astype(jnp.bfloat16)
    kept = lax.dynamic_index_in_dim(value, mine, dim, keepdims=False)
    return kept, flipped(sent, {axis: 1 << bit})


def scattered_sum(part):
    ctx_bits, dp_bits = bits_of(lax.axis_size("ctx")), bits_of(lax.axis_size("dp"))
    order = [("ctx", b) for b in reversed(range(ctx_bits))] + [("dp", b) for b in reversed(range(dp_bits))]
    while len(order) > 2:
        axis, bit = order[-1]
        kept, got = halve(part, axis, bit, len(order) - 1)
        part = kept + got.astype(jnp.float32)
        order.pop()
    mine = [(lax.axis_index(axis) >> bit) & 1 for axis, bit in order]
    own = part
    for m in mine:
        own = lax.dynamic_index_in_dim(own, m, 0, keepdims=False)
    total = own
    for code in range(1, 1 << len(order)):
        chosen, flips = part, {}
        for place, (axis, bit) in enumerate(order):
            flip = (code >> place) & 1
            chosen = lax.dynamic_index_in_dim(chosen, mine[place] ^ flip, 0, keepdims=False)
            if flip:
                flips[axis] = flips.get(axis, 0) | (1 << bit)
        total = total + flipped(chosen.astype(jnp.bfloat16), flips).astype(jnp.float32)
    return total


def relayed(section_held, hop):
    pipes, ctxs = lax.axis_size("pipe"), lax.axis_size("ctx")
    pairs = [
        (p * ctxs + c, ((p + 1) % pipes) * ctxs + c + hop)
        for p in range(pipes)
        for c in range(ctxs - hop)
    ]
    return lax.ppermute(section_held, ("pipe", "ctx"), pairs)


def on_device(section_held, segments, norm_gain, w_qkv, w_out, grad_parts, master, moment, second):
    ctxs = lax.axis_size("ctx")
    row_count = section_held.shape[2]
    head_cols = H * DH
    blocks = [relayed(section_held, hop)[0, 0] for hop in range(ctxs)]

    count = grad_parts.shape[-1]
    shards = ctxs * lax.axis_size("dp")
    twos = (2,) * bits_of(shards)
    rows = count // shards // lane
    grads = grad_parts.reshape(twos + (rows, lane))
    step = rows // cuts
    grad_sum = jnp.concatenate(
        [scattered_sum(grads[..., i * step : (i + 1) * step, :]) for i in range(cuts)], axis=0
    ).reshape(-1)

    my_ctx = lax.axis_index("ctx")
    seg_all = segments[0, 0]

    def normed_of(block):
        values = block.astype(jnp.float32)
        meansq = jnp.mean(values * values, axis=-1, keepdims=True)
        return (values * lax.rsqrt(meansq + eps_norm) * norm_gain[0]).astype(jnp.bfloat16)

    def seg_of(hop):
        return lax.dynamic_slice_in_dim(seg_all, jnp.maximum(my_ctx - hop, 0) * row_count, row_count)

    own = blocks[0]
    projected = jnp.dot(normed_of(own), w_qkv[0], preferred_element_type=jnp.float32).astype(jnp.bfloat16)
    queries = projected[:, :head_cols].reshape(row_count, H, DH)
    keys, values = [projected[:, head_cols : 2 * head_cols]], [projected[:, 2 * head_cols :]]
    query_seg = seg_of(0)
    place = jnp.arange(row_count, dtype=jnp.int32)
    masks = [(place[None, :] <= place[:, None]) & (query_seg[None, :] == query_seg[:, None])]
    for hop in range(1, ctxs):
        both = jnp.dot(
            normed_of(blocks[hop]), w_qkv[0][:, head_cols:], preferred_element_type=jnp.float32
        ).astype(jnp.bfloat16)
        keys.append(both[:, :head_cols])
        values.append(both[:, head_cols:])
        masks.append((my_ctx >= hop) & (seg_of(hop)[None, :] == query_seg[:, None]))
    key_heads = jnp.concatenate(keys, axis=0).reshape(-1, H, DH)
    value_heads = jnp.concatenate(values, axis=0).reshape(-1, H, DH)
    allowed = jnp.concatenate(masks, axis=1)
    scores = (
        jnp.einsum("qhd,khd->hqk", queries, key_heads, preferred_element_type=jnp.float32)
        * DH ** (-0.5)
    )
    scores = jnp.where(allowed[None], scores, -1e30)
    newest = jnp.max(scores, axis=-1)
    weights = jnp.where(allowed[None], jnp.exp(scores - newest[:, :, None]), 0.0)
    totals = jnp.sum(weights, axis=-1)
    weighted = jnp.einsum(
        "hqk,khd->hqd",
        weights.astype(jnp.bfloat16),
        value_heads,
        preferred_element_type=jnp.float32,
    )
    attended = (
        jnp.transpose(weighted / totals[:, :, None], (1, 0, 2))
        .reshape(row_count, head_cols)
        .astype(jnp.bfloat16)
    )
    section_next = (
        (jnp.dot(attended, w_out[0], preferred_element_type=jnp.float32) + own.astype(jnp.float32))
        .astype(jnp.bfloat16)
        .reshape(section_held.shape)
    )

    master_row = master[0]
    new_moment = beta_one * moment[0] + (1.0 - beta_one) * grad_sum
    new_second = beta_two * second[0] + (1.0 - beta_two) * grad_sum * grad_sum
    update = new_moment / fix_one / (jnp.sqrt(new_second / fix_two) + adam_eps) + decay * master_row
    new_master = master_row - rate * update
    return (
        section_next,
        new_master.reshape(master.shape),
        new_moment.reshape(moment.shape),
        new_second.reshape(second.shape),
    )


def solution(mesh):
    in_specs = (
        P("pipe", "dp", "ctx", None),
        P("pipe", "dp", None),
        P("pipe", None),
        P("pipe", None, None),
        P("pipe", None, None),
        P("pipe", "ctx", "dp", None),
        P("pipe", ("ctx", "dp")),
        P("pipe", ("ctx", "dp")),
        P("pipe", ("ctx", "dp")),
    )
    out_specs = (
        P("pipe", "dp", "ctx", None),
        P("pipe", ("ctx", "dp")),
        P("pipe", ("ctx", "dp")),
        P("pipe", ("ctx", "dp")),
    )
    return jax.shard_map(
        on_device, mesh=mesh, in_specs=in_specs, out_specs=out_specs, check_vma=False
    )
```

time: 126 us -> 55.5 us (0.44)
  waiting for transfers between devices: 69.7 us -> 14.8 us
  blocking collectives: 22.7 us -> 0 us
  starting transfers between devices: 0.54 us -> 15.9 us
  between operations: 14.8 us -> 0.86 us
  matrix products: 6.79 us -> 11.7 us
    unnamed x2 -> x0, waiting for transfers between devices: 65.5 us -> none
    all_gather x2 -> x0, blocking collectives: 22.7 us -> none  [the longest x1 14.1 us: on_device(): value_part = lax.all_gather(value_rows, 'ctx', axis=0, tiled=True)]
    ppermute x1 -> x10, starting transfers between devices: 0.5 us -> 15.9 us  [the longest x6 7.52 us: flipped(): return lax.ppermute(value, axes[0], pairs)]
    ppermute x1 -> x10, waiting for transfers between devices: 4.22 us -> 14.8 us  [the longest x6 10.4 us: flipped(): return lax.ppermute(value, axes[0], pairs)]
    mul x2 -> x0, other arithmetic: 2.89 us -> none  [the longest x1 1.92 us: on_device(): new_second = beta_two * second[0] + (1.0 - beta_two) * grad_sum * grad_sum]
    sub x0 -> x1, matrix products: none -> 2.09 us  [on_device(): scores - newest[:, :, None]]
    dot_general x2 -> x3, matrix products: 4.39 us -> 6.26 us  [the longest x1 2.3 us: on_device(): jnp.dot(attended, w_out[0], preferred_element_type=jnp.float32)]
    slice x0 -> x2, local copies, waits for them, and re-layouts: none -> 1.74 us  [the longest x1 1.7 us: on_device(): grads[..., i * step:(i + 1) * step, :]]
  transfers between devices with their start and end apart: 2 -> 10, of which waited for: 2 -> 7; matrix products, arithmetic and copies ran while one was open for 12% -> 19% of each run, Pallas kernels for 0% -> 0%
where the time goes in v1:
time: 55.5 us; the launch traced here: 55 us
  starting transfers between devices  15.9 us (29%)
  waiting for transfers between devices  14.8 us (27%)
  matrix products  11.7 us (21%)
  other arithmetic  6.46 us (12%)
  local copies, waits for them, and re-layouts  5.19 us (9%)
  between operations  0.86 us (2%)
    ppermute x6, waiting for transfers between devices, flipped(): return lax.ppermute(value, axes[0], pairs)  10.4 us
    ppermute x6, starting transfers between devices, flipped(): return lax.ppermute(value, axes[0], pairs)  7.52 us
    ppermute x2, starting transfers between devices, relayed(): return lax.ppermute(section_held, ('pipe', 'ctx'), pairs)  6.91 us
    ppermute x2, waiting for transfers between devices, flipped(): return lax.ppermute(value, axes, pairs)  4.4 us
    sub x1, other arithmetic, on_device(): new_master = master_row - rate * update  2.66 us
    reduce_sum x2, other arithmetic, normed_of(): meansq = jnp.mean(values * values, axis=-1, keepdims=True)  2.45 us
    dot_general x1, matrix products, on_device(): jnp.dot(attended, w_out[0], preferred_element_type=jnp.float32)  2.3 us
    dot_general x1, matrix products, on_device(): jnp.dot(normed_of(own), w_qkv[0], preferred_element_type=jnp.float32)  2.14 us
  transfers between devices with their start and end apart: 10, of which 7 were waited for; matrix products, arithmetic and copies ran while one was open for 19% of the time, Pallas kernels for 0%

profile of v1, /device:TPU:0, one launch (start us, length us, event | category | flops | bytes accessed | tf_op | source)
XLA Modules:
  0.0 55.0 jit_solution(14926909112283950483)
XLA Ops:
  0.6 0.0 copy-start
  0.6 0.5 collective-permute-start
  1.2 6.4 %collective-permute-start.1 = (bf16[1,1,256,1024]{3,2,1,0:T(8,128)(2,1)}, bf16[1,1,256,1024]{3,2,1,0:T(8,128)(2,1)}, u32[]{:S(2)}, u32[]{:S(2)}) collective-permute-start(bf16[1,1,256,1024]{3,2,1,0:T(8,128)(2,1)} %param.9), channel_id=1, source_target_pairs={{0,12},{8,20},{16,28},{24,4},{1,13},{9,21},{17,29},{25,5},{2,14},{... | collective-permute-start | bytes 1572872 | tf_op jit(solution)/shard_map/ppermute | solution.py:77
  7.6 1.7 %fusion.68 = (f32[2,2,2,256,128]{4,3,2,1,0:T(8,128)S(1)}, f32[2,2,2,256,128]{4,3,2,1,0:T(8,128)S(1)}) fusion(f32[2,2,2,512,128]{4,3,2,1,0:T(8,128)} %bitcast.117), kind=kLoop, calls=%fused_computation.88 | loop fusion | bytes 4194304 | tf_op jit(solution)/shard_map/slice | solution.py:93
  9.3 0.7 %fusion.36 = bf16[2,2,256,128]{3,2,1,0:T(8,128)(2,1)} fusion(f32[2,2,2,256,128]{4,3,2,1,0:T(8,128)S(1)} %get-tuple-element.8, s32[]{:T(128)S(6)} %select_n.61), kind=kLoop, calls=%fused_computation.49 | loop fusion | bytes 524292 | tf_op jit(solution)/shard_map/convert_element_type | solution.py:41
  10.0 1.6 %collective-permute-start.6 = (bf16[2,2,256,128]{3,2,1,0:T(8,128)(2,1)}, bf16[2,2,256,128]{3,2,1,0:T(8,128)(2,1)}, u32[]{:S(2)}, u32[]{:S(2)}) collective-permute-start(bf16[2,2,256,128]{3,2,1,0:T(8,128)(2,1)} %fusion.36), channel_id=1, source_target_pairs={{0,1},{1,0},{2,3},{3,2},{4,5},{5,4},{6,7},{7,6},{8,9},{9,8},{10,11... | collective-permute-start | bytes 786440 | tf_op jit(solution)/shard_map/ppermute | solution.py:32
  11.6 0.7 %fusion.35 = bf16[2,2,256,128]{3,2,1,0:T(8,128)(2,1)} fusion(f32[2,2,2,256,128]{4,3,2,1,0:T(8,128)S(1)} %get-tuple-element.7, s32[]{:T(128)S(6)} %select_n.61), kind=kLoop, calls=%fused_computation.48 | loop fusion | bytes 524292 | tf_op jit(solution)/shard_map/convert_element_type | solution.py:41
  12.3 0.4 collective-permute-start.2
  12.8 0.0 copy-done.4
  12.8 0.1 fusion.39
  13.0 6.5 %collective-permute-done.6 = bf16[2,2,256,128]{3,2,1,0:T(8,128)(2,1)} collective-permute-done((bf16[2,2,256,128]{3,2,1,0:T(8,128)(2,1)}, bf16[2,2,256,128]{3,2,1,0:T(8,128)(2,1)}, u32[]{:S(2)}, u32[]{:S(2)}) %collective-permute-start.6) | collective-permute-done | bytes 262176 | tf_op jit(solution)/shard_map/ppermute | solution.py:32
  19.5 1.0 %bitcast_add_fusion = f32[2,2,256,128]{3,2,1,0:T(8,128)S(1)} fusion(bf16[2,2,256,128]{3,2,1,0:T(8,128)(2,1)} %collective-permute-done.6, f32[2,2,2,256,128]{4,3,2,1,0:T(8,128)S(1)} %get-tuple-element.8, s32[]{:T(128)S(6)} %select_n.60), kind=kLoop, calls=%fused_computation.37 | loop fusion | flops 262144 | bytes 1310724 | tf_op jit(solution)/shard_map/add | solution.py:52
  20.5 0.0 copy-start.1
  20.5 0.0 copy-start.2
  20.5 0.0 copy-start.3
  20.6 0.1 collective-permute-start.9
  20.7 2.7 %collective-permute-start.8 = (bf16[256,128]{1,0:T(8,128)(2,1)S(1)}, bf16[256,128]{1,0:T(8,128)(2,1)S(1)}, u32[]{:S(2)}, u32[]{:S(2)}) collective-permute-start(bf16[256,128]{1,0:T(8,128)(2,1)S(1)} %get-tuple-element.17), channel_id=1, source_target_pairs={{0,2},{1,3},{2,0},{3,1},{4,6},{5,7},{6,4},{7,5},{8,10},{9,11},{10,... | collective-permute-start | bytes 196616 | tf_op jit(solution)/shard_map/ppermute | solution.py:32
  23.3 3.1 %collective-permute-done.2 = bf16[2,2,256,128]{3,2,1,0:T(8,128)(2,1)S(1)} collective-permute-done((bf16[2,2,256,128]{3,2,1,0:T(8,128)(2,1)}, bf16[2,2,256,128]{3,2,1,0:T(8,128)(2,1)S(1)}, u32[]{:S(2)}, u32[]{:S(2)}) %collective-permute-start.2) | collective-permute-done | bytes 262176 | tf_op jit(solution)/shard_map/ppermute | solution.py:32
  26.4 0.0 collective-permute-start.7
  26.5 0.0 copy-start.5
  26.5 0.0 copy-start.6
  26.6 1.8 %collective-permute-done.9 = bf16[256,128]{1,0:T(8,128)(2,1)S(1)} collective-permute-done((bf16[256,128]{1,0:T(8,128)(2,1)S(1)}, bf16[256,128]{1,0:T(8,128)(2,1)S(1)}, u32[]{:S(2)}, u32[]{:S(2)}) %collective-permute-start.9) | collective-permute-done | bytes 65568 | tf_op jit(solution)/shard_map/ppermute | solution.py:36
  28.3 1.4 %collective-permute-start.5 = (bf16[256,128]{1,0:T(8,128)(2,1)S(1)}, bf16[256,128]{1,0:T(8,128)(2,1)S(1)}, u32[]{:S(2)}, u32[]{:S(2)}) collective-permute-start(bf16[256,128]{1,0:T(8,128)(2,1)S(1)} %get-tuple-element.13), channel_id=1, source_target_pairs={{0,6},{1,7},{2,4},{3,5},{4,2},{5,3},{6,0},{7,1},{8,14},{9,15},{10,... | collective-permute-start | bytes 196616 | tf_op jit(solution)/shard_map/ppermute | solution.py:36
  29.7 0.0 collective-permute-done.8
  29.7 1.3 %collective-permute-start.4 = (bf16[256,128]{1,0:T(8,128)(2,1)S(1)}, bf16[256,128]{1,0:T(8,128)(2,1)S(1)}, u32[]{:S(2)}, u32[]{:S(2)}) collective-permute-start(bf16[256,128]{1,0:T(8,128)(2,1)S(1)} %get-tuple-element.14), channel_id=1, source_target_pairs={{0,2},{1,3},{2,0},{3,1},{4,6},{5,7},{6,4},{7,5},{8,10},{9,11},{10,... | collective-permute-start | bytes 196616 | tf_op jit(solution)/shard_map/ppermute | solution.py:32
  31.0 0.2 collective-permute-done.7
  31.2 1.5 %collective-permute-start.3 = (bf16[256,128]{1,0:T(8,128)(2,1)S(1)}, bf16[256,128]{1,0:T(8,128)(2,1)S(1)}, u32[]{:S(2)}, u32[]{:S(2)}) collective-permute-start(bf16[256,128]{1,0:T(8,128)(2,1)S(1)} %get-tuple-element.12), channel_id=1, source_target_pairs={{0,4},{4,0},{1,5},{5,1},{2,6},{6,2},{3,7},{7,3},{8,12},{12,8},{9,1... | collective-permute-start | bytes 196616 | tf_op jit(solution)/shard_map/ppermute | solution.py:32
  32.8 2.6 %collective-permute-done.5 = bf16[256,128]{1,0:T(8,128)(2,1)S(1)} collective-permute-done((bf16[256,128]{1,0:T(8,128)(2,1)S(1)}, bf16[256,128]{1,0:T(8,128)(2,1)S(1)}, u32[]{:S(2)}, u32[]{:S(2)}) %collective-permute-start.5) | collective-permute-done | bytes 65568 | tf_op jit(solution)/shard_map/ppermute | solution.py:36
  35.4 0.2 collective-permute-done.4
  35.6 0.4 collective-permute-done.3
  36.1 0.0 copy-done.1
  36.1 0.0 copy-done.2
  36.1 2.7 %multiply_subtract_fusion = (f32[1,65536]{1,0:T(1,128)}, f32[1,65536]{1,0:T(1,128)}, f32[1,65536]{1,0:T(1,128)}) fusion(f32[1,65536]{1,0:T(1,128)S(1)} %copy-done.1, f32[1,65536]{1,0:T(1,128)S(1)} %bitcast.118, f32[1,65536]{1,0:T(1,128)S(1)} %copy-done.2, f32[1,65536]{1,0:T(1,128)S(1)} %copy-done.3), kind=kLoop, calls=%fused_computation.54 | loop fusion | flops 983040 | bytes 1835008 | tf_op jit(solution)/shard_map/sub | solution.py:153
  38.8 0.0 collective-permute-done.1
  38.8 1.2 %fusion.15 = f32[256]{0:T(256)S(1)} fusion(bf16[1,1,256,1024]{3,2,1,0:T(8,128)(2,1)} %collective-permute-done.1), kind=kLoop, calls=%fused_computation.22 | loop fusion | flops 786176 | bytes 525312 | tf_op jit(solution)/shard_map/reduce_sum | solution.py:101
  40.0 0.0 copy-done.5
  40.0 0.0 copy-done.6
  40.0 1.8 %fusion.5 = bf16[256,1024]{1,0:T(8,128)(2,1)S(1)} fusion(bf16[1024,1536]{1,0:T(8,128)(2,1)S(1)} %bitcast.123, bf16[1,1,256,1024]{3,2,1,0:T(8,128)(2,1)} %collective-permute-done.1, f32[1024]{0:T(1024)S(1)} %bitcast.124, f32[256]{0:T(256)S(1)} %add_rsqrt_fusion), kind=kOutput, calls=%fused_computation.13 | convolution fusion | flops 538181632 | bytes 3150848 | tf_op jit(solution)/shard_map/dot_general | solution.py:115
  41.9 0.0 collective-permute-done
  41.9 1.2 %fusion.12 = f32[256]{0:T(256)S(1)} fusion(bf16[1,1,256,1024]{3,2,1,0:T(8,128)(2,1)} %collective-permute-done), kind=kLoop, calls=%fused_computation.19 | loop fusion | flops 786176 | bytes 525312 | tf_op jit(solution)/shard_map/reduce_sum | solution.py:101
  43.2 2.1 %convolution_convert_fusion = bf16[256,1536]{1,0:T(8,128)(2,1)S(1)} fusion(bf16[1,1,256,1024]{3,2,1,0:T(8,128)(2,1)} %collective-permute-done, f32[1024]{0:T(1024)S(1)} %bitcast.125, f32[256]{0:T(256)S(1)} %add_rsqrt_fusion.1, bf16[1,1024,1536]{2,1,0:T(8,128)(2,1)S(1)} %copy-done.5), kind=kOutput, calls=%fused_computation.1 | convolution fusion | flops 806748160 | bytes 4461568 | tf_op jit(solution)/shard_map/dot_general | solution.py:108
  45.3 0.8 %slice_bitcast_fusion = (bf16[32,4,8,128]{3,2,1,0:T(8,128)(2,1)}, bf16[256,512]{1,0:T(8,128)(2,1)S(1)}, bf16[256,512]{1,0:T(8,128)(2,1)}) fusion(bf16[256,1536]{1,0:T(8,128)(2,1)S(1)} %convolution_convert_fusion), kind=kLoop, calls=%fused_computation.52 | loop fusion | bytes 1572864
  46.2 1.0 %copy.18 = bf16[512,512]{0,1:T(8,128)(2,1)} copy(bf16[512,512]{1,0:T(8,128)(2,1)S(1)} %pad_maximum_fusion) | data formatting | bytes 1048576 | tf_op jit(solution)/shard_map/reshape | solution.py:122
  47.2 1.5 %fusion.26 = f32[4,256,512]{2,1,0:T(8,128)S(1)} fusion(bf16[32,4,8,128]{3,2,1,0:T(8,128)(2,1)} %get-tuple-element.9, bf16[256,512]{1,0:T(8,128)(2,1)S(1)} %get-tuple-element.18, bf16[256,512]{1,0:T(8,128)(2,1)} %get-tuple-element.11), kind=kOutput, calls=%fused_computation.31 | convolution fusion | flops 135266304 | bytes 2883584 | tf_op jit(solution)/shard_map/qhd,khd->hqk/dot_general | solution.py:125
  48.6 2.1 %fusion.70 = f32[4,256]{1,0:T(4,128)S(1)} fusion(pred[256,512]{1,0:T(8,128)(4,1)S(1)} %pad_add_fusion, bf16[32,4,8,128]{3,2,1,0:T(8,128)(2,1)} %get-tuple-element.9, bf16[256,512]{1,0:T(8,128)(2,1)S(1)} %get-tuple-element.18, bf16[256,512]{1,0:T(8,128)(2,1)} %get-tuple-element.11), kind=kOutput, calls=%fused_computation.90 | convolution fusion | flops 137888256 | bytes 921600 | tf_op jit(solution)/shard_map/sub | solution.py:130
  50.7 1.9 %fusion.11 = bf16[256,4,128]{0,2,1:T(8,128)(2,1)S(1)} fusion(bf16[512,4,128]{0,2,1:T(8,128)(2,1)} %bitcast.119, f32[256,4]{0,1:T(4,128)S(1)} %bitcast.126, f32[4,256,512]{2,1,0:T(8,128)S(1)} %fusion.26, pred[256,512]{1,0:T(8,128)(4,1)S(1)} %pad_add_fusion), kind=kOutput, calls=%fused_computation.18 | convolution fusion | flops 137102848 | bytes 3018752 | tf_op jit(solution)/shard_map/hqk,khd->hqd/dot_general | solution.py:132
  52.7 0.0 copy-done
  52.7 2.3 %fusion.9 = bf16[1,1,256,1024]{3,2,1,0:T(8,128)(2,1)} fusion(bf16[1,1,256,1024]{3,2,1,0:T(8,128)(2,1)} %collective-permute-done, bf16[256,512]{0,1:T(8,128)(2,1)S(1)} %bitcast.120, bf16[1,512,1024]{2,1,0:T(8,128)(2,1)S(1)} %copy-done), kind=kOutput, calls=%fused_computation.15 | convolution fusion | flops 269221888 | bytes 2359296 | tf_op jit(solution)/shard_map/dot_general | solution.py:144
  (14 shorter events, 0.3 us)
Async XLA Ops:
  0.6 52.1 %copy-start = (bf16[1,512,1024]{2,1,0:T(8,128)(2,1)S(1)}, bf16[1,512,1024]{2,1,0:T(8,128)(2,1)}, u32[]{:S(2)}) copy-start(bf16[1,512,1024]{2,1,0:T(8,128)(2,1)} %param.13) | copy-start | bytes 3145732
  0.6 41.3 %collective-permute-start = (bf16[1,1,256,1024]{3,2,1,0:T(8,128)(2,1)}, bf16[1,1,256,1024]{3,2,1,0:T(8,128)(2,1)}, u32[]{:S(2)}, u32[]{:S(2)}) collective-permute-start(bf16[1,1,256,1024]{3,2,1,0:T(8,128)(2,1)} %param.9), channel_id=1, source_target_pairs={{0,8},{4,12},{8,16},{12,20},{16,24},{20,28},{24,0},{28,4},{1,9},{5... | collective-permute-start | bytes 1572872 | tf_op jit(solution)/shard_map/ppermute | solution.py:77
  1.2 37.6 %collective-permute-start.1 = (bf16[1,1,256,1024]{3,2,1,0:T(8,128)(2,1)}, bf16[1,1,256,1024]{3,2,1,0:T(8,128)(2,1)}, u32[]{:S(2)}, u32[]{:S(2)}) collective-permute-start(bf16[1,1,256,1024]{3,2,1,0:T(8,128)(2,1)} %param.9), channel_id=1, source_target_pairs={{0,12},{8,20},{16,28},{24,4},{1,13},{9,21},{17,29},{25,5},{2,14},{... | collective-permute-start | bytes 1572872 | tf_op jit(solution)/shard_map/ppermute | solution.py:77
  7.6 5.2 %copy-start.4 = (s32[1,1,512]{2,1,0:T(1,128)S(1)}, s32[1,1,512]{2,1,0:T(1,128)}, u32[]{:S(2)}) copy-start(s32[1,1,512]{2,1,0:T(1,128)} %param.10) | copy-start | bytes 6148
  10.0 9.5 %collective-permute-start.6 = (bf16[2,2,256,128]{3,2,1,0:T(8,128)(2,1)}, bf16[2,2,256,128]{3,2,1,0:T(8,128)(2,1)}, u32[]{:S(2)}, u32[]{:S(2)}) collective-permute-start(bf16[2,2,256,128]{3,2,1,0:T(8,128)(2,1)} %fusion.36), channel_id=1, source_target_pairs={{0,1},{1,0},{2,3},{3,2},{4,5},{5,4},{6,7},{7,6},{8,9},{9,8},{10,11... | collective-permute-start | bytes 786440 | tf_op jit(solution)/shard_map/ppermute | solution.py:32
  12.3 14.1 %collective-permute-start.2 = (bf16[2,2,256,128]{3,2,1,0:T(8,128)(2,1)}, bf16[2,2,256,128]{3,2,1,0:T(8,128)(2,1)S(1)}, u32[]{:S(2)}, u32[]{:S(2)}) collective-permute-start(bf16[2,2,256,128]{3,2,1,0:T(8,128)(2,1)} %fusion.35), channel_id=1, source_target_pairs={{0,1},{1,0},{2,3},{3,2},{4,5},{5,4},{6,7},{7,6},{8,9},{9,8},{10,11... | collective-permute-start | bytes 786440 | tf_op jit(solution)/shard_map/ppermute | solution.py:32
  20.5 15.6 %copy-start.1 = (f32[1,65536]{1,0:T(1,128)S(1)}, f32[1,65536]{1,0:T(1,128)}, u32[]{:S(2)}) copy-start(f32[1,65536]{1,0:T(1,128)} %param.15) | copy-start | bytes 786436
  20.5 15.6 %copy-start.2 = (f32[1,65536]{1,0:T(1,128)S(1)}, f32[1,65536]{1,0:T(1,128)}, u32[]{:S(2)}) copy-start(f32[1,65536]{1,0:T(1,128)} %param.16) | copy-start | bytes 786436
  20.5 15.6 %copy-start.3 = (f32[1,65536]{1,0:T(1,128)S(1)}, f32[1,65536]{1,0:T(1,128)}, u32[]{:S(2)}) copy-start(f32[1,65536]{1,0:T(1,128)} %param.17) | copy-start | bytes 786436
  20.6 7.7 %collective-permute-start.9 = (bf16[256,128]{1,0:T(8,128)(2,1)S(1)}, bf16[256,128]{1,0:T(8,128)(2,1)S(1)}, u32[]{:S(2)}, u32[]{:S(2)}) collective-permute-start(bf16[256,128]{1,0:T(8,128)(2,1)S(1)} %get-tuple-element.16), channel_id=1, source_target_pairs={{0,6},{1,7},{2,4},{3,5},{4,2},{5,3},{6,0},{7,1},{8,14},{9,15},{10,... | collective-permute-start | bytes 196616 | tf_op jit(solution)/shard_map/ppermute | solution.py:36
  20.7 9.1 %collective-permute-start.8 = (bf16[256,128]{1,0:T(8,128)(2,1)S(1)}, bf16[256,128]{1,0:T(8,128)(2,1)S(1)}, u32[]{:S(2)}, u32[]{:S(2)}) collective-permute-start(bf16[256,128]{1,0:T(8,128)(2,1)S(1)} %get-tuple-element.17), channel_id=1, source_target_pairs={{0,2},{1,3},{2,0},{3,1},{4,6},{5,7},{6,4},{7,5},{8,10},{9,11},{10,... | collective-permute-start | bytes 196616 | tf_op jit(solution)/shard_map/ppermute | solution.py:32
  26.4 4.8 %collective-permute-start.7 = (bf16[256,128]{1,0:T(8,128)(2,1)S(1)}, bf16[256,128]{1,0:T(8,128)(2,1)S(1)}, u32[]{:S(2)}, u32[]{:S(2)}) collective-permute-start(bf16[256,128]{1,0:T(8,128)(2,1)S(1)} %get-tuple-element.15), channel_id=1, source_target_pairs={{0,4},{4,0},{1,5},{5,1},{2,6},{6,2},{3,7},{7,3},{8,12},{12,8},{9,1... | collective-permute-start | bytes 196616 | tf_op jit(solution)/shard_map/ppermute | solution.py:32
  26.5 13.5 %copy-start.5 = (bf16[1,1024,1536]{2,1,0:T(8,128)(2,1)S(1)}, bf16[1,1024,1536]{2,1,0:T(8,128)(2,1)}, u32[]{:S(2)}) copy-start(bf16[1,1024,1536]{2,1,0:T(8,128)(2,1)} %param.12) | copy-start | bytes 9437188
  26.5 13.5 %copy-start.6 = (f32[1,1024]{1,0:T(1,128)S(1)}, f32[1,1024]{1,0:T(1,128)}, u32[]{:S(2)}) copy-start(f32[1,1024]{1,0:T(1,128)} %param.11) | copy-start | bytes 12292
  28.3 7.0 %collective-permute-start.5 = (bf16[256,128]{1,0:T(8,128)(2,1)S(1)}, bf16[256,128]{1,0:T(8,128)(2,1)S(1)}, u32[]{:S(2)}, u32[]{:S(2)}) collective-permute-start(bf16[256,128]{1,0:T(8,128)(2,1)S(1)} %get-tuple-element.13), channel_id=1, source_target_pairs={{0,6},{1,7},{2,4},{3,5},{4,2},{5,3},{6,0},{7,1},{8,14},{9,15},{10,... | collective-permute-start | bytes 196616 | tf_op jit(solution)/shard_map/ppermute | solution.py:36
  29.7 5.9 %collective-permute-start.4 = (bf16[256,128]{1,0:T(8,128)(2,1)S(1)}, bf16[256,128]{1,0:T(8,128)(2,1)S(1)}, u32[]{:S(2)}, u32[]{:S(2)}) collective-permute-start(bf16[256,128]{1,0:T(8,128)(2,1)S(1)} %get-tuple-element.14), channel_id=1, source_target_pairs={{0,2},{1,3},{2,0},{3,1},{4,6},{5,7},{6,4},{7,5},{8,10},{9,11},{10,... | collective-permute-start | bytes 196616 | tf_op jit(solution)/shard_map/ppermute | solution.py:32
  31.2 4.8 %collective-permute-start.3 = (bf16[256,128]{1,0:T(8,128)(2,1)S(1)}, bf16[256,128]{1,0:T(8,128)(2,1)S(1)}, u32[]{:S(2)}, u32[]{:S(2)}) collective-permute-start(bf16[256,128]{1,0:T(8,128)(2,1)S(1)} %get-tuple-element.12), channel_id=1, source_target_pairs={{0,4},{4,0},{1,5},{5,1},{2,6},{6,2},{3,7},{7,3},{8,12},{12,8},{9,1... | collective-permute-start | bytes 196616 | tf_op jit(solution)/shard_map/ppermute | solution.py:32

commit v2 on v1

v2 whole, which is shorter than its diff:
```python
import functools

import jax
import jax.numpy as jnp
from jax import lax
from jax.experimental import pallas as pl
from jax.experimental.pallas import tpu as pltpu
from jax.sharding import PartitionSpec as P

H = 4
DH = 128


eps_norm = 1e-06
rate = 0.001
beta_one = 0.9
beta_two = 0.999
adam_eps = 1e-08
decay = 0.1
fix_one = 0.9999734386011124
fix_two = 0.09520785288629038
lane = 128
cuts = 2


def bits_of(count):
    return count.bit_length() - 1


def flipped(value, flips):
    axes = tuple(flips)
    sizes = [lax.axis_size(axis) for axis in axes]
    pairs = []
    if len(axes) == 1:
        pairs = [(i, i ^ flips[axes[0]]) for i in range(sizes[0])]
        return lax.ppermute(value, axes[0], pairs)
    for i in range(sizes[0]):
        for j in range(sizes[1]):
            pairs.append((i * sizes[1] + j, (i ^ flips[axes[0]]) * sizes[1] + (j ^ flips[axes[1]])))
    return lax.ppermute(value, axes, pairs)


def halve(value, axis, bit, dim):
    mine = (lax.axis_index(axis) >> bit) & 1
    sent = lax.dynamic_index_in_dim(value, 1 - mine, dim, keepdims=False).astype(jnp.bfloat16)
    kept = lax.dynamic_index_in_dim(value, mine, dim, keepdims=False)
    return kept, flipped(sent, {axis: 1 << bit})


def after(value, *others):
    return lax.optimization_barrier((value, *others))[0]


def scatter_order():
    ctx_bits, dp_bits = bits_of(lax.axis_size("ctx")), bits_of(lax.axis_size("dp"))
    return [("ctx", b) for b in reversed(range(ctx_bits))] + [("dp", b) for b in reversed(range(dp_bits))]


def halved(part, order):
    while len(order) > 3:
        axis, bit = order[-1]
        kept, got = halve(part, axis, bit, len(order) - 1)
        part = kept + got.astype(jnp.float32)
        order = order[:-1]
    axis, bit = order[-1]
    return halve(part, axis, bit, len(order) - 1)


def exchanged(part, order):
    mine = [(lax.axis_index(axis) >> bit) & 1 for axis, bit in order]
    own = part
    for m in mine:
        own = lax.dynamic_index_in_dim(own, m, 0, keepdims=False)
    got = []
    for code in reversed(range(1, 1 << len(order))):
        chosen, flips = part, {}
        for place, (axis, bit) in enumerate(order):
            flip = (code >> (len(order) - 1 - place)) & 1
            chosen = lax.dynamic_index_in_dim(chosen, mine[place] ^ flip, 0, keepdims=False)
            if flip:
                flips[axis] = flips.get(axis, 0) | (1 << bit)
        got.append(flipped(chosen.astype(jnp.bfloat16), flips))
    return own, got


def relayed(section_held, hop):
    pipes, ctxs = lax.axis_size("pipe"), lax.axis_size("ctx")
    pairs = [
        (p * ctxs + c, ((p + 1) % pipes) * ctxs + c + hop)
        for p in range(pipes)
        for c in range(ctxs - hop)
    ]
    return lax.ppermute(section_held, ("pipe", "ctx"), pairs)


def normed_rows(block, gain):
    values = block.astype(jnp.float32)
    meansq = jnp.mean(values * values, axis=-1, keepdims=True)
    return (values * lax.rsqrt(meansq + eps_norm) * gain).astype(jnp.bfloat16)


def project_kernel(rows_ref, gain_ref, w_ref, out_ref):
    normed = normed_rows(rows_ref[...], gain_ref[...])
    out_ref[...] = jnp.dot(normed, w_ref[...], preferred_element_type=jnp.float32).astype(jnp.bfloat16)


def attend_kernel(ctxs, ctx_ref, own_ref, qkv_ref, seg_ref, gain_ref, w_ref, w_out_ref, *refs):
    earlier, out_ref = refs[:-1], refs[-1]
    rows = own_ref.shape[0]
    head_cols = H * DH
    my_ctx = ctx_ref[0]

    def seg_of(hop):
        start = pl.multiple_of(jnp.maximum(my_ctx - hop, 0) * rows, rows)
        return seg_ref[:, pl.ds(start, rows)]

    across = lax.broadcasted_iota(jnp.int32, (rows, rows), 1)
    down = lax.broadcasted_iota(jnp.int32, (rows, rows), 0)
    own_seg = seg_of(0)
    query_seg = jnp.sum(jnp.where(across == down, own_seg, 0), axis=1, keepdims=True)
    masks = [(across <= down) & (own_seg == query_seg)]
    keys = [qkv_ref[:, head_cols : 2 * head_cols]]
    values = [qkv_ref[:, 2 * head_cols :]]
    for hop in range(1, ctxs):
        normed = normed_rows(earlier[hop - 1][...], gain_ref[...])
        both = jnp.dot(normed, w_ref[:, head_cols:], preferred_element_type=jnp.float32).astype(jnp.bfloat16)
        keys.append(both[:, :head_cols])
        values.append(both[:, head_cols:])
        masks.append((seg_of(hop) == query_seg) & (my_ctx >= hop))
    heads = []
    for h in range(H):
        cols = slice(h * DH, (h + 1) * DH)
        queries = qkv_ref[:, cols]
        scores = [
            jnp.where(
                mask,
                lax.dot_general(
                    queries, key[:, cols], (((1,), (1,)), ((), ())), preferred_element_type=jnp.float32
                )
                * DH ** (-0.5),
                -1e30,
            )
            for key, mask in zip(keys, masks)
        ]
        top = functools.reduce(jnp.maximum, [jnp.max(s, axis=1, keepdims=True) for s in scores])
        total, summed = 0.0, 0.0
        for score, value in zip(scores, values):
            weights = jnp.exp(score - top)
            total = total + jnp.sum(weights, axis=1, keepdims=True)
            summed = summed + jnp.dot(
                weights.astype(jnp.bfloat16), value[:, cols], preferred_element_type=jnp.float32
            )
        heads.append((summed / total).astype(jnp.bfloat16))
    attended = jnp.concatenate(heads, axis=1)
    out_ref[...] = (
        jnp.dot(attended, w_out_ref[...], preferred_element_type=jnp.float32)
        + own_ref[...].astype(jnp.float32)
    ).astype(jnp.bfloat16)


def adam_kernel(grad_ref, master_ref, moment_ref, second_ref, new_master_ref, new_moment_ref, new_second_ref):
    grad_sum = grad_ref[...]
    master_row = master_ref[...]
    new_moment = beta_one * moment_ref[...] + (1.0 - beta_one) * grad_sum
    new_second = beta_two * second_ref[...] + (1.0 - beta_two) * grad_sum * grad_sum
    update = new_moment / fix_one / (jnp.sqrt(new_second / fix_two) + adam_eps) + decay * master_row
    new_master_ref[...] = master_row - rate * update
    new_moment_ref[...] = new_moment
    new_second_ref[...] = new_second


def on_device(section_held, segments, norm_gain, w_qkv, w_out, grad_parts, master, moment, second):
    ctxs = lax.axis_size("ctx")
    row_count = section_held.shape[2]
    head_cols = H * DH
    width = section_held.shape[3]
    blocks = [relayed(section_held, hop)[0, 0] for hop in range(ctxs)]

    count = grad_parts.shape[-1]
    shards = ctxs * lax.axis_size("dp")
    twos = (2,) * bits_of(shards)
    rows = count // shards // lane
    grads = grad_parts.reshape(twos + (rows, lane))
    step = rows // cuts
    order = scatter_order()
    parts = [halved(grads[..., i * step : (i + 1) * step, :], order) for i in range(cuts)]

    my_ctx = lax.axis_index("ctx").astype(jnp.int32).reshape(1)
    vmem = pl.BlockSpec(memory_space=pltpu.VMEM)
    qkv = pl.pallas_call(
        project_kernel,
        out_shape=jax.ShapeDtypeStruct((row_count, 3 * head_cols), jnp.bfloat16),
        in_specs=[vmem] * 3,
        out_specs=vmem,
        compiler_params=pltpu.CompilerParams(vmem_limit_bytes=24 << 20),
        cost_estimate=pl.CostEstimate(
            flops=2 * row_count * width * 3 * head_cols, bytes_accessed=8 << 20, transcendentals=0
        ),
        name="project",
    )(blocks[0], norm_gain, w_qkv[0])
    sums = []
    for kept, got in parts:
        got = after(got, qkv)
        sums.append(exchanged(kept + got.astype(jnp.float32), order[:2]))

    section_next = pl.pallas_call(
        functools.partial(attend_kernel, ctxs),
        out_shape=jax.ShapeDtypeStruct((row_count, width), jnp.bfloat16),
        in_specs=[pl.BlockSpec(memory_space=pltpu.SMEM)] + [vmem] * (5 + ctxs),
        out_specs=vmem,
        compiler_params=pltpu.CompilerParams(vmem_limit_bytes=32 << 20),
        cost_estimate=pl.CostEstimate(
            flops=2 * row_count * width * 3 * head_cols, bytes_accessed=8 << 20, transcendentals=0
        ),
        name="attend",
    )(my_ctx, blocks[0], qkv, segments[0], norm_gain, w_qkv[0], w_out[0], *blocks[1:])

    shard = (rows, lane)
    grad_sum = jnp.concatenate(
        [functools.reduce(lambda t, g: t + after(g, section_next).astype(jnp.float32), got, own) for own, got in sums],
        axis=0,
    )
    new_master, new_moment, new_second = pl.pallas_call(
        adam_kernel,
        out_shape=[jax.ShapeDtypeStruct(shard, jnp.float32)] * 3,
        in_specs=[vmem] * 4,
        out_specs=[vmem] * 3,
        compiler_params=pltpu.CompilerParams(vmem_limit_bytes=16 << 20),
        name="adam",
    )(grad_sum, master.reshape(shard), moment.reshape(shard), second.reshape(shard))
    return (
        section_next.reshape(section_held.shape),
        new_master.reshape(master.shape),
        new_moment.reshape(moment.shape),
        new_second.reshape(second.shape),
    )


def solution(mesh):
    in_specs = (
        P("pipe", "dp", "ctx", None),
        P("pipe", "dp", None),
        P("pipe", None),
        P("pipe", None, None),
        P("pipe", None, None),
        P("pipe", "ctx", "dp", None),
        P("pipe", ("ctx", "dp")),
        P("pipe", ("ctx", "dp")),
        P("pipe", ("ctx", "dp")),
    )
    out_specs = (
        P("pipe", "dp", "ctx", None),
        P("pipe", ("ctx", "dp")),
        P("pipe", ("ctx", "dp")),
        P("pipe", ("ctx", "dp")),
    )
    return jax.shard_map(
        on_device, mesh=mesh, in_specs=in_specs, out_specs=out_specs, check_vma=False
    )
```

time: 55.5 us -> 36 us (0.65)
  the two profiles are of different devices: /device:TPU:0 before, /device:TPU:1 now
where the time goes in v2:
time: 36 us; the launch traced here: 35.8 us
  starting transfers between devices  22.1 us (61%)
  Pallas kernels  7.66 us (21%)
  local copies, waits for them, and re-layouts  3.52 us (10%)
  other arithmetic  1.23 us (3%)
  between operations  0.83 us (2%)
  waiting for transfers between devices  0.46 us (1%)
    ppermute x6, starting transfers between devices, flipped(): return lax.ppermute(value, axes[0], pairs)  9.22 us
    ppermute x2, starting transfers between devices, relayed(): return lax.ppermute(section_held, ('pipe', 'ctx'), pairs)  6.63 us
    ppermute x2, starting transfers between devices, flipped(): return lax.ppermute(value, axes, pairs)  6.25 us
    pallas_call x1, Pallas kernels, on_device(): pl.pallas_call(functools.partial(attend_kernel, ctxs), out_shape=jax.Shap...  4.41 us
    pallas_call x1, Pallas kernels, on_device(): pl.pallas_call(project_kernel, out_shape=jax.ShapeDtypeStruct((row_count,...  2.26 us
    slice x1, local copies, waits for them, and re-layouts, on_device(): grads[..., i * step:(i + 1) * step, :]  1.84 us
    convert_element_type x2, local copies, waits for them, and re-layouts, halve(): lax.dynamic_index_in_dim(value, 1 - mine, dim, keepdims=False)  1.55 us
    add x2, other arithmetic, on_device(): sums.append(exchanged(kept + got.astype(jnp.float32), order[:2]))  1.14 us
  transfers between devices with their start and end apart: 10, of which 1 were waited for; matrix products, arithmetic and copies ran while one was open for 13% of the time, Pallas kernels for 19%

profile of v2, /device:TPU:1, one launch (start us, length us, event | category | flops | bytes accessed | tf_op | source)
XLA Modules:
  0.0 35.8 jit_solution(12783100696204384968)
XLA Ops:
  0.6 2.7 %collective-permute-start = (bf16[1,1,256,1024]{3,2,1,0:T(8,128)(2,1)}, bf16[1,1,256,1024]{3,2,1,0:T(8,128)(2,1)}, u32[]{:S(2)}, u32[]{:S(2)}) collective-permute-start(bf16[1,1,256,1024]{3,2,1,0:T(8,128)(2,1)} %param.9), channel_id=1, source_target_pairs={{0,8},{4,12},{8,16},{12,20},{16,24},{20,28},{24,0},{28,4},{1,9},{5... | collective-permute-start | bytes 1572872 | tf_op jit(solution)/shard_map/ppermute | solution.py:93
  3.3 0.0 copy-start
  3.3 0.0 copy-start.5
  3.3 1.8 %fusion.12 = (f32[2,2,2,256,128]{4,3,2,1,0:T(8,128)S(1)}, f32[2,2,2,256,128]{4,3,2,1,0:T(8,128)S(1)}) fusion(f32[2,2,2,512,128]{4,3,2,1,0:T(8,128)} %bitcast.65), kind=kLoop, calls=%fused_computation.25 | loop fusion | bytes 4194304 | tf_op jit(solution)/shard_map/slice | solution.py:186
  5.1 0.0 copy-start.7
  5.1 0.0 copy-start.9
  5.2 0.8 %fusion = bf16[2,2,256,128]{3,2,1,0:T(8,128)(2,1)} fusion(f32[2,2,2,256,128]{4,3,2,1,0:T(8,128)S(1)} %get-tuple-element.26, s32[]{:T(128)S(6)} %select_n.44), kind=kLoop, calls=%fused_computation.4 | loop fusion | bytes 524292 | tf_op jit(solution)/shard_map/convert_element_type | solution.py:45
  6.0 1.3 %collective-permute-start.2 = (bf16[2,2,256,128]{3,2,1,0:T(8,128)(2,1)}, bf16[2,2,256,128]{3,2,1,0:T(8,128)(2,1)}, u32[]{:S(2)}, u32[]{:S(2)}) collective-permute-start(bf16[2,2,256,128]{3,2,1,0:T(8,128)(2,1)} %fusion), channel_id=1, source_target_pairs={{0,1},{1,0},{2,3},{3,2},{4,5},{5,4},{6,7},{7,6},{8,9},{9,8},{10,11... | collective-permute-start | bytes 786440 | tf_op jit(solution)/shard_map/ppermute | solution.py:36
  7.3 4.0 %collective-permute-start.1 = (bf16[1,1,256,1024]{3,2,1,0:T(8,128)(2,1)}, bf16[1,1,256,1024]{3,2,1,0:T(8,128)(2,1)}, u32[]{:S(2)}, u32[]{:S(2)}) collective-permute-start(bf16[1,1,256,1024]{3,2,1,0:T(8,128)(2,1)} %param.9), channel_id=1, source_target_pairs={{0,12},{8,20},{16,28},{24,4},{1,13},{9,21},{17,29},{25,5},{2,14},{... | collective-permute-start | bytes 1572872 | tf_op jit(solution)/shard_map/ppermute | solution.py:93
  11.2 0.0 copy-done.7
  11.2 0.7 %fusion.1 = bf16[2,2,256,128]{3,2,1,0:T(8,128)(2,1)} fusion(f32[2,2,2,256,128]{4,3,2,1,0:T(8,128)S(1)} %get-tuple-element.27, s32[]{:T(128)S(6)} %select_n.44), kind=kLoop, calls=%fused_computation.5 | loop fusion | bytes 524292 | tf_op jit(solution)/shard_map/convert_element_type | solution.py:45
  12.0 0.0 copy-done.9
  12.0 0.2 collective-permute-start.6
  12.2 0.0 collective-permute-done
  12.2 0.0 copy-done
  12.2 0.0 copy-done.5
  12.2 0.0 copy-start.10
  12.2 0.0 copy-start.8
  12.2 2.3 %project.1.qkv_ref = bf16[256,1536]{1,0:T(8,128)(2,1)S(1)} custom-call(bf16[256,1024]{1,0:T(8,128)(2,1)} %bitcast.1.rows_ref.own_ref, f32[1,1024]{1,0:T(1,128)S(1)} %copy-done.5, bf16[1024,1536]{1,0:T(8,128)(2,1)S(1)} %bitcast.58), custom_call_target="tpu_custom_call" | custom-call | flops 805306368 | bytes 8388608 | tf_op jit(solution)/shard_map/project/pallas_call | solution.py:190
  14.5 0.0 copy-start.1
  14.5 0.0 copy-start.6
  14.5 0.0 collective-permute-done.2
  14.5 0.0 copy-done.10
  14.5 1.1 %bitcast_add_fusion.1 = f32[2,2,256,128]{3,2,1,0:T(8,128)S(1)} fusion(bf16[2,2,256,128]{3,2,1,0:T(8,128)(2,1)} %collective-permute-done.2, f32[2,2,2,256,128]{4,3,2,1,0:T(8,128)S(1)} %copy-done.10, s32[]{:T(128)S(6)} %select_n.43), kind=kLoop, calls=%fused_computation.3 | loop fusion | flops 262144 | bytes 1310724 | tf_op jit(solution)/shard_map/add | solution.py:204
  15.6 3.3 %collective-permute-start.3 = (bf16[256,128]{1,0:T(8,128)(2,1)S(1)}, bf16[256,128]{1,0:T(8,128)(2,1)S(1)}, u32[]{:S(2)}, u32[]{:S(2)}) collective-permute-start(bf16[256,128]{1,0:T(8,128)(2,1)S(1)} %get-tuple-element.28), channel_id=1, source_target_pairs={{0,6},{1,7},{2,4},{3,5},{4,2},{5,3},{6,0},{7,1},{8,14},{9,15},{10,... | collective-permute-start | bytes 196616 | tf_op jit(solution)/shard_map/ppermute | solution.py:40
  18.9 0.3 collective-permute-start.4
  19.2 0.1 collective-permute-start.5
  19.3 0.4 %collective-permute-done.6 = bf16[2,2,256,128]{3,2,1,0:T(8,128)(2,1)S(1)} collective-permute-done((bf16[2,2,256,128]{3,2,1,0:T(8,128)(2,1)}, bf16[2,2,256,128]{3,2,1,0:T(8,128)(2,1)S(1)}, u32[]{:S(2)}, u32[]{:S(2)}) %collective-permute-start.6) | collective-permute-done | bytes 262176 | tf_op jit(solution)/shard_map/ppermute | solution.py:36
  19.7 0.0 copy-done.8
  19.8 3.0 %collective-permute-start.7 = (bf16[256,128]{1,0:T(8,128)(2,1)S(1)}, bf16[256,128]{1,0:T(8,128)(2,1)S(1)}, u32[]{:S(2)}, u32[]{:S(2)}) collective-permute-start(bf16[256,128]{1,0:T(8,128)(2,1)S(1)} %get-tuple-element.31), channel_id=1, source_target_pairs={{0,6},{1,7},{2,4},{3,5},{4,2},{5,3},{6,0},{7,1},{8,14},{9,15},{10,... | collective-permute-start | bytes 196616 | tf_op jit(solution)/shard_map/ppermute | solution.py:40
  22.8 0.0 collective-permute-done.1
  22.8 3.9 %collective-permute-start.8 = (bf16[256,128]{1,0:T(8,128)(2,1)S(1)}, bf16[256,128]{1,0:T(8,128)(2,1)S(1)}, u32[]{:S(2)}, u32[]{:S(2)}) collective-permute-start(bf16[256,128]{1,0:T(8,128)(2,1)S(1)} %get-tuple-element.33), channel_id=1, source_target_pairs={{0,4},{4,0},{1,5},{5,1},{2,6},{6,2},{3,7},{7,3},{8,12},{12,8},{9,1... | collective-permute-start | bytes 196616 | tf_op jit(solution)/shard_map/ppermute | solution.py:36
  26.7 0.0 collective-permute-done.3
  26.7 3.5 %collective-permute-start.9 = (bf16[256,128]{1,0:T(8,128)(2,1)S(1)}, bf16[256,128]{1,0:T(8,128)(2,1)S(1)}, u32[]{:S(2)}, u32[]{:S(2)}) collective-permute-start(bf16[256,128]{1,0:T(8,128)(2,1)S(1)} %get-tuple-element.32), channel_id=1, source_target_pairs={{0,2},{1,3},{2,0},{3,1},{4,6},{5,7},{6,4},{7,5},{8,10},{9,11},{10,... | collective-permute-start | bytes 196616 | tf_op jit(solution)/shard_map/ppermute | solution.py:36
  30.2 0.0 copy-done.1
  30.2 0.0 copy-done.6
  30.2 0.0 copy-start.2
  30.2 0.0 copy-start.4
  30.2 4.4 %attend.1 = bf16[256,1024]{1,0:T(8,128)(2,1)} custom-call(s32[1]{0:T(128)} %bitcast.ctx_ref, bf16[256,1024]{1,0:T(8,128)(2,1)} %bitcast.1.rows_ref.own_ref, bf16[256,1536]{1,0:T(8,128)(2,1)S(1)} %project.1.qkv_ref, s32[1,512]{1,0:T(1,128)S(1)} %bitcast.64, f32[1,1024]{1,0:T(1,128)S(1)} %copy-done.5, bf16[1024,1536]{1,0:T(8,128)(2,1)S(1)} %bitcast.59, ...), custom_call_target="tpu_custom_call" | custom-call | flops 805306368 | bytes 8388608 | tf_op jit(solution)/shard_map/attend/pallas_call | solution.py:206
  34.6 0.0 collective-permute-done.4
  34.6 0.0 collective-permute-done.5
  34.6 0.0 collective-permute-done.7
  34.6 0.0 collective-permute-done.8
  34.7 0.0 collective-permute-done.9
  34.8 0.0 copy-done.2
  34.8 0.0 copy-done.3
  34.8 0.0 copy-done.4
  34.8 1.0 %adam.1 = (f32[512,128]{1,0:T(8,128)}, f32[512,128]{1,0:T(8,128)}, f32[512,128]{1,0:T(8,128)}) custom-call(f32[512,128]{1,0:T(8,128)S(1)} %pad_maximum_fusion.grad_ref, f32[512,128]{1,0:T(8,128)S(1)} %bitcast.61, f32[512,128]{1,0:T(8,128)S(1)} %bitcast.62, f32[512,128]{1,0:T(8,128)S(1)} %bitcast.63), custom_call_target="tpu_custom_call" | custom-call | tf_op jit(solution)/shard_map/adam/pallas_call | solution.py:223
  (7 shorter events, 0.2 us)
Async XLA Ops:
  0.6 11.5 %collective-permute-start = (bf16[1,1,256,1024]{3,2,1,0:T(8,128)(2,1)}, bf16[1,1,256,1024]{3,2,1,0:T(8,128)(2,1)}, u32[]{:S(2)}, u32[]{:S(2)}) collective-permute-start(bf16[1,1,256,1024]{3,2,1,0:T(8,128)(2,1)} %param.9), channel_id=1, source_target_pairs={{0,8},{4,12},{8,16},{12,20},{16,24},{20,28},{24,0},{28,4},{1,9},{5... | collective-permute-start | bytes 1572872 | tf_op jit(solution)/shard_map/ppermute | solution.py:93
  3.3 8.9 %copy-start = (bf16[1,1024,1536]{2,1,0:T(8,128)(2,1)S(1)}, bf16[1,1024,1536]{2,1,0:T(8,128)(2,1)}, u32[]{:S(2)}) copy-start(bf16[1,1024,1536]{2,1,0:T(8,128)(2,1)} %param.12) | copy-start | bytes 9437188
  3.3 8.9 %copy-start.5 = (f32[1,1024]{1,0:T(1,128)S(1)}, f32[1,1024]{1,0:T(1,128)}, u32[]{:S(2)}) copy-start(f32[1,1024]{1,0:T(1,128)} %gain_ref.3) | copy-start | bytes 12292
  5.1 6.1 %copy-start.7 = (f32[2,2,2,256,128]{4,3,2,1,0:T(8,128)}, f32[2,2,2,256,128]{4,3,2,1,0:T(8,128)S(1)}, u32[]{:S(2)}) copy-start(f32[2,2,2,256,128]{4,3,2,1,0:T(8,128)S(1)} %get-tuple-element.27) | copy-start | bytes 3145732
  5.1 6.8 %copy-start.9 = (f32[2,2,2,256,128]{4,3,2,1,0:T(8,128)}, f32[2,2,2,256,128]{4,3,2,1,0:T(8,128)S(1)}, u32[]{:S(2)}) copy-start(f32[2,2,2,256,128]{4,3,2,1,0:T(8,128)S(1)} %get-tuple-element.26) | copy-start | bytes 3145732
  6.0 8.5 %collective-permute-start.2 = (bf16[2,2,256,128]{3,2,1,0:T(8,128)(2,1)}, bf16[2,2,256,128]{3,2,1,0:T(8,128)(2,1)}, u32[]{:S(2)}, u32[]{:S(2)}) collective-permute-start(bf16[2,2,256,128]{3,2,1,0:T(8,128)(2,1)} %fusion), channel_id=1, source_target_pairs={{0,1},{1,0},{2,3},{3,2},{4,5},{5,4},{6,7},{7,6},{8,9},{9,8},{10,11... | collective-permute-start | bytes 786440 | tf_op jit(solution)/shard_map/ppermute | solution.py:36
  7.3 15.5 %collective-permute-start.1 = (bf16[1,1,256,1024]{3,2,1,0:T(8,128)(2,1)}, bf16[1,1,256,1024]{3,2,1,0:T(8,128)(2,1)}, u32[]{:S(2)}, u32[]{:S(2)}) collective-permute-start(bf16[1,1,256,1024]{3,2,1,0:T(8,128)(2,1)} %param.9), channel_id=1, source_target_pairs={{0,12},{8,20},{16,28},{24,4},{1,13},{9,21},{17,29},{25,5},{2,14},{... | collective-permute-start | bytes 1572872 | tf_op jit(solution)/shard_map/ppermute | solution.py:93
  12.0 7.7 %collective-permute-start.6 = (bf16[2,2,256,128]{3,2,1,0:T(8,128)(2,1)}, bf16[2,2,256,128]{3,2,1,0:T(8,128)(2,1)S(1)}, u32[]{:S(2)}, u32[]{:S(2)}) collective-permute-start(bf16[2,2,256,128]{3,2,1,0:T(8,128)(2,1)} %fusion.1), channel_id=1, source_target_pairs={{0,1},{1,0},{2,3},{3,2},{4,5},{5,4},{6,7},{7,6},{8,9},{9,8},{10,11... | collective-permute-start | bytes 786440 | tf_op jit(solution)/shard_map/ppermute | solution.py:36
  12.2 2.3 %copy-start.10 = (f32[2,2,2,256,128]{4,3,2,1,0:T(8,128)S(1)}, f32[2,2,2,256,128]{4,3,2,1,0:T(8,128)}, u32[]{:S(2)}) copy-start(f32[2,2,2,256,128]{4,3,2,1,0:T(8,128)} %copy-done.9) | copy-start | bytes 3145732
  12.2 7.6 %copy-start.8 = (f32[2,2,2,256,128]{4,3,2,1,0:T(8,128)S(1)}, f32[2,2,2,256,128]{4,3,2,1,0:T(8,128)}, u32[]{:S(2)}) copy-start(f32[2,2,2,256,128]{4,3,2,1,0:T(8,128)} %copy-done.7) | copy-start | bytes 3145732
  14.5 15.7 %copy-start.1 = (bf16[1,512,1024]{2,1,0:T(8,128)(2,1)S(1)}, bf16[1,512,1024]{2,1,0:T(8,128)(2,1)}, u32[]{:S(2)}) copy-start(bf16[1,512,1024]{2,1,0:T(8,128)(2,1)} %param.13) | copy-start | bytes 3145732
  14.5 15.7 %copy-start.6 = (s32[1,1,512]{2,1,0:T(1,128)S(1)}, s32[1,1,512]{2,1,0:T(1,128)}, u32[]{:S(2)}) copy-start(s32[1,1,512]{2,1,0:T(1,128)} %param.10) | copy-start | bytes 6148
  15.6 11.0 %collective-permute-start.3 = (bf16[256,128]{1,0:T(8,128)(2,1)S(1)}, bf16[256,128]{1,0:T(8,128)(2,1)S(1)}, u32[]{:S(2)}, u32[]{:S(2)}) collective-permute-start(bf16[256,128]{1,0:T(8,128)(2,1)S(1)} %get-tuple-element.28), channel_id=1, source_target_pairs={{0,6},{1,7},{2,4},{3,5},{4,2},{5,3},{6,0},{7,1},{8,14},{9,15},{10,... | collective-permute-start | bytes 196616 | tf_op jit(solution)/shard_map/ppermute | solution.py:40
  18.9 15.7 %collective-permute-start.4 = (bf16[256,128]{1,0:T(8,128)(2,1)S(1)}, bf16[256,128]{1,0:T(8,128)(2,1)S(1)}, u32[]{:S(2)}, u32[]{:S(2)}) collective-permute-start(bf16[256,128]{1,0:T(8,128)(2,1)S(1)} %get-tuple-element.30), channel_id=1, source_target_pairs={{0,4},{4,0},{1,5},{5,1},{2,6},{6,2},{3,7},{7,3},{8,12},{12,8},{9,1... | collective-permute-start | bytes 196616 | tf_op jit(solution)/shard_map/ppermute | solution.py:36
  19.2 15.4 %collective-permute-start.5 = (bf16[256,128]{1,0:T(8,128)(2,1)S(1)}, bf16[256,128]{1,0:T(8,128)(2,1)S(1)}, u32[]{:S(2)}, u32[]{:S(2)}) collective-permute-start(bf16[256,128]{1,0:T(8,128)(2,1)S(1)} %get-tuple-element.29), channel_id=1, source_target_pairs={{0,2},{1,3},{2,0},{3,1},{4,6},{5,7},{6,4},{7,5},{8,10},{9,11},{10,... | collective-permute-start | bytes 196616 | tf_op jit(solution)/shard_map/ppermute | solution.py:36
  19.8 14.8 %collective-permute-start.7 = (bf16[256,128]{1,0:T(8,128)(2,1)S(1)}, bf16[256,128]{1,0:T(8,128)(2,1)S(1)}, u32[]{:S(2)}, u32[]{:S(2)}) collective-permute-start(bf16[256,128]{1,0:T(8,128)(2,1)S(1)} %get-tuple-element.31), channel_id=1, source_target_pairs={{0,6},{1,7},{2,4},{3,5},{4,2},{5,3},{6,0},{7,1},{8,14},{9,15},{10,... | collective-permute-start | bytes 196616 | tf_op jit(solution)/shard_map/ppermute | solution.py:40
  22.8 11.9 %collective-permute-start.8 = (bf16[256,128]{1,0:T(8,128)(2,1)S(1)}, bf16[256,128]{1,0:T(8,128)(2,1)S(1)}, u32[]{:S(2)}, u32[]{:S(2)}) collective-permute-start(bf16[256,128]{1,0:T(8,128)(2,1)S(1)} %get-tuple-element.33), channel_id=1, source_target_pairs={{0,4},{4,0},{1,5},{5,1},{2,6},{6,2},{3,7},{7,3},{8,12},{12,8},{9,1... | collective-permute-start | bytes 196616 | tf_op jit(solution)/shard_map/ppermute | solution.py:36
  26.7 8.0 %collective-permute-start.9 = (bf16[256,128]{1,0:T(8,128)(2,1)S(1)}, bf16[256,128]{1,0:T(8,128)(2,1)S(1)}, u32[]{:S(2)}, u32[]{:S(2)}) collective-permute-start(bf16[256,128]{1,0:T(8,128)(2,1)S(1)} %get-tuple-element.32), channel_id=1, source_target_pairs={{0,2},{1,3},{2,0},{3,1},{4,6},{5,7},{6,4},{7,5},{8,10},{9,11},{10,... | collective-permute-start | bytes 196616 | tf_op jit(solution)/shard_map/ppermute | solution.py:36
  30.2 4.6 %copy-start.2 = (f32[1,65536]{1,0:T(1,128)S(1)}, f32[1,65536]{1,0:T(1,128)}, u32[]{:S(2)}) copy-start(f32[1,65536]{1,0:T(1,128)} %param.15) | copy-start | bytes 786436
  30.2 4.6 %copy-start.3 = (f32[1,65536]{1,0:T(1,128)S(1)}, f32[1,65536]{1,0:T(1,128)}, u32[]{:S(2)}) copy-start(f32[1,65536]{1,0:T(1,128)} %param.16) | copy-start | bytes 786436
  30.2 4.6 %copy-start.4 = (f32[1,65536]{1,0:T(1,128)S(1)}, f32[1,65536]{1,0:T(1,128)}, u32[]{:S(2)}) copy-start(f32[1,65536]{1,0:T(1,128)} %param.17) | copy-start | bytes 786436

commit v3 on v2

v3 whole, which is shorter than its diff:
```python
import functools

import jax
import jax.numpy as jnp
from jax import lax
from jax.experimental import pallas as pl
from jax.experimental.pallas import tpu as pltpu
from jax.sharding import PartitionSpec as P

H = 4
DH = 128


eps_norm = 1e-06
rate = 0.001
beta_one = 0.9
beta_two = 0.999
adam_eps = 1e-08
decay = 0.1
fix_one = 0.9999734386011124
fix_two = 0.09520785288629038
lane = 128
shares = (1, 1)


def bits_of(count):
    return count.bit_length() - 1


def after(value, *others):
    return lax.optimization_barrier((value, *others))[0]


vmem = pl.BlockSpec(memory_space=pltpu.VMEM)


def limit(mib):
    return pltpu.CompilerParams(vmem_limit_bytes=mib << 20)


def takes(microseconds):
    return pl.CostEstimate(flops=1, bytes_accessed=int(microseconds * 3.69e6), transcendentals=0)


def scatter_bits():
    return [(axis, b) for axis in ("ctx", "dp") for b in reversed(range(bits_of(lax.axis_size(axis))))]


def scatter_steps(left):
    first = left[-1:]
    return first + [b for b in left[:-1] if b[0] == "ctx"] + [b for b in left[:-1] if b[0] == "dp"][::-1]


def flipped(value, axis, bit):
    return lax.ppermute(value, axis, [(i, i ^ (1 << bit)) for i in range(lax.axis_size(axis))])


def side(axis, bit):
    return (lax.axis_index(axis) >> bit) & 1


def with_bit(k, place, value):
    low = k & ((1 << place) - 1)
    return ((k >> place) << (place + 1)) | (value << place) | low


def join_kernel(left, this, start, part_ref, got_ref, kept_ref, sent_ref):
    place, rows = len(left) - 1 - left.index(this), got_ref.shape[1]
    mine = side(*this)

    def total(k, value):
        chunk = with_bit(k, place, value)
        return part_ref[chunk, pl.ds(start, rows)] + got_ref[chunk].astype(jnp.float32)

    for k in range(sent_ref.shape[0]):
        sent_ref[k] = total(k, 1 - mine).astype(jnp.bfloat16)
    for k in range(kept_ref.shape[0]):
        kept_ref[k] = total(k, mine)


def join(left, this, part, got, start):
    half = (got.shape[0] // 2,) + got.shape[1:]
    return pl.pallas_call(
        functools.partial(join_kernel, left, this, start),
        out_shape=[jax.ShapeDtypeStruct(half, jnp.float32), jax.ShapeDtypeStruct(half, jnp.bfloat16)],
        in_specs=[vmem] * 2,
        out_specs=[vmem] * 2,
        compiler_params=limit(5),
        cost_estimate=takes(0.1),
        name="join",
    )(part, got)


def relayed(section_held, hop):
    pipes, ctxs = lax.axis_size("pipe"), lax.axis_size("ctx")
    pairs = [
        (p * ctxs + c, ((p + 1) % pipes) * ctxs + c + hop)
        for p in range(pipes)
        for c in range(ctxs - hop)
    ]
    return lax.ppermute(section_held, ("pipe", "ctx"), pairs)


def normed_rows(block, gain):
    values = block.astype(jnp.float32)
    meansq = jnp.mean(values * values, axis=-1, keepdims=True)
    return (values * lax.rsqrt(meansq + eps_norm) * gain).astype(jnp.bfloat16)


def project_kernel(gain_ref, w_ref, *refs):
    pieces, out_ref = refs[:-1], refs[-1]
    normed = jnp.concatenate([normed_rows(piece[...], gain_ref[...]) for piece in pieces], axis=0)
    out_ref[...] = jnp.dot(normed, w_ref[...], preferred_element_type=jnp.float32).astype(jnp.bfloat16)


def attend_kernel(ctxs, cuts, qkv_ref, seg_ref, gain_ref, w_ref, w_out_ref, *refs):
    own, earlier, out_ref = refs[: cuts[0]], refs[cuts[0] : -1], refs[-1]
    rows = qkv_ref.shape[0]
    head_cols = H * DH
    my_ctx = lax.axis_index("ctx")

    def seg_of(hop):
        start = pl.multiple_of(jnp.maximum(my_ctx - hop, 0) * rows, rows)
        return seg_ref[:, pl.ds(start, rows)]

    across = lax.broadcasted_iota(jnp.int32, (rows, rows), 1)
    down = lax.broadcasted_iota(jnp.int32, (rows, rows), 0)
    own_seg = seg_of(0)
    query_seg = jnp.sum(jnp.where(across == down, own_seg, 0), axis=1, keepdims=True)
    masks = [(across <= down) & (own_seg == query_seg)]
    keys = [qkv_ref[:, head_cols : 2 * head_cols]]
    values = [qkv_ref[:, 2 * head_cols :]]
    for hop in range(1, ctxs):
        pieces = earlier[(hop - 1) * cuts[1] : hop * cuts[1]]
        normed = jnp.concatenate([normed_rows(piece[...], gain_ref[...]) for piece in pieces], axis=0)
        both = jnp.dot(normed, w_ref[:, head_cols:], preferred_element_type=jnp.float32).astype(jnp.bfloat16)
        keys.append(both[:, :head_cols])
        values.append(both[:, head_cols:])
        masks.append((seg_of(hop) == query_seg) & (my_ctx >= hop))
    heads = []
    for h in range(H):
        cols = slice(h * DH, (h + 1) * DH)
        queries = qkv_ref[:, cols]
        scores = [
            jnp.where(
                mask,
                lax.dot_general(
                    queries, key[:, cols], (((1,), (1,)), ((), ())), preferred_element_type=jnp.float32
                )
                * DH ** (-0.5),
                -1e30,
            )
            for key, mask in zip(keys, masks)
        ]
        top = functools.reduce(jnp.maximum, [jnp.max(s, axis=1, keepdims=True) for s in scores])
        total, summed = 0.0, 0.0
        for score, value in zip(scores, values):
            weights = jnp.exp(score - top)
            total = total + jnp.sum(weights, axis=1, keepdims=True)
            summed = summed + jnp.dot(
                weights.astype(jnp.bfloat16), value[:, cols], preferred_element_type=jnp.float32
            )
        heads.append((summed / total).astype(jnp.bfloat16))
    attended = jnp.concatenate(heads, axis=1)
    added = jnp.dot(attended, w_out_ref[...], preferred_element_type=jnp.float32)
    size = rows // cuts[0]
    for i, piece in enumerate(own):
        span = slice(i * size, (i + 1) * size)
        out_ref[span, :] = (added[span, :] + piece[...].astype(jnp.float32)).astype(jnp.bfloat16)


def adam_kernel(starts, *refs):
    sums, (master_ref, moment_ref, second_ref, new_master_ref, new_moment_ref, new_second_ref) = refs[:-6], refs[-6:]
    for place, start in enumerate(starts):
        kept_ref, got_ref = sums[2 * place : 2 * place + 2]
        span = pl.ds(start, got_ref.shape[1])
        grad_sum = kept_ref[0] + got_ref[0].astype(jnp.float32)
        master_row = master_ref[span, :]
        new_moment = beta_one * moment_ref[span, :] + (1.0 - beta_one) * grad_sum
        new_second = beta_two * second_ref[span, :] + (1.0 - beta_two) * grad_sum * grad_sum
        update = new_moment / fix_one / (jnp.sqrt(new_second / fix_two) + adam_eps) + decay * master_row
        new_master_ref[span, :] = master_row - rate * update
        new_moment_ref[span, :] = new_moment
        new_second_ref[span, :] = new_second


def on_device(section_held, segments, norm_gain, w_qkv, w_out, grad_parts, master, moment, second):
    ctxs = lax.axis_size("ctx")
    row_count = section_held.shape[2]
    head_cols = H * DH
    width = section_held.shape[3]
    count = grad_parts.shape[-1]
    left = scatter_bits()
    steps = scatter_steps(left)
    shards = 1 << len(left)
    rows = count // shards // lane
    part = grad_parts.reshape(shards, rows, lane)
    starts = [rows * sum(shares[:i]) // sum(shares) for i in range(len(shares) + 1)]
    spans = list(zip(starts[:-1], starts[1:]))
    pairs = part.reshape(shards // 2, 2, rows, lane)
    mine, sent = side(*steps[0]), []
    for lo, hi in spans:
        mine = after(mine, *sent)
        taken = lax.dynamic_slice(pairs, (0, 1 - mine, lo, 0), (shards // 2, 1, hi - lo, lane))
        sent.append(taken.astype(jnp.bfloat16).reshape(shards // 2, hi - lo, lane))
    mine = after(mine, *sent)
    kept = lax.dynamic_slice(pairs, (0, mine, 0, 0), (shards // 2, 1, rows, lane)).reshape(shards // 2, rows, lane)
    got = [flipped(s, *steps[0]) for s in sent]
    cuts = (1, 1)
    blocks = []
    for hop in reversed(range(ctxs)):
        size = row_count // cuts[min(hop, 1)]
        cutted = [section_held[:, :, i : i + size] for i in range(0, row_count, size)]
        blocks.append([relayed(piece, hop)[0, 0] for piece in cutted])
    own, *earlier = blocks[::-1]

    kept, left = [kept] * len(spans), left[:-1]
    kept[0], sent[0] = join(left, steps[1], kept[0], got[0], 0)
    own = [after(piece, sent[0]) for piece in own]
    qkv = pl.pallas_call(
        project_kernel,
        out_shape=jax.ShapeDtypeStruct((row_count, 3 * head_cols), jnp.bfloat16),
        in_specs=[vmem] * (2 + cuts[0]),
        out_specs=vmem,
        compiler_params=limit(12),
        cost_estimate=takes(1.1),
        name="project",
    )(norm_gain, w_qkv[0], *own)

    got[0] = flipped(sent[0], *steps[1])
    got[1:] = [after(g, qkv) for g in got[1:]]
    for i, (lo, _) in list(enumerate(spans))[1:]:
        kept[i], sent[i] = join(left, steps[1], kept[i], got[i], lo)
        got[i] = flipped(sent[i], *steps[1])
    for last, this in zip(steps[1:-1], steps[2:]):
        left = [b for b in left if b != last]
        for i in range(len(spans)):
            kept[i], sent[i] = join(left, this, kept[i], got[i], 0)
            got[i] = flipped(sent[i], *this)

    section_next = pl.pallas_call(
        functools.partial(attend_kernel, ctxs, cuts),
        out_shape=jax.ShapeDtypeStruct((row_count, width), jnp.bfloat16),
        in_specs=[vmem] * (5 + cuts[0] + (ctxs - 1) * cuts[1]),
        out_specs=vmem,
        compiler_params=limit(16 + 2 * ctxs),
        cost_estimate=takes(3.2),
        name="attend",
    )(qkv, segments[0], norm_gain, w_qkv[0], w_out[0], *own, *[piece for pieces in earlier for piece in pieces])

    shard = (rows, lane)
    terms = [term for k, g in zip(kept, got) for term in (k, after(g, section_next))]
    new_master, new_moment, new_second = pl.pallas_call(
        functools.partial(adam_kernel, starts[:-1]),
        out_shape=[jax.ShapeDtypeStruct(shard, jnp.float32)] * 3,
        in_specs=[vmem] * (len(terms) + 3),
        out_specs=[vmem] * 3,
        compiler_params=limit(6),
        cost_estimate=takes(1.0),
        name="adam",
    )(*terms, master.reshape(shard), moment.reshape(shard), second.reshape(shard))
    return (
        section_next.reshape(section_held.shape),
        new_master.reshape(master.shape),
        new_moment.reshape(moment.shape),
        new_second.reshape(second.shape),
    )


def solution(mesh):
    in_specs = (
        P("pipe", "dp", "ctx", None),
        P("pipe", "dp", None),
        P("pipe", None),
        P("pipe", None, None),
        P("pipe", None, None),
        P("pipe", "ctx", "dp", None),
        P("pipe", ("ctx", "dp")),
        P("pipe", ("ctx", "dp")),
        P("pipe", ("ctx", "dp")),
    )
    out_specs = (
        P("pipe", "dp", "ctx", None),
        P("pipe", ("ctx", "dp")),
        P("pipe", ("ctx", "dp")),
        P("pipe", ("ctx", "dp")),
    )
    return jax.shard_map(
        on_device, mesh=mesh, in_specs=in_specs, out_specs=out_specs, check_vma=False
    )
```

time: 36 us -> 33.7 us (0.936)
  the two profiles are of different devices: /device:TPU:1 before, /device:TPU:0 now
where the time goes in v3:
time: 33.7 us; the launch traced here: 33.6 us
  starting transfers between devices  13.6 us (40%)
  waiting for transfers between devices  11.3 us (34%)
  Pallas kernels  6.29 us (19%)
  local copies, waits for them, and re-layouts  1.6 us (5%)
  between operations  0.8 us (2%)
    ppermute x6, waiting for transfers between devices, flipped(): lax.ppermute(value, axis, [(i, i ^ 1 << bit) for i in range(lax.axis_size...  11.3 us
    ppermute x6, starting transfers between devices, flipped(): lax.ppermute(value, axis, [(i, i ^ 1 << bit) for i in range(lax.axis_size...  7.48 us
    ppermute x2, starting transfers between devices, relayed(): return lax.ppermute(section_held, ('pipe', 'ctx'), pairs)  6.15 us
    pallas_call x1, Pallas kernels, on_device(): pl.pallas_call(functools.partial(attend_kernel, ctxs, cuts), out_shape=ja...  3.15 us
    reshape x2, local copies, waits for them, and re-layouts, on_device(): sent.append(taken.astype(jnp.bfloat16).reshape(shards // 2, hi - lo, lane))  1.48 us
    pallas_call x4, Pallas kernels, join(): pl.pallas_call(functools.partial(join_kernel, left, this, start), out_sha...  1.08 us
    pallas_call x1, Pallas kernels, on_device(): pl.pallas_call(project_kernel, out_shape=jax.ShapeDtypeStruct((row_count,...  1.07 us
    pallas_call x1, Pallas kernels, on_device(): pl.pallas_call(functools.partial(adam_kernel, starts[:-1]), out_shape=[ja...  0.99 us
  transfers between devices with their start and end apart: 8, of which 4 were waited for; matrix products, arithmetic and copies ran while one was open for 5% of the time, Pallas kernels for 16%

profile of v3, /device:TPU:0, one launch (start us, length us, event | category | flops | bytes accessed | tf_op | source)
XLA Modules:
  0.0 33.6 jit_solution(12730532083966247612)
XLA Ops:
  0.6 0.0 copy-start
  0.6 0.5 %collective-permute-start = (bf16[1,1,256,1024]{3,2,1,0:T(8,128)(2,1)}, bf16[1,1,256,1024]{3,2,1,0:T(8,128)(2,1)S(1)}, u32[]{:S(2)}, u32[]{:S(2)}) collective-permute-start(bf16[1,1,256,1024]{3,2,1,0:T(8,128)(2,1)} %param.9), channel_id=1, source_target_pairs={{0,8},{4,12},{8,16},{12,20},{16,24},{20,28},{24,0},{28,4},{1,9},{5... | collective-permute-start | bytes 1572872 | tf_op jit(solution)/shard_map/ppermute | solution.py:101
  1.1 5.6 %collective-permute-start.2 = (bf16[1,1,256,1024]{3,2,1,0:T(8,128)(2,1)}, bf16[1,1,256,1024]{3,2,1,0:T(8,128)(2,1)S(1)}, u32[]{:S(2)}, u32[]{:S(2)}) collective-permute-start(bf16[1,1,256,1024]{3,2,1,0:T(8,128)(2,1)} %param.9), channel_id=1, source_target_pairs={{0,12},{8,20},{16,28},{24,4},{1,13},{9,21},{17,29},{25,5},{2,14},{... | collective-permute-start | bytes 1572872 | tf_op jit(solution)/shard_map/ppermute | solution.py:101
  6.8 0.0 copy-done
  6.8 0.7 %fusion = bf16[4,256,128]{2,1,0:T(8,128)(2,1)} fusion(f32[4,2,512,128]{3,2,1,0:T(8,128)S(1)} %bitcast.29, s32[]{:T(128)S(6)} %select_n.9), kind=kLoop, calls=%fused_computation.3 | loop fusion | bytes 524292 | tf_op jit(solution)/shard_map/reshape | solution.py:205
  7.6 0.0 copy-start.6
  7.6 1.6 %collective-permute-start.1 = (bf16[4,256,128]{2,1,0:T(8,128)(2,1)}, bf16[4,256,128]{2,1,0:T(8,128)(2,1)}, u32[]{:S(2)}, u32[]{:S(2)}) collective-permute-start(bf16[4,256,128]{2,1,0:T(8,128)(2,1)} %fusion), channel_id=1, source_target_pairs={{0,1},{1,0},{2,3},{3,2},{4,5},{5,4},{6,7},{7,6},{8,9},{9,8},{10,11... | collective-permute-start | bytes 786440 | tf_op jit(solution)/shard_map/ppermute | solution.py:55
  9.1 0.7 %fusion.1 = bf16[4,256,128]{2,1,0:T(8,128)(2,1)} fusion(f32[4,2,512,128]{3,2,1,0:T(8,128)S(1)} %bitcast.27, s32[]{:T(128)S(6)} %select_n.10), kind=kLoop, calls=%fused_computation.4 | loop fusion | bytes 524292 | tf_op jit(solution)/shard_map/reshape | solution.py:205
  9.9 0.4 %collective-permute-start.5 = (bf16[4,256,128]{2,1,0:T(8,128)(2,1)}, bf16[4,256,128]{2,1,0:T(8,128)(2,1)S(1)}, u32[]{:S(2)}, u32[]{:S(2)}) collective-permute-start(bf16[4,256,128]{2,1,0:T(8,128)(2,1)} %fusion.1), channel_id=1, source_target_pairs={{0,1},{1,0},{2,3},{3,2},{4,5},{5,4},{6,7},{7,6},{8,9},{9,8},{10,11... | collective-permute-start | bytes 786440 | tf_op jit(solution)/shard_map/ppermute | solution.py:55
  10.3 0.0 copy-start.1
  10.3 0.1 dynamic-slice_bitcast_fusion.part_ref
  10.4 6.7 %collective-permute-done.1.got_ref = bf16[4,256,128]{2,1,0:T(8,128)(2,1)} collective-permute-done((bf16[4,256,128]{2,1,0:T(8,128)(2,1)}, bf16[4,256,128]{2,1,0:T(8,128)(2,1)}, u32[]{:S(2)}, u32[]{:S(2)}) %collective-permute-start.1) | collective-permute-done | bytes 262176 | tf_op jit(solution)/shard_map/ppermute | solution.py:55
  17.1 1.0 %join.4 = (f32[2,256,128]{2,1,0:T(8,128)S(1)}, bf16[2,256,128]{2,1,0:T(8,128)(2,1)S(1)}) custom-call(f32[4,512,128]{2,1,0:T(8,128)S(1)} %dynamic-slice_bitcast_fusion.part_ref, bf16[4,256,128]{2,1,0:T(8,128)(2,1)} %collective-permute-done.1.got_ref), custom_call_target="tpu_custom_call" | custom-call | flops 1 | bytes 369000 | tf_op jit(solution)/shard_map/join/pallas_call | solution.py:83
  18.1 0.1 collective-permute-start.3
  18.1 0.0 collective-permute-done
  18.1 0.0 copy-done.6
  18.2 0.0 copy-done.1
  18.2 1.1 %project.1.qkv_ref = bf16[256,1536]{1,0:T(8,128)(2,1)S(1)} custom-call(f32[1,1024]{1,0:T(1,128)S(1)} %copy-done.6, bf16[1024,1536]{1,0:T(8,128)(2,1)S(1)} %bitcast.30, bf16[256,1024]{1,0:T(8,128)(2,1)S(1)} %bitcast.32), custom_call_target="tpu_custom_call" | custom-call | flops 1 | bytes 4059000 | tf_op jit(solution)/shard_map/project/pallas_call | solution.py:220
  19.2 0.0 copy-start.2
  19.3 0.0 copy-start.7
  19.3 2.3 %collective-permute-done.5.got_ref = bf16[4,256,128]{2,1,0:T(8,128)(2,1)S(1)} collective-permute-done((bf16[4,256,128]{2,1,0:T(8,128)(2,1)}, bf16[4,256,128]{2,1,0:T(8,128)(2,1)S(1)}, u32[]{:S(2)}, u32[]{:S(2)}) %collective-permute-start.5) | collective-permute-done | bytes 262176 | tf_op jit(solution)/shard_map/ppermute | solution.py:55
  21.6 0.1 collective-permute-start.6
  21.7 1.4 %collective-permute-done.3.got_ref = bf16[2,256,128]{2,1,0:T(8,128)(2,1)S(1)} collective-permute-done((bf16[2,256,128]{2,1,0:T(8,128)(2,1)S(1)}, bf16[2,256,128]{2,1,0:T(8,128)(2,1)S(1)}, u32[]{:S(2)}, u32[]{:S(2)}) %collective-permute-start.3) | collective-permute-done | bytes 131104 | tf_op jit(solution)/shard_map/ppermute | solution.py:55
  23.1 2.7 %collective-permute-start.4 = (bf16[1,256,128]{2,1,0:T(8,128)(2,1)S(1)}, bf16[1,256,128]{2,1,0:T(8,128)(2,1)S(1)}, u32[]{:S(2)}, u32[]{:S(2)}) collective-permute-start(bf16[1,256,128]{2,1,0:T(8,128)(2,1)S(1)} %get-tuple-element.27), channel_id=1, source_target_pairs={{0,2},{1,3},{2,0},{3,1},{4,6},{5,7},{6,4},{7,5},{8,10},{9,11},{10,... | collective-permute-start | bytes 196616 | tf_op jit(solution)/shard_map/ppermute | solution.py:55
  25.8 0.9 %collective-permute-done.6.got_ref = bf16[2,256,128]{2,1,0:T(8,128)(2,1)S(1)} collective-permute-done((bf16[2,256,128]{2,1,0:T(8,128)(2,1)S(1)}, bf16[2,256,128]{2,1,0:T(8,128)(2,1)S(1)}, u32[]{:S(2)}, u32[]{:S(2)}) %collective-permute-start.6) | collective-permute-done | bytes 131104 | tf_op jit(solution)/shard_map/ppermute | solution.py:55
  26.7 2.7 %collective-permute-start.7 = (bf16[1,256,128]{2,1,0:T(8,128)(2,1)S(1)}, bf16[1,256,128]{2,1,0:T(8,128)(2,1)S(1)}, u32[]{:S(2)}, u32[]{:S(2)}) collective-permute-start(bf16[1,256,128]{2,1,0:T(8,128)(2,1)S(1)} %get-tuple-element.33), channel_id=1, source_target_pairs={{0,2},{1,3},{2,0},{3,1},{4,6},{5,7},{6,4},{7,5},{8,10},{9,11},{10,... | collective-permute-start | bytes 196616 | tf_op jit(solution)/shard_map/ppermute | solution.py:55
  29.4 0.0 collective-permute-done.2
  29.4 0.0 copy-done.2
  29.4 0.0 copy-done.7
  29.4 0.0 copy-start.3
  29.4 0.0 copy-start.4
  29.4 0.0 copy-start.5
  29.4 3.1 %attend.1 = bf16[256,1024]{1,0:T(8,128)(2,1)} custom-call(bf16[256,1536]{1,0:T(8,128)(2,1)S(1)} %project.1.qkv_ref, s32[1,512]{1,0:T(1,128)S(1)} %bitcast.39, f32[1,1024]{1,0:T(1,128)S(1)} %copy-done.6, bf16[1024,1536]{1,0:T(8,128)(2,1)S(1)} %bitcast.31, bf16[512,1024]{1,0:T(8,128)(2,1)S(1)} %bitcast.34, bf16[256,1024]{1,0:T(8,128)(2,1)S(1)} %bitcast.33, ...), custom_call_target="tpu_custom_call" | custom-call | flops 1 | bytes 11808000 | tf_op jit(solution)/shard_map/attend/pallas_call | solution.py:241
  32.6 0.0 collective-permute-done.4.refs_1_
  32.6 0.0 collective-permute-done.7.refs_3_
  32.6 0.0 copy-done.3
  32.6 0.0 copy-done.4
  32.6 0.0 copy-done.5
  32.6 1.0 %adam.1 = (f32[512,128]{1,0:T(8,128)}, f32[512,128]{1,0:T(8,128)}, f32[512,128]{1,0:T(8,128)}) custom-call(f32[1,256,128]{2,1,0:T(8,128)S(1)} %get-tuple-element.26.refs_0_, bf16[1,256,128]{2,1,0:T(8,128)(2,1)S(1)} %collective-permute-done.4.refs_1_, f32[1,256,128]{2,1,0:T(8,128)S(1)} %get-tuple-element.32.refs_2_, ...), custom_call_target="tpu_custom_call" | custom-call | flops 1 | bytes 3690000 | tf_op jit(solution)/shard_map/adam/pallas_call | solution.py:253
  (3 shorter events, 0.1 us)
Async XLA Ops:
  0.6 6.2 %copy-start = (f32[1,1,1,524288]{3,2,1,0:T(1,128)S(1)}, f32[1,1,1,524288]{3,2,1,0:T(1,128)}, u32[]{:S(2)}) copy-start(f32[1,1,1,524288]{3,2,1,0:T(1,128)} %param.14) | copy-start | bytes 6291460
  0.6 17.5 %collective-permute-start = (bf16[1,1,256,1024]{3,2,1,0:T(8,128)(2,1)}, bf16[1,1,256,1024]{3,2,1,0:T(8,128)(2,1)S(1)}, u32[]{:S(2)}, u32[]{:S(2)}) collective-permute-start(bf16[1,1,256,1024]{3,2,1,0:T(8,128)(2,1)} %param.9), channel_id=1, source_target_pairs={{0,8},{4,12},{8,16},{12,20},{16,24},{20,28},{24,0},{28,4},{1,9},{5... | collective-permute-start | bytes 1572872 | tf_op jit(solution)/shard_map/ppermute | solution.py:101
  1.1 28.2 %collective-permute-start.2 = (bf16[1,1,256,1024]{3,2,1,0:T(8,128)(2,1)}, bf16[1,1,256,1024]{3,2,1,0:T(8,128)(2,1)S(1)}, u32[]{:S(2)}, u32[]{:S(2)}) collective-permute-start(bf16[1,1,256,1024]{3,2,1,0:T(8,128)(2,1)} %param.9), channel_id=1, source_target_pairs={{0,12},{8,20},{16,28},{24,4},{1,13},{9,21},{17,29},{25,5},{2,14},{... | collective-permute-start | bytes 1572872 | tf_op jit(solution)/shard_map/ppermute | solution.py:101
  7.6 10.6 %copy-start.6 = (f32[1,1024]{1,0:T(1,128)S(1)}, f32[1,1024]{1,0:T(1,128)}, u32[]{:S(2)}) copy-start(f32[1,1024]{1,0:T(1,128)} %gain_ref.3) | copy-start | bytes 12292
  7.6 9.5 %collective-permute-start.1 = (bf16[4,256,128]{2,1,0:T(8,128)(2,1)}, bf16[4,256,128]{2,1,0:T(8,128)(2,1)}, u32[]{:S(2)}, u32[]{:S(2)}) collective-permute-start(bf16[4,256,128]{2,1,0:T(8,128)(2,1)} %fusion), channel_id=1, source_target_pairs={{0,1},{1,0},{2,3},{3,2},{4,5},{5,4},{6,7},{7,6},{8,9},{9,8},{10,11... | collective-permute-start | bytes 786440 | tf_op jit(solution)/shard_map/ppermute | solution.py:55
  9.9 11.7 %collective-permute-start.5 = (bf16[4,256,128]{2,1,0:T(8,128)(2,1)}, bf16[4,256,128]{2,1,0:T(8,128)(2,1)S(1)}, u32[]{:S(2)}, u32[]{:S(2)}) collective-permute-start(bf16[4,256,128]{2,1,0:T(8,128)(2,1)} %fusion.1), channel_id=1, source_target_pairs={{0,1},{1,0},{2,3},{3,2},{4,5},{5,4},{6,7},{7,6},{8,9},{9,8},{10,11... | collective-permute-start | bytes 786440 | tf_op jit(solution)/shard_map/ppermute | solution.py:55
  10.3 7.8 %copy-start.1 = (bf16[1,1024,1536]{2,1,0:T(8,128)(2,1)S(1)}, bf16[1,1024,1536]{2,1,0:T(8,128)(2,1)}, u32[]{:S(2)}) copy-start(bf16[1,1024,1536]{2,1,0:T(8,128)(2,1)} %param.12) | copy-start | bytes 9437188
  18.1 5.0 %collective-permute-start.3 = (bf16[2,256,128]{2,1,0:T(8,128)(2,1)S(1)}, bf16[2,256,128]{2,1,0:T(8,128)(2,1)S(1)}, u32[]{:S(2)}, u32[]{:S(2)}) collective-permute-start(bf16[2,256,128]{2,1,0:T(8,128)(2,1)S(1)} %get-tuple-element.23), channel_id=1, source_target_pairs={{0,4},{4,0},{1,5},{5,1},{2,6},{6,2},{3,7},{7,3},{8,12},{12,8},{9,1... | collective-permute-start | bytes 393224 | tf_op jit(solution)/shard_map/ppermute | solution.py:55
  19.2 10.1 %copy-start.2 = (bf16[1,512,1024]{2,1,0:T(8,128)(2,1)S(1)}, bf16[1,512,1024]{2,1,0:T(8,128)(2,1)}, u32[]{:S(2)}) copy-start(bf16[1,512,1024]{2,1,0:T(8,128)(2,1)} %param.13) | copy-start | bytes 3145732
  19.3 10.1 %copy-start.7 = (s32[1,1,512]{2,1,0:T(1,128)S(1)}, s32[1,1,512]{2,1,0:T(1,128)}, u32[]{:S(2)}) copy-start(s32[1,1,512]{2,1,0:T(1,128)} %param.10) | copy-start | bytes 6148
  21.6 5.0 %collective-permute-start.6 = (bf16[2,256,128]{2,1,0:T(8,128)(2,1)S(1)}, bf16[2,256,128]{2,1,0:T(8,128)(2,1)S(1)}, u32[]{:S(2)}, u32[]{:S(2)}) collective-permute-start(bf16[2,256,128]{2,1,0:T(8,128)(2,1)S(1)} %get-tuple-element.31), channel_id=1, source_target_pairs={{0,4},{4,0},{1,5},{5,1},{2,6},{6,2},{3,7},{7,3},{8,12},{12,8},{9,1... | collective-permute-start | bytes 393224 | tf_op jit(solution)/shard_map/ppermute | solution.py:55
  23.1 9.4 %collective-permute-start.4 = (bf16[1,256,128]{2,1,0:T(8,128)(2,1)S(1)}, bf16[1,256,128]{2,1,0:T(8,128)(2,1)S(1)}, u32[]{:S(2)}, u32[]{:S(2)}) collective-permute-start(bf16[1,256,128]{2,1,0:T(8,128)(2,1)S(1)} %get-tuple-element.27), channel_id=1, source_target_pairs={{0,2},{1,3},{2,0},{3,1},{4,6},{5,7},{6,4},{7,5},{8,10},{9,11},{10,... | collective-permute-start | bytes 196616 | tf_op jit(solution)/shard_map/ppermute | solution.py:55
  26.7 5.9 %collective-permute-start.7 = (bf16[1,256,128]{2,1,0:T(8,128)(2,1)S(1)}, bf16[1,256,128]{2,1,0:T(8,128)(2,1)S(1)}, u32[]{:S(2)}, u32[]{:S(2)}) collective-permute-start(bf16[1,256,128]{2,1,0:T(8,128)(2,1)S(1)} %get-tuple-element.33), channel_id=1, source_target_pairs={{0,2},{1,3},{2,0},{3,1},{4,6},{5,7},{6,4},{7,5},{8,10},{9,11},{10,... | collective-permute-start | bytes 196616 | tf_op jit(solution)/shard_map/ppermute | solution.py:55
  29.4 3.2 %copy-start.3 = (f32[1,65536]{1,0:T(1,128)S(1)}, f32[1,65536]{1,0:T(1,128)}, u32[]{:S(2)}) copy-start(f32[1,65536]{1,0:T(1,128)} %param.15) | copy-start | bytes 786436
  29.4 3.2 %copy-start.4 = (f32[1,65536]{1,0:T(1,128)S(1)}, f32[1,65536]{1,0:T(1,128)}, u32[]{:S(2)}) copy-start(f32[1,65536]{1,0:T(1,128)} %param.16) | copy-start | bytes 786436
  29.4 3.2 %copy-start.5 = (f32[1,65536]{1,0:T(1,128)S(1)}, f32[1,65536]{1,0:T(1,128)}, u32[]{:S(2)}) copy-start(f32[1,65536]{1,0:T(1,128)} %param.17) | copy-start | bytes 786436

commit v4 on v3

--- a/solution.py
+++ b/solution.py
@@ -20,7 +20,8 @@
 fix_one = 0.9999734386011124
 fix_two = 0.09520785288629038
 lane = 128
-shares = (1, 1)
+shares = (5, 3)
+ctx_first = (True, True)
 
 
 def bits_of(count):
@@ -46,9 +47,10 @@
     return [(axis, b) for axis in ("ctx", "dp") for b in reversed(range(bits_of(lax.axis_size(axis))))]
 
 
-def scatter_steps(left):
-    first = left[-1:]
-    return first + [b for b in left[:-1] if b[0] == "ctx"] + [b for b in left[:-1] if b[0] == "dp"][::-1]
+def scatter_steps(left, ctx_first):
+    near = [b for b in left if b[0] == "ctx"][::-1]
+    far = [b for b in left[:-1] if b[0] == "dp"][::-1]
+    return left[-1:] + (near + far if ctx_first else far + near)
 
 
 def flipped(value, axis, bit):
@@ -94,9 +96,9 @@
 def relayed(section_held, hop):
     pipes, ctxs = lax.axis_size("pipe"), lax.axis_size("ctx")
     pairs = [
-        (p * ctxs + c, ((p + 1) % pipes) * ctxs + c + hop)
+        (p * ctxs + c, ((p + 1) % pipes) * ctxs + (c + hop) % ctxs)
         for p in range(pipes)
-        for c in range(ctxs - hop)
+        for c in range(ctxs)
     ]
     return lax.ppermute(section_held, ("pipe", "ctx"), pairs)
 
@@ -191,32 +193,39 @@
     width = section_held.shape[3]
     count = grad_parts.shape[-1]
     left = scatter_bits()
-    steps = scatter_steps(left)
+    steps = [scatter_steps(left, flag) for flag in ctx_first]
     shards = 1 << len(left)
     rows = count // shards // lane
     part = grad_parts.reshape(shards, rows, lane)
     starts = [rows * sum(shares[:i]) // sum(shares) for i in range(len(shares) + 1)]
     spans = list(zip(starts[:-1], starts[1:]))
     pairs = part.reshape(shards // 2, 2, rows, lane)
-    mine, sent = side(*steps[0]), []
+    mine, sent = side(*left[-1]), []
     for lo, hi in spans:
         mine = after(mine, *sent)
         taken = lax.dynamic_slice(pairs, (0, 1 - mine, lo, 0), (shards // 2, 1, hi - lo, lane))
         sent.append(taken.astype(jnp.bfloat16).reshape(shards // 2, hi - lo, lane))
     mine = after(mine, *sent)
     kept = lax.dynamic_slice(pairs, (0, mine, 0, 0), (shards // 2, 1, rows, lane)).reshape(shards // 2, rows, lane)
-    got = [flipped(s, *steps[0]) for s in sent]
+    got = [flipped(s, *left[-1]) for s in sent]
     cuts = (1, 1)
     blocks = []
     for hop in reversed(range(ctxs)):
         size = row_count // cuts[min(hop, 1)]
-        cutted = [section_held[:, :, i : i + size] for i in range(0, row_count, size)]
+        held = section_held if hop else after(section_held, kept)
+        cutted = [held[:, :, i : i + size] for i in range(0, row_count, size)]
         blocks.append([relayed(piece, hop)[0, 0] for piece in cutted])
     own, *earlier = blocks[::-1]
 
-    kept, left = [kept] * len(spans), left[:-1]
-    kept[0], sent[0] = join(left, steps[1], kept[0], got[0], 0)
-    own = [after(piece, sent[0]) for piece in own]
+    kept, left = [kept] * len(spans), [left[:-1]] * len(spans)
+
+    def advance(i, step, start=0):
+        this = steps[i][step]
+        kept[i], sent[i] = join(left[i], this, kept[i], got[i], start)
+        left[i] = [b for b in left[i] if b != this]
+
+    advance(0, 1)
+    own = [after(piece, sent[0], *[p for pieces in earlier for p in pieces]) for piece in own]
     qkv = pl.pallas_call(
         project_kernel,
         out_shape=jax.ShapeDtypeStruct((row_count, 3 * head_cols), jnp.bfloat16),
@@ -227,16 +236,15 @@
         name="project",
     )(norm_gain, w_qkv[0], *own)
 
-    got[0] = flipped(sent[0], *steps[1])
+    got[0] = flipped(sent[0], *steps[0][1])
     got[1:] = [after(g, qkv) for g in got[1:]]
     for i, (lo, _) in list(enumerate(spans))[1:]:
-        kept[i], sent[i] = join(left, steps[1], kept[i], got[i], lo)
-        got[i] = flipped(sent[i], *steps[1])
-    for last, this in zip(steps[1:-1], steps[2:]):
-        left = [b for b in left if b != last]
+        advance(i, 1, lo)
+        got[i] = flipped(sent[i], *steps[i][1])
+    for step in range(2, len(steps[0])):
         for i in range(len(spans)):
-            kept[i], sent[i] = join(left, this, kept[i], got[i], 0)
-            got[i] = flipped(sent[i], *this)
+            advance(i, step)
+            got[i] = flipped(sent[i], *steps[i][step])
 
     section_next = pl.pallas_call(
         functools.partial(attend_kernel, ctxs, cuts),

time: 33.7 us -> 31.1 us (0.923)
  starting transfers between devices: 13.6 us -> 12.2 us
  local copies, waits for them, and re-layouts: 1.6 us -> 0.2 us
  waiting for transfers between devices: 11.3 us -> 12.4 us
  Pallas kernels: 6.29 us -> 5.37 us
    ppermute x2, starting transfers between devices: 6.15 us -> 4.11 us  [relayed(): return lax.ppermute(section_held, ('pipe', 'ctx'), pairs)]
    ppermute x2, waiting for transfers between devices: 0.01 us -> 1.84 us  [relayed(): return lax.ppermute(section_held, ('pipe', 'ctx'), pairs)]
    reshape x2, local copies, waits for them, and re-layouts: 1.48 us -> 0.08 us  [on_device(): sent.append(taken.astype(jnp.bfloat16).reshape(shards // 2, hi - lo, lane))]
    pallas_call x4, Pallas kernels: 1.08 us -> 0.15 us  [join(): pl.pallas_call(functools.partial(join_kernel, left, this, start), out_sha...]
    ppermute x6, waiting for transfers between devices: 11.3 us -> 10.6 us  [flipped(): lax.ppermute(value, axis, [(i, i ^ 1 << bit) for i in range(lax.axis_size...]
    ppermute x6, starting transfers between devices: 7.48 us -> 8.1 us  [flipped(): lax.ppermute(value, axis, [(i, i ^ 1 << bit) for i in range(lax.axis_size...]
  transfers between devices with their start and end apart: 8 -> 8, of which waited for: 4 -> 5; matrix products, arithmetic and copies ran while one was open for 5% -> 1% of each run, Pallas kernels for 16% -> 14%
where the time goes in v4:
time: 31.1 us; the launch traced here: 31 us
  waiting for transfers between devices  12.4 us (40%)
  starting transfers between devices  12.2 us (39%)
  Pallas kernels  5.37 us (17%)
  between operations  0.75 us (2%)
    ppermute x6, waiting for transfers between devices, flipped(): lax.ppermute(value, axis, [(i, i ^ 1 << bit) for i in range(lax.axis_size...  10.6 us
    ppermute x6, starting transfers between devices, flipped(): lax.ppermute(value, axis, [(i, i ^ 1 << bit) for i in range(lax.axis_size...  8.1 us
    ppermute x2, starting transfers between devices, relayed(): return lax.ppermute(section_held, ('pipe', 'ctx'), pairs)  4.11 us
    pallas_call x1, Pallas kernels, on_device(): pl.pallas_call(functools.partial(attend_kernel, ctxs, cuts), out_shape=ja...  3.15 us
    ppermute x2, waiting for transfers between devices, relayed(): return lax.ppermute(section_held, ('pipe', 'ctx'), pairs)  1.84 us
    pallas_call x1, Pallas kernels, on_device(): pl.pallas_call(project_kernel, out_shape=jax.ShapeDtypeStruct((row_count,...  1.08 us
    pallas_call x1, Pallas kernels, on_device(): pl.pallas_call(functools.partial(adam_kernel, starts[:-1]), out_shape=[ja...  0.99 us
  transfers between devices with their start and end apart: 8, of which 5 were waited for; matrix products, arithmetic and copies ran while one was open for 1% of the time, Pallas kernels for 14%

profile of v4, /device:TPU:0, one launch (start us, length us, event | category | flops | bytes accessed | tf_op | source)
XLA Modules:
  0.0 31.0 jit_solution(12676521349542812346)
XLA Ops:
  0.6 0.0 copy-start
  0.6 2.5 %collective-permute-start.2 = (bf16[1,1,256,1024]{3,2,1,0:T(8,128)(2,1)}, bf16[1,1,256,1024]{3,2,1,0:T(8,128)(2,1)S(1)}, u32[]{:S(2)}, u32[]{:S(2)}) collective-permute-start(bf16[1,1,256,1024]{3,2,1,0:T(8,128)(2,1)} %param.9), channel_id=1, source_target_pairs={{0,12},{4,8},{8,20},{12,16},{16,28},{20,24},{24,4},{28,0},{1,13},{... | collective-permute-start | bytes 1572872 | tf_op jit(solution)/shard_map/ppermute | solution.py:103
  3.1 0.0 copy-done
  3.2 0.0 copy-start.6
  3.2 0.0 copy-start.1
  3.2 0.1 dynamic-slice_bitcast_fusion.part_ref
  3.3 1.7 %collective-permute-start = (bf16[1,1,256,1024]{3,2,1,0:T(8,128)(2,1)}, bf16[1,1,256,1024]{3,2,1,0:T(8,128)(2,1)S(1)}, u32[]{:S(2)}, u32[]{:S(2)}) collective-permute-start(bf16[1,1,256,1024]{3,2,1,0:T(8,128)(2,1)} %param.9), channel_id=1, source_target_pairs={{0,8},{4,12},{8,16},{12,20},{16,24},{20,28},{24,0},{28,4},{1,9},{5... | collective-permute-start | bytes 1572872 | tf_op jit(solution)/shard_map/ppermute | solution.py:103
  5.0 1.6 %collective-permute-start.1 = (bf16[4,320,128]{2,1,0:T(8,128)(2,1)S(1)}, bf16[4,320,128]{2,1,0:T(8,128)(2,1)S(1)}, u32[]{:S(2)}, u32[]{:S(2)}) collective-permute-start(bf16[4,320,128]{2,1,0:T(8,128)(2,1)S(1)} %fusion), channel_id=1, source_target_pairs={{0,1},{1,0},{2,3},{3,2},{4,5},{5,4},{6,7},{7,6},{8,9},{9,8},{10,11... | collective-permute-start | bytes 983048 | tf_op jit(solution)/shard_map/ppermute | solution.py:57
  6.5 0.4 %collective-permute-start.5 = (bf16[4,192,128]{2,1,0:T(8,128)(2,1)S(1)}, bf16[4,192,128]{2,1,0:T(8,128)(2,1)S(1)}, u32[]{:S(2)}, u32[]{:S(2)}) collective-permute-start(bf16[4,192,128]{2,1,0:T(8,128)(2,1)S(1)} %fusion.1), channel_id=1, source_target_pairs={{0,1},{1,0},{2,3},{3,2},{4,5},{5,4},{6,7},{7,6},{8,9},{9,8},{10,11... | collective-permute-start | bytes 589832 | tf_op jit(solution)/shard_map/ppermute | solution.py:57
  7.0 8.5 %collective-permute-done.1.got_ref = bf16[4,320,128]{2,1,0:T(8,128)(2,1)S(1)} collective-permute-done((bf16[4,320,128]{2,1,0:T(8,128)(2,1)S(1)}, bf16[4,320,128]{2,1,0:T(8,128)(2,1)S(1)}, u32[]{:S(2)}, u32[]{:S(2)}) %collective-permute-start.1) | collective-permute-done | bytes 327712 | tf_op jit(solution)/shard_map/ppermute | solution.py:57
  15.5 0.1 join.4
  15.5 0.2 collective-permute-start.3
  15.7 0.0 collective-permute-done.2
  15.7 1.8 %collective-permute-done = bf16[1,1,256,1024]{3,2,1,0:T(8,128)(2,1)S(1)} collective-permute-done((bf16[1,1,256,1024]{3,2,1,0:T(8,128)(2,1)}, bf16[1,1,256,1024]{3,2,1,0:T(8,128)(2,1)S(1)}, u32[]{:S(2)}, u32[]{:S(2)}) %collective-permute-start) | collective-permute-done | bytes 524320 | tf_op jit(solution)/shard_map/ppermute | solution.py:103
  17.6 0.0 copy-done.6
  17.6 0.0 copy-done.1
  17.6 0.0 copy-start.7
  17.6 1.1 %project.1.qkv_ref = bf16[256,1536]{1,0:T(8,128)(2,1)S(1)} custom-call(f32[1,1024]{1,0:T(1,128)S(1)} %copy-done.6, bf16[1024,1536]{1,0:T(8,128)(2,1)S(1)} %bitcast.30, bf16[256,1024]{1,0:T(8,128)(2,1)S(1)} %bitcast.32), custom_call_target="tpu_custom_call" | custom-call | flops 1 | bytes 4059000 | tf_op jit(solution)/shard_map/project/pallas_call | solution.py:229
  18.7 0.0 copy-start.2
  18.7 0.7 %collective-permute-done.5.got_ref = bf16[4,192,128]{2,1,0:T(8,128)(2,1)S(1)} collective-permute-done((bf16[4,192,128]{2,1,0:T(8,128)(2,1)S(1)}, bf16[4,192,128]{2,1,0:T(8,128)(2,1)S(1)}, u32[]{:S(2)}, u32[]{:S(2)}) %collective-permute-start.5) | collective-permute-done | bytes 196640 | tf_op jit(solution)/shard_map/ppermute | solution.py:57
  19.4 0.5 %collective-permute-start.6 = (bf16[2,192,128]{2,1,0:T(8,128)(2,1)S(1)}, bf16[2,192,128]{2,1,0:T(8,128)(2,1)S(1)}, u32[]{:S(2)}, u32[]{:S(2)}) collective-permute-start(bf16[2,192,128]{2,1,0:T(8,128)(2,1)S(1)} %get-tuple-element.33), channel_id=1, source_target_pairs={{0,4},{4,0},{1,5},{5,1},{2,6},{6,2},{3,7},{7,3},{8,12},{12,8},{9,1... | collective-permute-start | bytes 294920 | tf_op jit(solution)/shard_map/ppermute | solution.py:57
  20.0 1.3 %collective-permute-done.3.got_ref = bf16[2,320,128]{2,1,0:T(8,128)(2,1)S(1)} collective-permute-done((bf16[2,320,128]{2,1,0:T(8,128)(2,1)S(1)}, bf16[2,320,128]{2,1,0:T(8,128)(2,1)S(1)}, u32[]{:S(2)}, u32[]{:S(2)}) %collective-permute-start.3) | collective-permute-done | bytes 163872 | tf_op jit(solution)/shard_map/ppermute | solution.py:57
  21.2 2.7 %collective-permute-start.4 = (bf16[1,320,128]{2,1,0:T(8,128)(2,1)S(1)}, bf16[1,320,128]{2,1,0:T(8,128)(2,1)S(1)}, u32[]{:S(2)}, u32[]{:S(2)}) collective-permute-start(bf16[1,320,128]{2,1,0:T(8,128)(2,1)S(1)} %get-tuple-element.29), channel_id=1, source_target_pairs={{0,2},{1,3},{2,0},{3,1},{4,6},{5,7},{6,4},{7,5},{8,10},{9,11},{10,... | collective-permute-start | bytes 245768 | tf_op jit(solution)/shard_map/ppermute | solution.py:57
  23.9 0.2 collective-permute-done.6.got_ref
  24.1 2.7 %collective-permute-start.7 = (bf16[1,192,128]{2,1,0:T(8,128)(2,1)S(1)}, bf16[1,192,128]{2,1,0:T(8,128)(2,1)S(1)}, u32[]{:S(2)}, u32[]{:S(2)}) collective-permute-start(bf16[1,192,128]{2,1,0:T(8,128)(2,1)S(1)} %get-tuple-element.35), channel_id=1, source_target_pairs={{0,2},{1,3},{2,0},{3,1},{4,6},{5,7},{6,4},{7,5},{8,10},{9,11},{10,... | collective-permute-start | bytes 147464 | tf_op jit(solution)/shard_map/ppermute | solution.py:57
  26.8 0.0 copy-done.7
  26.8 0.0 copy-done.2
  26.8 0.0 copy-start.3
  26.8 0.0 copy-start.4
  26.8 0.0 copy-start.5
  26.8 3.2 %attend.1 = bf16[256,1024]{1,0:T(8,128)(2,1)} custom-call(bf16[256,1536]{1,0:T(8,128)(2,1)S(1)} %project.1.qkv_ref, s32[1,512]{1,0:T(1,128)S(1)} %bitcast.39, f32[1,1024]{1,0:T(1,128)S(1)} %copy-done.6, bf16[1024,1536]{1,0:T(8,128)(2,1)S(1)} %bitcast.31, bf16[512,1024]{1,0:T(8,128)(2,1)S(1)} %bitcast.34, bf16[256,1024]{1,0:T(8,128)(2,1)S(1)} %bitcast.33, ...), custom_call_target="tpu_custom_call" | custom-call | flops 1 | bytes 11808000 | tf_op jit(solution)/shard_map/attend/pallas_call | solution.py:249
  30.0 0.0 collective-permute-done.4.refs_1_
  30.0 0.0 collective-permute-done.7.refs_3_
  30.0 0.0 copy-done.3
  30.0 0.0 copy-done.4
  30.0 0.0 copy-done.5
  30.0 1.0 %adam.1 = (f32[512,128]{1,0:T(8,128)}, f32[512,128]{1,0:T(8,128)}, f32[512,128]{1,0:T(8,128)}) custom-call(f32[1,320,128]{2,1,0:T(8,128)S(1)} %get-tuple-element.28.refs_0_, bf16[1,320,128]{2,1,0:T(8,128)(2,1)S(1)} %collective-permute-done.4.refs_1_, f32[1,192,128]{2,1,0:T(8,128)S(1)} %get-tuple-element.34.refs_2_, ...), custom_call_target="tpu_custom_call" | custom-call | flops 1 | bytes 3690000 | tf_op jit(solution)/shard_map/adam/pallas_call | solution.py:261
  (5 shorter events, 0.2 us)
Async XLA Ops:
  0.6 2.5 %copy-start = (f32[1,1,1,524288]{3,2,1,0:T(1,128)S(1)}, f32[1,1,1,524288]{3,2,1,0:T(1,128)}, u32[]{:S(2)}) copy-start(f32[1,1,1,524288]{3,2,1,0:T(1,128)} %param.14) | copy-start | bytes 6291460
  0.6 15.1 %collective-permute-start.2 = (bf16[1,1,256,1024]{3,2,1,0:T(8,128)(2,1)}, bf16[1,1,256,1024]{3,2,1,0:T(8,128)(2,1)S(1)}, u32[]{:S(2)}, u32[]{:S(2)}) collective-permute-start(bf16[1,1,256,1024]{3,2,1,0:T(8,128)(2,1)} %param.9), channel_id=1, source_target_pairs={{0,12},{4,8},{8,20},{12,16},{16,28},{20,24},{24,4},{28,0},{1,13},{... | collective-permute-start | bytes 1572872 | tf_op jit(solution)/shard_map/ppermute | solution.py:103
  3.2 14.4 %copy-start.6 = (f32[1,1024]{1,0:T(1,128)S(1)}, f32[1,1024]{1,0:T(1,128)}, u32[]{:S(2)}) copy-start(f32[1,1024]{1,0:T(1,128)} %gain_ref.3) | copy-start | bytes 12292
  3.2 14.4 %copy-start.1 = (bf16[1,1024,1536]{2,1,0:T(8,128)(2,1)S(1)}, bf16[1,1024,1536]{2,1,0:T(8,128)(2,1)}, u32[]{:S(2)}) copy-start(bf16[1,1024,1536]{2,1,0:T(8,128)(2,1)} %param.12) | copy-start | bytes 9437188
  3.3 14.3 %collective-permute-start = (bf16[1,1,256,1024]{3,2,1,0:T(8,128)(2,1)}, bf16[1,1,256,1024]{3,2,1,0:T(8,128)(2,1)S(1)}, u32[]{:S(2)}, u32[]{:S(2)}) collective-permute-start(bf16[1,1,256,1024]{3,2,1,0:T(8,128)(2,1)} %param.9), channel_id=1, source_target_pairs={{0,8},{4,12},{8,16},{12,20},{16,24},{20,28},{24,0},{28,4},{1,9},{5... | collective-permute-start | bytes 1572872 | tf_op jit(solution)/shard_map/ppermute | solution.py:103
  5.0 10.5 %collective-permute-start.1 = (bf16[4,320,128]{2,1,0:T(8,128)(2,1)S(1)}, bf16[4,320,128]{2,1,0:T(8,128)(2,1)S(1)}, u32[]{:S(2)}, u32[]{:S(2)}) collective-permute-start(bf16[4,320,128]{2,1,0:T(8,128)(2,1)S(1)} %fusion), channel_id=1, source_target_pairs={{0,1},{1,0},{2,3},{3,2},{4,5},{5,4},{6,7},{7,6},{8,9},{9,8},{10,11... | collective-permute-start | bytes 983048 | tf_op jit(solution)/shard_map/ppermute | solution.py:57
  6.5 12.8 %collective-permute-start.5 = (bf16[4,192,128]{2,1,0:T(8,128)(2,1)S(1)}, bf16[4,192,128]{2,1,0:T(8,128)(2,1)S(1)}, u32[]{:S(2)}, u32[]{:S(2)}) collective-permute-start(bf16[4,192,128]{2,1,0:T(8,128)(2,1)S(1)} %fusion.1), channel_id=1, source_target_pairs={{0,1},{1,0},{2,3},{3,2},{4,5},{5,4},{6,7},{7,6},{8,9},{9,8},{10,11... | collective-permute-start | bytes 589832 | tf_op jit(solution)/shard_map/ppermute | solution.py:57
  15.5 5.7 %collective-permute-start.3 = (bf16[2,320,128]{2,1,0:T(8,128)(2,1)S(1)}, bf16[2,320,128]{2,1,0:T(8,128)(2,1)S(1)}, u32[]{:S(2)}, u32[]{:S(2)}) collective-permute-start(bf16[2,320,128]{2,1,0:T(8,128)(2,1)S(1)} %get-tuple-element.25), channel_id=1, source_target_pairs={{0,4},{4,0},{1,5},{5,1},{2,6},{6,2},{3,7},{7,3},{8,12},{12,8},{9,1... | collective-permute-start | bytes 491528 | tf_op jit(solution)/shard_map/ppermute | solution.py:57
  17.6 9.2 %copy-start.7 = (s32[1,1,512]{2,1,0:T(1,128)S(1)}, s32[1,1,512]{2,1,0:T(1,128)}, u32[]{:S(2)}) copy-start(s32[1,1,512]{2,1,0:T(1,128)} %param.10) | copy-start | bytes 6148
  18.7 8.1 %copy-start.2 = (bf16[1,512,1024]{2,1,0:T(8,128)(2,1)S(1)}, bf16[1,512,1024]{2,1,0:T(8,128)(2,1)}, u32[]{:S(2)}) copy-start(bf16[1,512,1024]{2,1,0:T(8,128)(2,1)} %param.13) | copy-start | bytes 3145732
  19.4 4.7 %collective-permute-start.6 = (bf16[2,192,128]{2,1,0:T(8,128)(2,1)S(1)}, bf16[2,192,128]{2,1,0:T(8,128)(2,1)S(1)}, u32[]{:S(2)}, u32[]{:S(2)}) collective-permute-start(bf16[2,192,128]{2,1,0:T(8,128)(2,1)S(1)} %get-tuple-element.33), channel_id=1, source_target_pairs={{0,4},{4,0},{1,5},{5,1},{2,6},{6,2},{3,7},{7,3},{8,12},{12,8},{9,1... | collective-permute-start | bytes 294920 | tf_op jit(solution)/shard_map/ppermute | solution.py:57
  21.2 8.7 %collective-permute-start.4 = (bf16[1,320,128]{2,1,0:T(8,128)(2,1)S(1)}, bf16[1,320,128]{2,1,0:T(8,128)(2,1)S(1)}, u32[]{:S(2)}, u32[]{:S(2)}) collective-permute-start(bf16[1,320,128]{2,1,0:T(8,128)(2,1)S(1)} %get-tuple-element.29), channel_id=1, source_target_pairs={{0,2},{1,3},{2,0},{3,1},{4,6},{5,7},{6,4},{7,5},{8,10},{9,11},{10,... | collective-permute-start | bytes 245768 | tf_op jit(solution)/shard_map/ppermute | solution.py:57
  24.1 5.8 %collective-permute-start.7 = (bf16[1,192,128]{2,1,0:T(8,128)(2,1)S(1)}, bf16[1,192,128]{2,1,0:T(8,128)(2,1)S(1)}, u32[]{:S(2)}, u32[]{:S(2)}) collective-permute-start(bf16[1,192,128]{2,1,0:T(8,128)(2,1)S(1)} %get-tuple-element.35), channel_id=1, source_target_pairs={{0,2},{1,3},{2,0},{3,1},{4,6},{5,7},{6,4},{7,5},{8,10},{9,11},{10,... | collective-permute-start | bytes 147464 | tf_op jit(solution)/shard_map/ppermute | solution.py:57
  26.8 3.2 %copy-start.3 = (f32[1,65536]{1,0:T(1,128)S(1)}, f32[1,65536]{1,0:T(1,128)}, u32[]{:S(2)}) copy-start(f32[1,65536]{1,0:T(1,128)} %param.15) | copy-start | bytes 786436
  26.8 3.2 %copy-start.4 = (f32[1,65536]{1,0:T(1,128)S(1)}, f32[1,65536]{1,0:T(1,128)}, u32[]{:S(2)}) copy-start(f32[1,65536]{1,0:T(1,128)} %param.16) | copy-start | bytes 786436
  26.8 3.2 %copy-start.5 = (f32[1,65536]{1,0:T(1,128)S(1)}, f32[1,65536]{1,0:T(1,128)}, u32[]{:S(2)}) copy-start(f32[1,65536]{1,0:T(1,128)} %param.17) | copy-start | bytes 786436

commit v5 on v4

--- a/solution.py
+++ b/solution.py
@@ -40,7 +40,7 @@
 
 
 def takes(microseconds):
-    return pl.CostEstimate(flops=1, bytes_accessed=int(microseconds * 3.69e6), transcendentals=0)
+    return pl.CostEstimate(flops=int(microseconds * 1.15e9), bytes_accessed=int(microseconds * 3.69e6), transcendentals=0)
 
 
 def scatter_bits():
@@ -115,8 +115,7 @@
     out_ref[...] = jnp.dot(normed, w_ref[...], preferred_element_type=jnp.float32).astype(jnp.bfloat16)
 
 
-def attend_kernel(ctxs, cuts, qkv_ref, seg_ref, gain_ref, w_ref, w_out_ref, *refs):
-    own, earlier, out_ref = refs[: cuts[0]], refs[cuts[0] : -1], refs[-1]
+def attend_heads(ctxs, heads, seg_ref, qkv_ref, others_ref):
     rows = qkv_ref.shape[0]
     head_cols = H * DH
     my_ctx = lax.axis_index("ctx")
@@ -130,42 +129,50 @@
     own_seg = seg_of(0)
     query_seg = jnp.sum(jnp.where(across == down, own_seg, 0), axis=1, keepdims=True)
     masks = [(across <= down) & (own_seg == query_seg)]
-    keys = [qkv_ref[:, head_cols : 2 * head_cols]]
-    values = [qkv_ref[:, 2 * head_cols :]]
-    for hop in range(1, ctxs):
-        pieces = earlier[(hop - 1) * cuts[1] : hop * cuts[1]]
-        normed = jnp.concatenate([normed_rows(piece[...], gain_ref[...]) for piece in pieces], axis=0)
-        both = jnp.dot(normed, w_ref[:, head_cols:], preferred_element_type=jnp.float32).astype(jnp.bfloat16)
-        keys.append(both[:, :head_cols])
-        values.append(both[:, head_cols:])
-        masks.append((seg_of(hop) == query_seg) & (my_ctx >= hop))
-    heads = []
-    for h in range(H):
+    masks += [(seg_of(hop) == query_seg) & (my_ctx >= hop) for hop in range(1, ctxs)]
+    done = []
+    for h in heads:
         cols = slice(h * DH, (h + 1) * DH)
+        key_cols = slice(head_cols + h * DH, head_cols + (h + 1) * DH)
+        value_cols = slice(2 * head_cols + h * DH, 2 * head_cols + (h + 1) * DH)
         queries = qkv_ref[:, cols]
+        keys, values = [qkv_ref[:, key_cols]], [qkv_ref[:, value_cols]]
+        for hop in range(1, ctxs):
+            span = slice((hop - 1) * rows, hop * rows)
+            keys.append(others_ref[span, cols])
+            values.append(others_ref[span, key_cols])
         scores = [
             jnp.where(
                 mask,
-                lax.dot_general(
-                    queries, key[:, cols], (((1,), (1,)), ((), ())), preferred_element_type=jnp.float32
-                )
+                lax.dot_general(queries, key, (((1,), (1,)), ((), ())), preferred_element_type=jnp.float32)
                 * DH ** (-0.5),
                 -1e30,
             )
             for key, mask in zip(keys, masks)
         ]
-        top = functools.reduce(jnp.maximum, [jnp.max(s, axis=1, keepdims=True) for s in scores])
+        top = functools.reduce(jnp.maximum, [jnp.max(score, axis=1, keepdims=True) for score in scores])
         total, summed = 0.0, 0.0
         for score, value in zip(scores, values):
             weights = jnp.exp(score - top)
             total = total + jnp.sum(weights, axis=1, keepdims=True)
             summed = summed + jnp.dot(
-                weights.astype(jnp.bfloat16), value[:, cols], preferred_element_type=jnp.float32
+                weights.astype(jnp.bfloat16), value, preferred_element_type=jnp.float32
             )
-        heads.append((summed / total).astype(jnp.bfloat16))
-    attended = jnp.concatenate(heads, axis=1)
+        done.append((summed / total).astype(jnp.bfloat16))
+    return jnp.concatenate(done, axis=1)
+
+
+def others_kernel(ctxs, gain_ref, w_ref, *refs):
+    earlier, out_ref = refs[:-1], refs[-1]
+    normed = jnp.concatenate([normed_rows(piece[...], gain_ref[...]) for piece in earlier], axis=0)
+    out_ref[...] = jnp.dot(normed, w_ref[:, H * DH :], preferred_element_type=jnp.float32).astype(jnp.bfloat16)
+
+
+def finish_kernel(ctxs, heads, qkv_ref, seg_ref, others_ref, w_out_ref, *refs):
+    own, out_ref = refs[:-1], refs[-1]
+    attended = attend_heads(ctxs, heads, seg_ref, qkv_ref, others_ref)
     added = jnp.dot(attended, w_out_ref[...], preferred_element_type=jnp.float32)
-    size = rows // cuts[0]
+    size = out_ref.shape[0] // len(own)
     for i, piece in enumerate(own):
         span = slice(i * size, (i + 1) * size)
         out_ref[span, :] = (added[span, :] + piece[...].astype(jnp.float32)).astype(jnp.bfloat16)
@@ -197,7 +204,7 @@
     shards = 1 << len(left)
     rows = count // shards // lane
     part = grad_parts.reshape(shards, rows, lane)
-    starts = [rows * sum(shares[:i]) // sum(shares) for i in range(len(shares) + 1)]
+    starts = [rows * sum(shares[:i]) // sum(shares) // 16 * 16 for i in range(len(shares) + 1)]
     spans = list(zip(starts[:-1], starts[1:]))
     pairs = part.reshape(shards // 2, 2, rows, lane)
     mine, sent = side(*left[-1]), []
@@ -224,8 +231,23 @@
         kept[i], sent[i] = join(left[i], this, kept[i], got[i], start)
         left[i] = [b for b in left[i] if b != this]
 
-    advance(0, 1)
-    own = [after(piece, sent[0], *[p for pieces in earlier for p in pieces]) for piece in own]
+    advance(0, 1, spans[0][0])
+    got[0] = flipped(sent[0], *steps[0][1])
+    flat = [piece for pieces in earlier for piece in pieces]
+    others = pl.pallas_call(
+        functools.partial(others_kernel, ctxs),
+        out_shape=jax.ShapeDtypeStruct(((ctxs - 1) * row_count, 2 * head_cols), jnp.bfloat16),
+        in_specs=[vmem] * (2 + len(flat)),
+        out_specs=vmem,
+        compiler_params=limit(10 + 2 * ctxs),
+        cost_estimate=takes(5),
+        name="others",
+    )(norm_gain, w_qkv[0], *[after(piece, sent[0]) for piece in flat])
+    for i, (lo, _) in list(enumerate(spans))[1:]:
+        got[i] = after(got[i], others)
+        advance(i, 1, lo)
+        got[i] = flipped(sent[i], *steps[i][1])
+    own = [after(piece, others, *sent) for piece in own]
     qkv = pl.pallas_call(
         project_kernel,
         out_shape=jax.ShapeDtypeStruct((row_count, 3 * head_cols), jnp.bfloat16),
@@ -236,25 +258,23 @@
         name="project",
     )(norm_gain, w_qkv[0], *own)
 
-    got[0] = flipped(sent[0], *steps[0][1])
-    got[1:] = [after(g, qkv) for g in got[1:]]
-    for i, (lo, _) in list(enumerate(spans))[1:]:
-        advance(i, 1, lo)
-        got[i] = flipped(sent[i], *steps[i][1])
+    got[0] = after(got[0], qkv)
+    first_heads = 0
+    got[0] = after(got[0], qkv)
     for step in range(2, len(steps[0])):
         for i in range(len(spans)):
             advance(i, step)
             got[i] = flipped(sent[i], *steps[i][step])
 
     section_next = pl.pallas_call(
-        functools.partial(attend_kernel, ctxs, cuts),
+        functools.partial(finish_kernel, ctxs, range(first_heads, H)),
         out_shape=jax.ShapeDtypeStruct((row_count, width), jnp.bfloat16),
-        in_specs=[vmem] * (5 + cuts[0] + (ctxs - 1) * cuts[1]),
+        in_specs=[vmem] * (4 + cuts[0]),
         out_specs=vmem,
-        compiler_params=limit(16 + 2 * ctxs),
-        cost_estimate=takes(3.2),
-        name="attend",
-    )(qkv, segments[0], norm_gain, w_qkv[0], w_out[0], *own, *[piece for pieces in earlier for piece in pieces])
+        compiler_params=limit(10 + 2 * ctxs),
+        cost_estimate=takes(3.0),
+        name="finish",
+    )(after(qkv, *sent), segments[0], others, w_out[0], *own)
 
     shard = (rows, lane)
     terms = [term for k, g in zip(kept, got) for term in (k, after(g, section_next))]

time: 31.1 us -> 31 us (level)
  waiting for transfers between devices: 12.4 us -> 8.72 us
  starting transfers between devices: 12.2 us -> 15 us
  local copies, waits for them, and re-layouts: 0.2 us -> 0.86 us
    ppermute x6, starting transfers between devices: 8.1 us -> 11.6 us  [flipped(): lax.ppermute(value, axis, [(i, i ^ 1 << bit) for i in range(lax.axis_size...]
    ppermute x6, waiting for transfers between devices: 10.6 us -> 8.47 us  [flipped(): lax.ppermute(value, axis, [(i, i ^ 1 << bit) for i in range(lax.axis_size...]
    ppermute x2, waiting for transfers between devices: 1.84 us -> 0.25 us  [relayed(): return lax.ppermute(section_held, ('pipe', 'ctx'), pairs)]
    ppermute x2, starting transfers between devices: 4.11 us -> 3.41 us  [relayed(): return lax.ppermute(section_held, ('pipe', 'ctx'), pairs)]
    reshape x2, local copies, waits for them, and re-layouts: 0.08 us -> 0.75 us  [on_device(): sent.append(taken.astype(jnp.bfloat16).reshape(shards // 2, hi - lo, lane))]
    pallas_call x1 -> x2, Pallas kernels: 3.15 us -> 3.34 us  [the longest x1 2.51 us: on_device(): pl.pallas_call(functools.partial(finish_kernel, ctxs, range(first_heads,...]
  transfers between devices with their start and end apart: 8 -> 8, of which waited for: 5 -> 5; matrix products, arithmetic and copies ran while one was open for 1% -> 3% of each run, Pallas kernels for 14% -> 15%
where the time goes in v5:
time: 31 us; the launch traced here: 30.9 us
  starting transfers between devices  15 us (48%)
  waiting for transfers between devices  8.72 us (28%)
  Pallas kernels  5.59 us (18%)
  local copies, waits for them, and re-layouts  0.86 us (3%)
  between operations  0.71 us (2%)
    ppermute x6, starting transfers between devices, flipped(): lax.ppermute(value, axis, [(i, i ^ 1 << bit) for i in range(lax.axis_size...  11.6 us
    ppermute x6, waiting for transfers between devices, flipped(): lax.ppermute(value, axis, [(i, i ^ 1 << bit) for i in range(lax.axis_size...  8.47 us
    ppermute x2, starting transfers between devices, relayed(): return lax.ppermute(section_held, ('pipe', 'ctx'), pairs)  3.41 us
    pallas_call x1, Pallas kernels, on_device(): pl.pallas_call(functools.partial(finish_kernel, ctxs, range(first_heads,...  2.51 us
    pallas_call x1, Pallas kernels, on_device(): pl.pallas_call(project_kernel, out_shape=jax.ShapeDtypeStruct((row_count,...  1.1 us
    pallas_call x1, Pallas kernels, on_device(): pl.pallas_call(functools.partial(adam_kernel, starts[:-1]), out_shape=[ja...  0.99 us
    pallas_call x1, Pallas kernels, on_device(): pl.pallas_call(functools.partial(others_kernel, ctxs), out_shape=jax.Shap...  0.83 us
    reshape x2, local copies, waits for them, and re-layouts, on_device(): sent.append(taken.astype(jnp.bfloat16).reshape(shards // 2, hi - lo, lane))  0.75 us
  transfers between devices with their start and end apart: 8, of which 5 were waited for; matrix products, arithmetic and copies ran while one was open for 3% of the time, Pallas kernels for 15%

profile of v5, /device:TPU:0, one launch (start us, length us, event | category | flops | bytes accessed | tf_op | source)
XLA Modules:
  0.0 30.9 jit_solution(17373006753374495269)
XLA Ops:
  0.6 0.0 copy-start
  0.6 2.5 %collective-permute-start.1 = (bf16[1,1,256,1024]{3,2,1,0:T(8,128)(2,1)}, bf16[1,1,256,1024]{3,2,1,0:T(8,128)(2,1)S(1)}, u32[]{:S(2)}, u32[]{:S(2)}) collective-permute-start(bf16[1,1,256,1024]{3,2,1,0:T(8,128)(2,1)} %param.9), channel_id=1, source_target_pairs={{0,12},{4,8},{8,20},{12,16},{16,28},{20,24},{24,4},{28,0},{1,13},{... | collective-permute-start | bytes 1572872 | tf_op jit(solution)/shard_map/ppermute | solution.py:103
  3.1 0.0 copy-done
  3.2 0.0 copy-start.6
  3.2 2.2 %collective-permute-start.2 = (bf16[4,320,128]{2,1,0:T(8,128)(2,1)S(1)}, bf16[4,320,128]{2,1,0:T(8,128)(2,1)S(1)}, u32[]{:S(2)}, u32[]{:S(2)}) collective-permute-start(bf16[4,320,128]{2,1,0:T(8,128)(2,1)S(1)} %fusion), channel_id=1, source_target_pairs={{0,1},{1,0},{2,3},{3,2},{4,5},{5,4},{6,7},{7,6},{8,9},{9,8},{10,11... | collective-permute-start | bytes 983048 | tf_op jit(solution)/shard_map/ppermute | solution.py:57
  5.4 0.7 %fusion.1 = bf16[4,192,128]{2,1,0:T(8,128)(2,1)} fusion(f32[4,2,512,128]{3,2,1,0:T(8,128)S(1)} %bitcast.27, s32[]{:T(128)S(6)} %select_n.10), kind=kLoop, calls=%fused_computation.4 | loop fusion | bytes 393220 | tf_op jit(solution)/shard_map/reshape | solution.py:214
  6.1 0.0 collective-permute-start.3
  6.1 0.0 copy-start.1
  6.1 0.1 dynamic-slice_bitcast_fusion.part_ref
  6.2 1.0 %collective-permute-start = (bf16[1,1,256,1024]{3,2,1,0:T(8,128)(2,1)}, bf16[1,1,256,1024]{3,2,1,0:T(8,128)(2,1)S(1)}, u32[]{:S(2)}, u32[]{:S(2)}) collective-permute-start(bf16[1,1,256,1024]{3,2,1,0:T(8,128)(2,1)} %param.9), channel_id=1, source_target_pairs={{0,8},{4,12},{8,16},{12,20},{16,24},{20,28},{24,0},{28,4},{1,9},{5... | collective-permute-start | bytes 1572872 | tf_op jit(solution)/shard_map/ppermute | solution.py:103
  7.1 6.4 %collective-permute-done.2.got_ref = bf16[4,320,128]{2,1,0:T(8,128)(2,1)S(1)} collective-permute-done((bf16[4,320,128]{2,1,0:T(8,128)(2,1)S(1)}, bf16[4,320,128]{2,1,0:T(8,128)(2,1)S(1)}, u32[]{:S(2)}, u32[]{:S(2)}) %collective-permute-start.2) | collective-permute-done | bytes 327712 | tf_op jit(solution)/shard_map/ppermute | solution.py:57
  13.5 0.1 join.4
  13.6 2.5 %collective-permute-start.4 = (bf16[2,320,128]{2,1,0:T(8,128)(2,1)S(1)}, bf16[2,320,128]{2,1,0:T(8,128)(2,1)S(1)}, u32[]{:S(2)}, u32[]{:S(2)}) collective-permute-start(bf16[2,320,128]{2,1,0:T(8,128)(2,1)S(1)} %get-tuple-element.29), channel_id=1, source_target_pairs={{0,4},{4,0},{1,5},{5,1},{2,6},{6,2},{3,7},{7,3},{8,12},{12,8},{9,1... | collective-permute-start | bytes 491528 | tf_op jit(solution)/shard_map/ppermute | solution.py:57
  16.0 0.3 collective-permute-done.1
  16.3 0.0 copy-done.6
  16.3 0.0 copy-done.1
  16.3 0.8 %others.1.others_ref = bf16[256,1024]{1,0:T(8,128)(2,1)S(1)} custom-call(f32[1,1024]{1,0:T(1,128)S(1)} %copy-done.6, bf16[1024,1536]{1,0:T(8,128)(2,1)S(1)} %bitcast.30, bf16[256,1024]{1,0:T(8,128)(2,1)S(1)} %bitcast.33), custom_call_target="tpu_custom_call" | custom-call | flops 5750000128 | bytes 18450000 | tf_op jit(solution)/shard_map/others/pallas_call | solution.py:237
  17.1 0.6 %collective-permute-done.3.got_ref = bf16[4,192,128]{2,1,0:T(8,128)(2,1)S(1)} collective-permute-done((bf16[4,192,128]{2,1,0:T(8,128)(2,1)}, bf16[4,192,128]{2,1,0:T(8,128)(2,1)S(1)}, u32[]{:S(2)}, u32[]{:S(2)}) %collective-permute-start.3) | collective-permute-done | bytes 196640 | tf_op jit(solution)/shard_map/ppermute | solution.py:57
  17.8 1.5 %collective-permute-start.5 = (bf16[2,192,128]{2,1,0:T(8,128)(2,1)S(1)}, bf16[2,192,128]{2,1,0:T(8,128)(2,1)S(1)}, u32[]{:S(2)}, u32[]{:S(2)}) collective-permute-start(bf16[2,192,128]{2,1,0:T(8,128)(2,1)S(1)} %get-tuple-element.32), channel_id=1, source_target_pairs={{0,4},{4,0},{1,5},{5,1},{2,6},{6,2},{3,7},{7,3},{8,12},{12,8},{9,1... | collective-permute-start | bytes 294920 | tf_op jit(solution)/shard_map/ppermute | solution.py:57
  19.3 0.0 collective-permute-done
  19.3 0.0 copy-start.2
  19.3 0.0 copy-start.7
  19.3 1.1 %project.1.qkv_ref = bf16[256,1536]{1,0:T(8,128)(2,1)S(1)} custom-call(f32[1,1024]{1,0:T(1,128)S(1)} %copy-done.6, bf16[1024,1536]{1,0:T(8,128)(2,1)S(1)} %bitcast.31, bf16[256,1024]{1,0:T(8,128)(2,1)S(1)} %bitcast.34), custom_call_target="tpu_custom_call" | custom-call | flops 1264999936 | bytes 4059000 | tf_op jit(solution)/shard_map/project/pallas_call | solution.py:251
  20.4 0.3 %collective-permute-done.4.got_ref = bf16[2,320,128]{2,1,0:T(8,128)(2,1)S(1)} collective-permute-done((bf16[2,320,128]{2,1,0:T(8,128)(2,1)S(1)}, bf16[2,320,128]{2,1,0:T(8,128)(2,1)S(1)}, u32[]{:S(2)}, u32[]{:S(2)}) %collective-permute-start.4) | collective-permute-done | bytes 163872 | tf_op jit(solution)/shard_map/ppermute | solution.py:57
  20.8 2.7 %collective-permute-start.6 = (bf16[1,320,128]{2,1,0:T(8,128)(2,1)S(1)}, bf16[1,320,128]{2,1,0:T(8,128)(2,1)S(1)}, u32[]{:S(2)}, u32[]{:S(2)}) collective-permute-start(bf16[1,320,128]{2,1,0:T(8,128)(2,1)S(1)} %get-tuple-element.37), channel_id=1, source_target_pairs={{0,2},{1,3},{2,0},{3,1},{4,6},{5,7},{6,4},{7,5},{8,10},{9,11},{10,... | collective-permute-start | bytes 245768 | tf_op jit(solution)/shard_map/ppermute | solution.py:57
  23.5 0.0 collective-permute-done.5.got_ref
  23.5 2.7 %collective-permute-start.7 = (bf16[1,192,128]{2,1,0:T(8,128)(2,1)S(1)}, bf16[1,192,128]{2,1,0:T(8,128)(2,1)S(1)}, u32[]{:S(2)}, u32[]{:S(2)}) collective-permute-start(bf16[1,192,128]{2,1,0:T(8,128)(2,1)S(1)} %get-tuple-element.39), channel_id=1, source_target_pairs={{0,2},{1,3},{2,0},{3,1},{4,6},{5,7},{6,4},{7,5},{8,10},{9,11},{10,... | collective-permute-start | bytes 147464 | tf_op jit(solution)/shard_map/ppermute | solution.py:57
  26.2 0.0 copy-done.2
  26.2 0.0 copy-done.7
  26.2 0.0 copy-start.3
  26.2 0.0 copy-start.4
  26.2 0.0 copy-start.5
  26.2 2.5 %finish.1 = bf16[256,1024]{1,0:T(8,128)(2,1)} custom-call(bf16[256,1536]{1,0:T(8,128)(2,1)S(1)} %project.1.qkv_ref, s32[1,512]{1,0:T(1,128)S(1)} %bitcast.39, bf16[256,1024]{1,0:T(8,128)(2,1)S(1)} %others.1.others_ref, bf16[512,1024]{1,0:T(8,128)(2,1)S(1)} %bitcast.32, bf16[256,1024]{1,0:T(8,128)(2,1)S(1)} %bitcast.35), custom_call_target="tpu_custom_call" | custom-call | flops 3449999872 | bytes 11070000 | tf_op jit(solution)/shard_map/finish/pallas_call | solution.py:269
  28.7 0.0 collective-permute-done.6.refs_1_
  28.8 1.1 %collective-permute-done.7.refs_3_ = bf16[1,192,128]{2,1,0:T(8,128)(2,1)S(1)} collective-permute-done((bf16[1,192,128]{2,1,0:T(8,128)(2,1)S(1)}, bf16[1,192,128]{2,1,0:T(8,128)(2,1)S(1)}, u32[]{:S(2)}, u32[]{:S(2)}) %collective-permute-start.7) | collective-permute-done | bytes 49184 | tf_op jit(solution)/shard_map/ppermute | solution.py:57
  29.9 0.0 copy-done.3
  29.9 0.0 copy-done.4
  29.9 0.0 copy-done.5
  29.9 1.0 %adam.1 = (f32[512,128]{1,0:T(8,128)}, f32[512,128]{1,0:T(8,128)}, f32[512,128]{1,0:T(8,128)}) custom-call(f32[1,320,128]{2,1,0:T(8,128)S(1)} %get-tuple-element.41.refs_0_, bf16[1,320,128]{2,1,0:T(8,128)(2,1)S(1)} %collective-permute-done.6.refs_1_, f32[1,192,128]{2,1,0:T(8,128)S(1)} %get-tuple-element.43.refs_2_, ...), custom_call_target="tpu_custom_call" | custom-call | flops 1150000000 | bytes 3690000 | tf_op jit(solution)/shard_map/adam/pallas_call | solution.py:281
  (4 shorter events, 0.1 us)
Async XLA Ops:
  0.6 2.5 %copy-start = (f32[1,1,1,524288]{3,2,1,0:T(1,128)S(1)}, f32[1,1,1,524288]{3,2,1,0:T(1,128)}, u32[]{:S(2)}) copy-start(f32[1,1,1,524288]{3,2,1,0:T(1,128)} %param.14) | copy-start | bytes 6291460
  0.6 15.6 %collective-permute-start.1 = (bf16[1,1,256,1024]{3,2,1,0:T(8,128)(2,1)}, bf16[1,1,256,1024]{3,2,1,0:T(8,128)(2,1)S(1)}, u32[]{:S(2)}, u32[]{:S(2)}) collective-permute-start(bf16[1,1,256,1024]{3,2,1,0:T(8,128)(2,1)} %param.9), channel_id=1, source_target_pairs={{0,12},{4,8},{8,20},{12,16},{16,28},{20,24},{24,4},{28,0},{1,13},{... | collective-permute-start | bytes 1572872 | tf_op jit(solution)/shard_map/ppermute | solution.py:103
  3.2 13.1 %copy-start.6 = (f32[1,1024]{1,0:T(1,128)S(1)}, f32[1,1024]{1,0:T(1,128)}, u32[]{:S(2)}) copy-start(f32[1,1024]{1,0:T(1,128)} %gain_ref.3) | copy-start | bytes 12292
  3.2 10.3 %collective-permute-start.2 = (bf16[4,320,128]{2,1,0:T(8,128)(2,1)S(1)}, bf16[4,320,128]{2,1,0:T(8,128)(2,1)S(1)}, u32[]{:S(2)}, u32[]{:S(2)}) collective-permute-start(bf16[4,320,128]{2,1,0:T(8,128)(2,1)S(1)} %fusion), channel_id=1, source_target_pairs={{0,1},{1,0},{2,3},{3,2},{4,5},{5,4},{6,7},{7,6},{8,9},{9,8},{10,11... | collective-permute-start | bytes 983048 | tf_op jit(solution)/shard_map/ppermute | solution.py:57
  6.1 11.7 %collective-permute-start.3 = (bf16[4,192,128]{2,1,0:T(8,128)(2,1)}, bf16[4,192,128]{2,1,0:T(8,128)(2,1)S(1)}, u32[]{:S(2)}, u32[]{:S(2)}) collective-permute-start(bf16[4,192,128]{2,1,0:T(8,128)(2,1)} %fusion.1), channel_id=1, source_target_pairs={{0,1},{1,0},{2,3},{3,2},{4,5},{5,4},{6,7},{7,6},{8,9},{9,8},{10,11... | collective-permute-start | bytes 589832 | tf_op jit(solution)/shard_map/ppermute | solution.py:57
  6.1 10.2 %copy-start.1 = (bf16[1,1024,1536]{2,1,0:T(8,128)(2,1)S(1)}, bf16[1,1024,1536]{2,1,0:T(8,128)(2,1)}, u32[]{:S(2)}) copy-start(bf16[1,1024,1536]{2,1,0:T(8,128)(2,1)} %param.12) | copy-start | bytes 9437188
  6.2 13.1 %collective-permute-start = (bf16[1,1,256,1024]{3,2,1,0:T(8,128)(2,1)}, bf16[1,1,256,1024]{3,2,1,0:T(8,128)(2,1)S(1)}, u32[]{:S(2)}, u32[]{:S(2)}) collective-permute-start(bf16[1,1,256,1024]{3,2,1,0:T(8,128)(2,1)} %param.9), channel_id=1, source_target_pairs={{0,8},{4,12},{8,16},{12,20},{16,24},{20,28},{24,0},{28,4},{1,9},{5... | collective-permute-start | bytes 1572872 | tf_op jit(solution)/shard_map/ppermute | solution.py:103
  13.6 7.2 %collective-permute-start.4 = (bf16[2,320,128]{2,1,0:T(8,128)(2,1)S(1)}, bf16[2,320,128]{2,1,0:T(8,128)(2,1)S(1)}, u32[]{:S(2)}, u32[]{:S(2)}) collective-permute-start(bf16[2,320,128]{2,1,0:T(8,128)(2,1)S(1)} %get-tuple-element.29), channel_id=1, source_target_pairs={{0,4},{4,0},{1,5},{5,1},{2,6},{6,2},{3,7},{7,3},{8,12},{12,8},{9,1... | collective-permute-start | bytes 491528 | tf_op jit(solution)/shard_map/ppermute | solution.py:57
  17.8 5.7 %collective-permute-start.5 = (bf16[2,192,128]{2,1,0:T(8,128)(2,1)S(1)}, bf16[2,192,128]{2,1,0:T(8,128)(2,1)S(1)}, u32[]{:S(2)}, u32[]{:S(2)}) collective-permute-start(bf16[2,192,128]{2,1,0:T(8,128)(2,1)S(1)} %get-tuple-element.32), channel_id=1, source_target_pairs={{0,4},{4,0},{1,5},{5,1},{2,6},{6,2},{3,7},{7,3},{8,12},{12,8},{9,1... | collective-permute-start | bytes 294920 | tf_op jit(solution)/shard_map/ppermute | solution.py:57
  19.3 6.9 %copy-start.2 = (bf16[1,512,1024]{2,1,0:T(8,128)(2,1)S(1)}, bf16[1,512,1024]{2,1,0:T(8,128)(2,1)}, u32[]{:S(2)}) copy-start(bf16[1,512,1024]{2,1,0:T(8,128)(2,1)} %param.13) | copy-start | bytes 3145732
  19.3 6.9 %copy-start.7 = (s32[1,1,512]{2,1,0:T(1,128)S(1)}, s32[1,1,512]{2,1,0:T(1,128)}, u32[]{:S(2)}) copy-start(s32[1,1,512]{2,1,0:T(1,128)} %param.10) | copy-start | bytes 6148
  20.8 8.0 %collective-permute-start.6 = (bf16[1,320,128]{2,1,0:T(8,128)(2,1)S(1)}, bf16[1,320,128]{2,1,0:T(8,128)(2,1)S(1)}, u32[]{:S(2)}, u32[]{:S(2)}) collective-permute-start(bf16[1,320,128]{2,1,0:T(8,128)(2,1)S(1)} %get-tuple-element.37), channel_id=1, source_target_pairs={{0,2},{1,3},{2,0},{3,1},{4,6},{5,7},{6,4},{7,5},{8,10},{9,11},{10,... | collective-permute-start | bytes 245768 | tf_op jit(solution)/shard_map/ppermute | solution.py:57
  23.5 6.4 %collective-permute-start.7 = (bf16[1,192,128]{2,1,0:T(8,128)(2,1)S(1)}, bf16[1,192,128]{2,1,0:T(8,128)(2,1)S(1)}, u32[]{:S(2)}, u32[]{:S(2)}) collective-permute-start(bf16[1,192,128]{2,1,0:T(8,128)(2,1)S(1)} %get-tuple-element.39), channel_id=1, source_target_pairs={{0,2},{1,3},{2,0},{3,1},{4,6},{5,7},{6,4},{7,5},{8,10},{9,11},{10,... | collective-permute-start | bytes 147464 | tf_op jit(solution)/shard_map/ppermute | solution.py:57
  26.2 3.7 %copy-start.3 = (f32[1,65536]{1,0:T(1,128)S(1)}, f32[1,65536]{1,0:T(1,128)}, u32[]{:S(2)}) copy-start(f32[1,65536]{1,0:T(1,128)} %param.15) | copy-start | bytes 786436
  26.2 3.7 %copy-start.4 = (f32[1,65536]{1,0:T(1,128)S(1)}, f32[1,65536]{1,0:T(1,128)}, u32[]{:S(2)}) copy-start(f32[1,65536]{1,0:T(1,128)} %param.16) | copy-start | bytes 786436
  26.2 3.7 %copy-start.5 = (f32[1,65536]{1,0:T(1,128)S(1)}, f32[1,65536]{1,0:T(1,128)}, u32[]{:S(2)}) copy-start(f32[1,65536]{1,0:T(1,128)} %param.17) | copy-start | bytes 786436

commit v6 on v4

--- a/solution.py
+++ b/solution.py
@@ -197,7 +197,7 @@
     shards = 1 << len(left)
     rows = count // shards // lane
     part = grad_parts.reshape(shards, rows, lane)
-    starts = [rows * sum(shares[:i]) // sum(shares) for i in range(len(shares) + 1)]
+    starts = [rows * sum(shares[:i]) // sum(shares) // 16 * 16 for i in range(len(shares) + 1)]
     spans = list(zip(starts[:-1], starts[1:]))
     pairs = part.reshape(shards // 2, 2, rows, lane)
     mine, sent = side(*left[-1]), []
@@ -224,8 +224,10 @@
         kept[i], sent[i] = join(left[i], this, kept[i], got[i], start)
         left[i] = [b for b in left[i] if b != this]
 
-    advance(0, 1)
-    own = [after(piece, sent[0], *[p for pieces in earlier for p in pieces]) for piece in own]
+    for i, (lo, _) in enumerate(spans):
+        advance(i, 1, lo)
+        got[i] = flipped(sent[i], *steps[i][1])
+    own = [after(piece, *sent, *[p for pieces in earlier for p in pieces]) for piece in own]
     qkv = pl.pallas_call(
         project_kernel,
         out_shape=jax.ShapeDtypeStruct((row_count, 3 * head_cols), jnp.bfloat16),
@@ -236,11 +238,7 @@
         name="project",
     )(norm_gain, w_qkv[0], *own)
 
-    got[0] = flipped(sent[0], *steps[0][1])
-    got[1:] = [after(g, qkv) for g in got[1:]]
-    for i, (lo, _) in list(enumerate(spans))[1:]:
-        advance(i, 1, lo)
-        got[i] = flipped(sent[i], *steps[i][1])
+    got[0] = after(got[0], qkv)
     for step in range(2, len(steps[0])):
         for i in range(len(spans)):
             advance(i, step)

time: 31.1 us -> 31.8 us (1.023)
  waiting for transfers between devices: 12.4 us -> 13.1 us
    ppermute x6, waiting for transfers between devices: 10.6 us -> 13.1 us  [flipped(): lax.ppermute(value, axis, [(i, i ^ 1 << bit) for i in range(lax.axis_size...]
    ppermute x2, waiting for transfers between devices: 1.84 us -> 0.01 us  [relayed(): return lax.ppermute(section_held, ('pipe', 'ctx'), pairs)]
  transfers between devices with their start and end apart: 8 -> 8, of which waited for: 5 -> 5; matrix products, arithmetic and copies ran while one was open for 1% -> 0% of each run, Pallas kernels for 14% -> 14%
where the time goes in v6:
time: 31.8 us; the launch traced here: 31.7 us
  waiting for transfers between devices  13.1 us (41%)
  starting transfers between devices  12.2 us (38%)
  Pallas kernels  5.37 us (17%)
  between operations  0.76 us (2%)
    ppermute x6, waiting for transfers between devices, flipped(): lax.ppermute(value, axis, [(i, i ^ 1 << bit) for i in range(lax.axis_size...  13.1 us
    ppermute x6, starting transfers between devices, flipped(): lax.ppermute(value, axis, [(i, i ^ 1 << bit) for i in range(lax.axis_size...  8.1 us
    ppermute x2, starting transfers between devices, relayed(): return lax.ppermute(section_held, ('pipe', 'ctx'), pairs)  4.11 us
    pallas_call x1, Pallas kernels, on_device(): pl.pallas_call(functools.partial(attend_kernel, ctxs, cuts), out_shape=ja...  3.15 us
    pallas_call x1, Pallas kernels, on_device(): pl.pallas_call(project_kernel, out_shape=jax.ShapeDtypeStruct((row_count,...  1.08 us
    pallas_call x1, Pallas kernels, on_device(): pl.pallas_call(functools.partial(adam_kernel, starts[:-1]), out_shape=[ja...  0.99 us
  transfers between devices with their start and end apart: 8, of which 5 were waited for; matrix products, arithmetic and copies ran while one was open for 0% of the time, Pallas kernels for 14%

profile of v6, /device:TPU:0, one launch (start us, length us, event | category | flops | bytes accessed | tf_op | source)
XLA Modules:
  0.0 31.7 jit_solution(10310070593664253427)
XLA Ops:
  0.6 0.0 copy-start
  0.6 2.5 %collective-permute-start.3 = (bf16[1,1,256,1024]{3,2,1,0:T(8,128)(2,1)}, bf16[1,1,256,1024]{3,2,1,0:T(8,128)(2,1)S(1)}, u32[]{:S(2)}, u32[]{:S(2)}) collective-permute-start(bf16[1,1,256,1024]{3,2,1,0:T(8,128)(2,1)} %param.9), channel_id=1, source_target_pairs={{0,12},{4,8},{8,20},{12,16},{16,28},{20,24},{24,4},{28,0},{1,13},{... | collective-permute-start | bytes 1572872 | tf_op jit(solution)/shard_map/ppermute | solution.py:103
  3.1 0.0 copy-done
  3.2 0.0 copy-start.1
  3.2 0.0 copy-start.6
  3.2 0.1 dynamic-slice_bitcast_fusion.part_ref
  3.3 1.7 %collective-permute-start = (bf16[1,1,256,1024]{3,2,1,0:T(8,128)(2,1)}, bf16[1,1,256,1024]{3,2,1,0:T(8,128)(2,1)S(1)}, u32[]{:S(2)}, u32[]{:S(2)}) collective-permute-start(bf16[1,1,256,1024]{3,2,1,0:T(8,128)(2,1)} %param.9), channel_id=1, source_target_pairs={{0,8},{4,12},{8,16},{12,20},{16,24},{20,28},{24,0},{28,4},{1,9},{5... | collective-permute-start | bytes 1572872 | tf_op jit(solution)/shard_map/ppermute | solution.py:103
  5.0 1.6 %collective-permute-start.1 = (bf16[4,320,128]{2,1,0:T(8,128)(2,1)S(1)}, bf16[4,320,128]{2,1,0:T(8,128)(2,1)S(1)}, u32[]{:S(2)}, u32[]{:S(2)}) collective-permute-start(bf16[4,320,128]{2,1,0:T(8,128)(2,1)S(1)} %fusion), channel_id=1, source_target_pairs={{0,1},{1,0},{2,3},{3,2},{4,5},{5,4},{6,7},{7,6},{8,9},{9,8},{10,11... | collective-permute-start | bytes 983048 | tf_op jit(solution)/shard_map/ppermute | solution.py:57
  6.5 0.4 %collective-permute-start.2 = (bf16[4,192,128]{2,1,0:T(8,128)(2,1)S(1)}, bf16[4,192,128]{2,1,0:T(8,128)(2,1)S(1)}, u32[]{:S(2)}, u32[]{:S(2)}) collective-permute-start(bf16[4,192,128]{2,1,0:T(8,128)(2,1)S(1)} %fusion.1), channel_id=1, source_target_pairs={{0,1},{1,0},{2,3},{3,2},{4,5},{5,4},{6,7},{7,6},{8,9},{9,8},{10,11... | collective-permute-start | bytes 589832 | tf_op jit(solution)/shard_map/ppermute | solution.py:57
  7.0 8.5 %collective-permute-done.1.got_ref = bf16[4,320,128]{2,1,0:T(8,128)(2,1)S(1)} collective-permute-done((bf16[4,320,128]{2,1,0:T(8,128)(2,1)S(1)}, bf16[4,320,128]{2,1,0:T(8,128)(2,1)S(1)}, u32[]{:S(2)}, u32[]{:S(2)}) %collective-permute-start.1) | collective-permute-done | bytes 327712 | tf_op jit(solution)/shard_map/ppermute | solution.py:57
  15.5 0.1 join.4
  15.5 0.2 collective-permute-start.4
  15.7 3.6 %collective-permute-done.2.got_ref = bf16[4,192,128]{2,1,0:T(8,128)(2,1)S(1)} collective-permute-done((bf16[4,192,128]{2,1,0:T(8,128)(2,1)S(1)}, bf16[4,192,128]{2,1,0:T(8,128)(2,1)S(1)}, u32[]{:S(2)}, u32[]{:S(2)}) %collective-permute-start.2) | collective-permute-done | bytes 196640 | tf_op jit(solution)/shard_map/ppermute | solution.py:57
  19.4 0.5 %collective-permute-start.6 = (bf16[2,192,128]{2,1,0:T(8,128)(2,1)S(1)}, bf16[2,192,128]{2,1,0:T(8,128)(2,1)S(1)}, u32[]{:S(2)}, u32[]{:S(2)}) collective-permute-start(bf16[2,192,128]{2,1,0:T(8,128)(2,1)S(1)} %get-tuple-element.26), channel_id=1, source_target_pairs={{0,4},{4,0},{1,5},{5,1},{2,6},{6,2},{3,7},{7,3},{8,12},{12,8},{9,1... | collective-permute-start | bytes 294920 | tf_op jit(solution)/shard_map/ppermute | solution.py:57
  20.0 0.0 collective-permute-done.3
  20.0 0.0 collective-permute-done
  20.0 0.0 copy-done.1
  20.0 0.0 copy-done.6
  20.0 0.0 copy-start.2
  20.0 0.0 copy-start.7
  20.0 1.1 %project.1.qkv_ref = bf16[256,1536]{1,0:T(8,128)(2,1)S(1)} custom-call(f32[1,1024]{1,0:T(1,128)S(1)} %copy-done.6, bf16[1024,1536]{1,0:T(8,128)(2,1)S(1)} %bitcast.30, bf16[256,1024]{1,0:T(8,128)(2,1)S(1)} %bitcast.32), custom_call_target="tpu_custom_call" | custom-call | flops 1 | bytes 4059000 | tf_op jit(solution)/shard_map/project/pallas_call | solution.py:231
  21.1 0.1 collective-permute-done.4.got_ref
  21.2 2.7 %collective-permute-start.5 = (bf16[1,320,128]{2,1,0:T(8,128)(2,1)S(1)}, bf16[1,320,128]{2,1,0:T(8,128)(2,1)S(1)}, u32[]{:S(2)}, u32[]{:S(2)}) collective-permute-start(bf16[1,320,128]{2,1,0:T(8,128)(2,1)S(1)} %get-tuple-element.31), channel_id=1, source_target_pairs={{0,2},{1,3},{2,0},{3,1},{4,6},{5,7},{6,4},{7,5},{8,10},{9,11},{10,... | collective-permute-start | bytes 245768 | tf_op jit(solution)/shard_map/ppermute | solution.py:57
  23.9 0.2 collective-permute-done.6.got_ref
  24.1 2.7 %collective-permute-start.7 = (bf16[1,192,128]{2,1,0:T(8,128)(2,1)S(1)}, bf16[1,192,128]{2,1,0:T(8,128)(2,1)S(1)}, u32[]{:S(2)}, u32[]{:S(2)}) collective-permute-start(bf16[1,192,128]{2,1,0:T(8,128)(2,1)S(1)} %get-tuple-element.35), channel_id=1, source_target_pairs={{0,2},{1,3},{2,0},{3,1},{4,6},{5,7},{6,4},{7,5},{8,10},{9,11},{10,... | collective-permute-start | bytes 147464 | tf_op jit(solution)/shard_map/ppermute | solution.py:57
  26.8 0.0 copy-done.2
  26.8 0.0 copy-done.7
  26.8 0.0 copy-start.3
  26.8 0.0 copy-start.4
  26.8 0.0 copy-start.5
  26.8 3.2 %attend.1 = bf16[256,1024]{1,0:T(8,128)(2,1)} custom-call(bf16[256,1536]{1,0:T(8,128)(2,1)S(1)} %project.1.qkv_ref, s32[1,512]{1,0:T(1,128)S(1)} %bitcast.39, f32[1,1024]{1,0:T(1,128)S(1)} %copy-done.6, bf16[1024,1536]{1,0:T(8,128)(2,1)S(1)} %bitcast.31, bf16[512,1024]{1,0:T(8,128)(2,1)S(1)} %bitcast.34, bf16[256,1024]{1,0:T(8,128)(2,1)S(1)} %bitcast.33, ...), custom_call_target="tpu_custom_call" | custom-call | flops 1 | bytes 11808000 | tf_op jit(solution)/shard_map/attend/pallas_call | solution.py:247
  30.0 0.7 %collective-permute-done.7.refs_3_ = bf16[1,192,128]{2,1,0:T(8,128)(2,1)S(1)} collective-permute-done((bf16[1,192,128]{2,1,0:T(8,128)(2,1)S(1)}, bf16[1,192,128]{2,1,0:T(8,128)(2,1)S(1)}, u32[]{:S(2)}, u32[]{:S(2)}) %collective-permute-start.7) | collective-permute-done | bytes 49184 | tf_op jit(solution)/shard_map/ppermute | solution.py:57
  30.6 0.0 collective-permute-done.5.refs_1_
  30.7 0.0 copy-done.3
  30.7 0.0 copy-done.4
  30.7 0.0 copy-done.5
  30.7 1.0 %adam.1 = (f32[512,128]{1,0:T(8,128)}, f32[512,128]{1,0:T(8,128)}, f32[512,128]{1,0:T(8,128)}) custom-call(f32[1,320,128]{2,1,0:T(8,128)S(1)} %get-tuple-element.30.refs_0_, bf16[1,320,128]{2,1,0:T(8,128)(2,1)S(1)} %collective-permute-done.5.refs_1_, f32[1,192,128]{2,1,0:T(8,128)S(1)} %get-tuple-element.34.refs_2_, ...), custom_call_target="tpu_custom_call" | custom-call | flops 1 | bytes 3690000 | tf_op jit(solution)/shard_map/adam/pallas_call | solution.py:259
  (5 shorter events, 0.2 us)
Async XLA Ops:
  0.6 2.5 %copy-start = (f32[1,1,1,524288]{3,2,1,0:T(1,128)S(1)}, f32[1,1,1,524288]{3,2,1,0:T(1,128)}, u32[]{:S(2)}) copy-start(f32[1,1,1,524288]{3,2,1,0:T(1,128)} %param.14) | copy-start | bytes 6291460
  0.6 19.3 %collective-permute-start.3 = (bf16[1,1,256,1024]{3,2,1,0:T(8,128)(2,1)}, bf16[1,1,256,1024]{3,2,1,0:T(8,128)(2,1)S(1)}, u32[]{:S(2)}, u32[]{:S(2)}) collective-permute-start(bf16[1,1,256,1024]{3,2,1,0:T(8,128)(2,1)} %param.9), channel_id=1, source_target_pairs={{0,12},{4,8},{8,20},{12,16},{16,28},{20,24},{24,4},{28,0},{1,13},{... | collective-permute-start | bytes 1572872 | tf_op jit(solution)/shard_map/ppermute | solution.py:103
  3.2 16.8 %copy-start.1 = (bf16[1,1024,1536]{2,1,0:T(8,128)(2,1)S(1)}, bf16[1,1024,1536]{2,1,0:T(8,128)(2,1)}, u32[]{:S(2)}) copy-start(bf16[1,1024,1536]{2,1,0:T(8,128)(2,1)} %param.12) | copy-start | bytes 9437188
  3.2 16.8 %copy-start.6 = (f32[1,1024]{1,0:T(1,128)S(1)}, f32[1,1024]{1,0:T(1,128)}, u32[]{:S(2)}) copy-start(f32[1,1024]{1,0:T(1,128)} %gain_ref.3) | copy-start | bytes 12292
  3.3 16.6 %collective-permute-start = (bf16[1,1,256,1024]{3,2,1,0:T(8,128)(2,1)}, bf16[1,1,256,1024]{3,2,1,0:T(8,128)(2,1)S(1)}, u32[]{:S(2)}, u32[]{:S(2)}) collective-permute-start(bf16[1,1,256,1024]{3,2,1,0:T(8,128)(2,1)} %param.9), channel_id=1, source_target_pairs={{0,8},{4,12},{8,16},{12,20},{16,24},{20,28},{24,0},{28,4},{1,9},{5... | collective-permute-start | bytes 1572872 | tf_op jit(solution)/shard_map/ppermute | solution.py:103
  5.0 10.5 %collective-permute-start.1 = (bf16[4,320,128]{2,1,0:T(8,128)(2,1)S(1)}, bf16[4,320,128]{2,1,0:T(8,128)(2,1)S(1)}, u32[]{:S(2)}, u32[]{:S(2)}) collective-permute-start(bf16[4,320,128]{2,1,0:T(8,128)(2,1)S(1)} %fusion), channel_id=1, source_target_pairs={{0,1},{1,0},{2,3},{3,2},{4,5},{5,4},{6,7},{7,6},{8,9},{9,8},{10,11... | collective-permute-start | bytes 983048 | tf_op jit(solution)/shard_map/ppermute | solution.py:57
  6.5 12.8 %collective-permute-start.2 = (bf16[4,192,128]{2,1,0:T(8,128)(2,1)S(1)}, bf16[4,192,128]{2,1,0:T(8,128)(2,1)S(1)}, u32[]{:S(2)}, u32[]{:S(2)}) collective-permute-start(bf16[4,192,128]{2,1,0:T(8,128)(2,1)S(1)} %fusion.1), channel_id=1, source_target_pairs={{0,1},{1,0},{2,3},{3,2},{4,5},{5,4},{6,7},{7,6},{8,9},{9,8},{10,11... | collective-permute-start | bytes 589832 | tf_op jit(solution)/shard_map/ppermute | solution.py:57
  15.5 5.7 %collective-permute-start.4 = (bf16[2,320,128]{2,1,0:T(8,128)(2,1)S(1)}, bf16[2,320,128]{2,1,0:T(8,128)(2,1)S(1)}, u32[]{:S(2)}, u32[]{:S(2)}) collective-permute-start(bf16[2,320,128]{2,1,0:T(8,128)(2,1)S(1)} %get-tuple-element.25), channel_id=1, source_target_pairs={{0,4},{4,0},{1,5},{5,1},{2,6},{6,2},{3,7},{7,3},{8,12},{12,8},{9,1... | collective-permute-start | bytes 491528 | tf_op jit(solution)/shard_map/ppermute | solution.py:57
  19.4 4.7 %collective-permute-start.6 = (bf16[2,192,128]{2,1,0:T(8,128)(2,1)S(1)}, bf16[2,192,128]{2,1,0:T(8,128)(2,1)S(1)}, u32[]{:S(2)}, u32[]{:S(2)}) collective-permute-start(bf16[2,192,128]{2,1,0:T(8,128)(2,1)S(1)} %get-tuple-element.26), channel_id=1, source_target_pairs={{0,4},{4,0},{1,5},{5,1},{2,6},{6,2},{3,7},{7,3},{8,12},{12,8},{9,1... | collective-permute-start | bytes 294920 | tf_op jit(solution)/shard_map/ppermute | solution.py:57
  20.0 6.8 %copy-start.2 = (bf16[1,512,1024]{2,1,0:T(8,128)(2,1)S(1)}, bf16[1,512,1024]{2,1,0:T(8,128)(2,1)}, u32[]{:S(2)}) copy-start(bf16[1,512,1024]{2,1,0:T(8,128)(2,1)} %param.13) | copy-start | bytes 3145732
  20.0 6.8 %copy-start.7 = (s32[1,1,512]{2,1,0:T(1,128)S(1)}, s32[1,1,512]{2,1,0:T(1,128)}, u32[]{:S(2)}) copy-start(s32[1,1,512]{2,1,0:T(1,128)} %param.10) | copy-start | bytes 6148
  21.2 9.4 %collective-permute-start.5 = (bf16[1,320,128]{2,1,0:T(8,128)(2,1)S(1)}, bf16[1,320,128]{2,1,0:T(8,128)(2,1)S(1)}, u32[]{:S(2)}, u32[]{:S(2)}) collective-permute-start(bf16[1,320,128]{2,1,0:T(8,128)(2,1)S(1)} %get-tuple-element.31), channel_id=1, source_target_pairs={{0,2},{1,3},{2,0},{3,1},{4,6},{5,7},{6,4},{7,5},{8,10},{9,11},{10,... | collective-permute-start | bytes 245768 | tf_op jit(solution)/shard_map/ppermute | solution.py:57
  24.1 6.5 %collective-permute-start.7 = (bf16[1,192,128]{2,1,0:T(8,128)(2,1)S(1)}, bf16[1,192,128]{2,1,0:T(8,128)(2,1)S(1)}, u32[]{:S(2)}, u32[]{:S(2)}) collective-permute-start(bf16[1,192,128]{2,1,0:T(8,128)(2,1)S(1)} %get-tuple-element.35), channel_id=1, source_target_pairs={{0,2},{1,3},{2,0},{3,1},{4,6},{5,7},{6,4},{7,5},{8,10},{9,11},{10,... | collective-permute-start | bytes 147464 | tf_op jit(solution)/shard_map/ppermute | solution.py:57
  26.8 3.9 %copy-start.3 = (f32[1,65536]{1,0:T(1,128)S(1)}, f32[1,65536]{1,0:T(1,128)}, u32[]{:S(2)}) copy-start(f32[1,65536]{1,0:T(1,128)} %param.15) | copy-start | bytes 786436
  26.8 3.9 %copy-start.4 = (f32[1,65536]{1,0:T(1,128)S(1)}, f32[1,65536]{1,0:T(1,128)}, u32[]{:S(2)}) copy-start(f32[1,65536]{1,0:T(1,128)} %param.16) | copy-start | bytes 786436
  26.8 3.9 %copy-start.5 = (f32[1,65536]{1,0:T(1,128)S(1)}, f32[1,65536]{1,0:T(1,128)}, u32[]{:S(2)}) copy-start(f32[1,65536]{1,0:T(1,128)} %param.17) | copy-start | bytes 786436

commit v7 on v5

--- a/solution.py
+++ b/solution.py
@@ -20,7 +20,7 @@
 fix_one = 0.9999734386011124
 fix_two = 0.09520785288629038
 lane = 128
-shares = (5, 3)
+shares = (19, 13)
 ctx_first = (True, True)
 
 

time: 31 us -> 31.3 us (level)
  starting transfers between devices: 15 us -> 15.4 us
    ppermute x6, waiting for transfers between devices: 8.47 us -> 7.67 us  [flipped(): lax.ppermute(value, axis, [(i, i ^ 1 << bit) for i in range(lax.axis_size...]
    ppermute x2, waiting for transfers between devices: 0.25 us -> 0.96 us  [relayed(): return lax.ppermute(section_held, ('pipe', 'ctx'), pairs)]
    ppermute x6, starting transfers between devices: 11.6 us -> 11.9 us  [flipped(): lax.ppermute(value, axis, [(i, i ^ 1 << bit) for i in range(lax.axis_size...]
where the time goes in v7:
time: 31.3 us; the launch traced here: 31.2 us
  starting transfers between devices  15.4 us (49%)
  waiting for transfers between devices  8.63 us (28%)
  Pallas kernels  5.6 us (18%)
  local copies, waits for them, and re-layouts  0.86 us (3%)
  between operations  0.72 us (2%)
    ppermute x6, starting transfers between devices, flipped(): lax.ppermute(value, axis, [(i, i ^ 1 << bit) for i in range(lax.axis_size...  11.9 us
    ppermute x6, waiting for transfers between devices, flipped(): lax.ppermute(value, axis, [(i, i ^ 1 << bit) for i in range(lax.axis_size...  7.67 us
    ppermute x2, starting transfers between devices, relayed(): return lax.ppermute(section_held, ('pipe', 'ctx'), pairs)  3.41 us
    pallas_call x1, Pallas kernels, on_device(): pl.pallas_call(functools.partial(finish_kernel, ctxs, range(first_heads,...  2.51 us
    pallas_call x1, Pallas kernels, on_device(): pl.pallas_call(project_kernel, out_shape=jax.ShapeDtypeStruct((row_count,...  1.1 us
    pallas_call x1, Pallas kernels, on_device(): pl.pallas_call(functools.partial(adam_kernel, starts[:-1]), out_shape=[ja...  0.99 us
    ppermute x2, waiting for transfers between devices, relayed(): return lax.ppermute(section_held, ('pipe', 'ctx'), pairs)  0.96 us
    pallas_call x1, Pallas kernels, on_device(): pl.pallas_call(functools.partial(others_kernel, ctxs), out_shape=jax.Shap...  0.83 us
  transfers between devices with their start and end apart: 8, of which 5 were waited for; matrix products, arithmetic and copies ran while one was open for 3% of the time, Pallas kernels for 15%

profile of v7, /device:TPU:0, one launch (start us, length us, event | category | flops | bytes accessed | tf_op | source)
XLA Modules:
  0.0 31.2 jit_solution(16342208299399102945)
XLA Ops:
  0.6 0.0 copy-start
  0.6 2.5 %collective-permute-start.1 = (bf16[1,1,256,1024]{3,2,1,0:T(8,128)(2,1)}, bf16[1,1,256,1024]{3,2,1,0:T(8,128)(2,1)S(1)}, u32[]{:S(2)}, u32[]{:S(2)}) collective-permute-start(bf16[1,1,256,1024]{3,2,1,0:T(8,128)(2,1)} %param.9), channel_id=1, source_target_pairs={{0,12},{4,8},{8,20},{12,16},{16,28},{20,24},{24,4},{28,0},{1,13},{... | collective-permute-start | bytes 1572872 | tf_op jit(solution)/shard_map/ppermute | solution.py:103
  3.1 0.0 copy-done
  3.2 0.0 copy-start.6
  3.2 2.2 %collective-permute-start.2 = (bf16[4,304,128]{2,1,0:T(8,128)(2,1)S(1)}, bf16[4,304,128]{2,1,0:T(8,128)(2,1)S(1)}, u32[]{:S(2)}, u32[]{:S(2)}) collective-permute-start(bf16[4,304,128]{2,1,0:T(8,128)(2,1)S(1)} %fusion), channel_id=1, source_target_pairs={{0,1},{1,0},{2,3},{3,2},{4,5},{5,4},{6,7},{7,6},{8,9},{9,8},{10,11... | collective-permute-start | bytes 933896 | tf_op jit(solution)/shard_map/ppermute | solution.py:57
  5.4 0.7 %fusion.1 = bf16[4,208,128]{2,1,0:T(8,128)(2,1)} fusion(f32[4,2,512,128]{3,2,1,0:T(8,128)S(1)} %bitcast.27, s32[]{:T(128)S(6)} %select_n.10), kind=kLoop, calls=%fused_computation.4 | loop fusion | bytes 425988 | tf_op jit(solution)/shard_map/reshape | solution.py:214
  6.1 0.0 collective-permute-start.3
  6.1 0.0 copy-start.1
  6.1 0.1 dynamic-slice_bitcast_fusion.part_ref
  6.2 1.0 %collective-permute-start = (bf16[1,1,256,1024]{3,2,1,0:T(8,128)(2,1)}, bf16[1,1,256,1024]{3,2,1,0:T(8,128)(2,1)S(1)}, u32[]{:S(2)}, u32[]{:S(2)}) collective-permute-start(bf16[1,1,256,1024]{3,2,1,0:T(8,128)(2,1)} %param.9), channel_id=1, source_target_pairs={{0,8},{4,12},{8,16},{12,20},{16,24},{20,28},{24,0},{28,4},{1,9},{5... | collective-permute-start | bytes 1572872 | tf_op jit(solution)/shard_map/ppermute | solution.py:103
  7.1 6.0 %collective-permute-done.2.got_ref = bf16[4,304,128]{2,1,0:T(8,128)(2,1)S(1)} collective-permute-done((bf16[4,304,128]{2,1,0:T(8,128)(2,1)S(1)}, bf16[4,304,128]{2,1,0:T(8,128)(2,1)S(1)}, u32[]{:S(2)}, u32[]{:S(2)}) %collective-permute-start.2) | collective-permute-done | bytes 311328 | tf_op jit(solution)/shard_map/ppermute | solution.py:57
  13.2 0.1 join.4
  13.2 2.5 %collective-permute-start.4 = (bf16[2,304,128]{2,1,0:T(8,128)(2,1)S(1)}, bf16[2,304,128]{2,1,0:T(8,128)(2,1)S(1)}, u32[]{:S(2)}, u32[]{:S(2)}) collective-permute-start(bf16[2,304,128]{2,1,0:T(8,128)(2,1)S(1)} %get-tuple-element.29), channel_id=1, source_target_pairs={{0,4},{4,0},{1,5},{5,1},{2,6},{6,2},{3,7},{7,3},{8,12},{12,8},{9,1... | collective-permute-start | bytes 466952 | tf_op jit(solution)/shard_map/ppermute | solution.py:57
  15.7 1.0 %collective-permute-done.1 = bf16[1,1,256,1024]{3,2,1,0:T(8,128)(2,1)S(1)} collective-permute-done((bf16[1,1,256,1024]{3,2,1,0:T(8,128)(2,1)}, bf16[1,1,256,1024]{3,2,1,0:T(8,128)(2,1)S(1)}, u32[]{:S(2)}, u32[]{:S(2)}) %collective-permute-start.1) | collective-permute-done | bytes 524320 | tf_op jit(solution)/shard_map/ppermute | solution.py:103
  16.6 0.0 copy-done.6
  16.6 0.0 copy-done.1
  16.6 0.8 %others.1.others_ref = bf16[256,1024]{1,0:T(8,128)(2,1)S(1)} custom-call(f32[1,1024]{1,0:T(1,128)S(1)} %copy-done.6, bf16[1024,1536]{1,0:T(8,128)(2,1)S(1)} %bitcast.30, bf16[256,1024]{1,0:T(8,128)(2,1)S(1)} %bitcast.33), custom_call_target="tpu_custom_call" | custom-call | flops 5750000128 | bytes 18450000 | tf_op jit(solution)/shard_map/others/pallas_call | solution.py:237
  17.5 0.3 collective-permute-done.3.got_ref
  17.8 1.5 %collective-permute-start.5 = (bf16[2,208,128]{2,1,0:T(8,128)(2,1)S(1)}, bf16[2,208,128]{2,1,0:T(8,128)(2,1)S(1)}, u32[]{:S(2)}, u32[]{:S(2)}) collective-permute-start(bf16[2,208,128]{2,1,0:T(8,128)(2,1)S(1)} %get-tuple-element.32), channel_id=1, source_target_pairs={{0,4},{4,0},{1,5},{5,1},{2,6},{6,2},{3,7},{7,3},{8,12},{12,8},{9,1... | collective-permute-start | bytes 319496 | tf_op jit(solution)/shard_map/ppermute | solution.py:57
  19.3 0.0 collective-permute-done
  19.3 0.0 copy-start.2
  19.3 0.0 copy-start.7
  19.3 1.1 %project.1.qkv_ref = bf16[256,1536]{1,0:T(8,128)(2,1)S(1)} custom-call(f32[1,1024]{1,0:T(1,128)S(1)} %copy-done.6, bf16[1024,1536]{1,0:T(8,128)(2,1)S(1)} %bitcast.31, bf16[256,1024]{1,0:T(8,128)(2,1)S(1)} %bitcast.34), custom_call_target="tpu_custom_call" | custom-call | flops 1264999936 | bytes 4059000 | tf_op jit(solution)/shard_map/project/pallas_call | solution.py:251
  20.4 0.0 collective-permute-done.4.got_ref
  20.5 2.7 %collective-permute-start.6 = (bf16[1,304,128]{2,1,0:T(8,128)(2,1)S(1)}, bf16[1,304,128]{2,1,0:T(8,128)(2,1)S(1)}, u32[]{:S(2)}, u32[]{:S(2)}) collective-permute-start(bf16[1,304,128]{2,1,0:T(8,128)(2,1)S(1)} %get-tuple-element.37), channel_id=1, source_target_pairs={{0,2},{1,3},{2,0},{3,1},{4,6},{5,7},{6,4},{7,5},{8,10},{9,11},{10,... | collective-permute-start | bytes 233480 | tf_op jit(solution)/shard_map/ppermute | solution.py:57
  23.1 0.1 collective-permute-done.5.got_ref
  23.3 3.1 %collective-permute-start.7 = (bf16[1,208,128]{2,1,0:T(8,128)(2,1)S(1)}, bf16[1,208,128]{2,1,0:T(8,128)(2,1)S(1)}, u32[]{:S(2)}, u32[]{:S(2)}) collective-permute-start(bf16[1,208,128]{2,1,0:T(8,128)(2,1)S(1)} %get-tuple-element.39), channel_id=1, source_target_pairs={{0,2},{1,3},{2,0},{3,1},{4,6},{5,7},{6,4},{7,5},{8,10},{9,11},{10,... | collective-permute-start | bytes 159752 | tf_op jit(solution)/shard_map/ppermute | solution.py:57
  26.4 0.0 copy-done.2
  26.4 0.0 copy-done.7
  26.4 0.0 copy-start.3
  26.4 0.0 copy-start.4
  26.4 0.0 copy-start.5
  26.4 2.5 %finish.1 = bf16[256,1024]{1,0:T(8,128)(2,1)} custom-call(bf16[256,1536]{1,0:T(8,128)(2,1)S(1)} %project.1.qkv_ref, s32[1,512]{1,0:T(1,128)S(1)} %bitcast.39, bf16[256,1024]{1,0:T(8,128)(2,1)S(1)} %others.1.others_ref, bf16[512,1024]{1,0:T(8,128)(2,1)S(1)} %bitcast.32, bf16[256,1024]{1,0:T(8,128)(2,1)S(1)} %bitcast.35), custom_call_target="tpu_custom_call" | custom-call | flops 3449999872 | bytes 11070000 | tf_op jit(solution)/shard_map/finish/pallas_call | solution.py:269
  28.9 0.0 collective-permute-done.6.refs_1_
  28.9 1.2 %collective-permute-done.7.refs_3_ = bf16[1,208,128]{2,1,0:T(8,128)(2,1)S(1)} collective-permute-done((bf16[1,208,128]{2,1,0:T(8,128)(2,1)S(1)}, bf16[1,208,128]{2,1,0:T(8,128)(2,1)S(1)}, u32[]{:S(2)}, u32[]{:S(2)}) %collective-permute-start.7) | collective-permute-done | bytes 53280 | tf_op jit(solution)/shard_map/ppermute | solution.py:57
  30.2 0.0 copy-done.3
  30.2 0.0 copy-done.4
  30.2 0.0 copy-done.5
  30.2 1.0 %adam.1 = (f32[512,128]{1,0:T(8,128)}, f32[512,128]{1,0:T(8,128)}, f32[512,128]{1,0:T(8,128)}) custom-call(f32[1,304,128]{2,1,0:T(8,128)S(1)} %get-tuple-element.41.refs_0_, bf16[1,304,128]{2,1,0:T(8,128)(2,1)S(1)} %collective-permute-done.6.refs_1_, f32[1,208,128]{2,1,0:T(8,128)S(1)} %get-tuple-element.43.refs_2_, ...), custom_call_target="tpu_custom_call" | custom-call | flops 1150000000 | bytes 3690000 | tf_op jit(solution)/shard_map/adam/pallas_call | solution.py:281
  (4 shorter events, 0.2 us)
Async XLA Ops:
  0.6 2.5 %copy-start = (f32[1,1,1,524288]{3,2,1,0:T(1,128)S(1)}, f32[1,1,1,524288]{3,2,1,0:T(1,128)}, u32[]{:S(2)}) copy-start(f32[1,1,1,524288]{3,2,1,0:T(1,128)} %param.14) | copy-start | bytes 6291460
  0.6 16.0 %collective-permute-start.1 = (bf16[1,1,256,1024]{3,2,1,0:T(8,128)(2,1)}, bf16[1,1,256,1024]{3,2,1,0:T(8,128)(2,1)S(1)}, u32[]{:S(2)}, u32[]{:S(2)}) collective-permute-start(bf16[1,1,256,1024]{3,2,1,0:T(8,128)(2,1)} %param.9), channel_id=1, source_target_pairs={{0,12},{4,8},{8,20},{12,16},{16,28},{20,24},{24,4},{28,0},{1,13},{... | collective-permute-start | bytes 1572872 | tf_op jit(solution)/shard_map/ppermute | solution.py:103
  3.2 13.5 %copy-start.6 = (f32[1,1024]{1,0:T(1,128)S(1)}, f32[1,1024]{1,0:T(1,128)}, u32[]{:S(2)}) copy-start(f32[1,1024]{1,0:T(1,128)} %gain_ref.3) | copy-start | bytes 12292
  3.2 10.0 %collective-permute-start.2 = (bf16[4,304,128]{2,1,0:T(8,128)(2,1)S(1)}, bf16[4,304,128]{2,1,0:T(8,128)(2,1)S(1)}, u32[]{:S(2)}, u32[]{:S(2)}) collective-permute-start(bf16[4,304,128]{2,1,0:T(8,128)(2,1)S(1)} %fusion), channel_id=1, source_target_pairs={{0,1},{1,0},{2,3},{3,2},{4,5},{5,4},{6,7},{7,6},{8,9},{9,8},{10,11... | collective-permute-start | bytes 933896 | tf_op jit(solution)/shard_map/ppermute | solution.py:57
  6.1 11.6 %collective-permute-start.3 = (bf16[4,208,128]{2,1,0:T(8,128)(2,1)}, bf16[4,208,128]{2,1,0:T(8,128)(2,1)S(1)}, u32[]{:S(2)}, u32[]{:S(2)}) collective-permute-start(bf16[4,208,128]{2,1,0:T(8,128)(2,1)} %fusion.1), channel_id=1, source_target_pairs={{0,1},{1,0},{2,3},{3,2},{4,5},{5,4},{6,7},{7,6},{8,9},{9,8},{10,11... | collective-permute-start | bytes 638984 | tf_op jit(solution)/shard_map/ppermute | solution.py:57
  6.1 10.5 %copy-start.1 = (bf16[1,1024,1536]{2,1,0:T(8,128)(2,1)S(1)}, bf16[1,1024,1536]{2,1,0:T(8,128)(2,1)}, u32[]{:S(2)}) copy-start(bf16[1,1024,1536]{2,1,0:T(8,128)(2,1)} %param.12) | copy-start | bytes 9437188
  6.2 13.1 %collective-permute-start = (bf16[1,1,256,1024]{3,2,1,0:T(8,128)(2,1)}, bf16[1,1,256,1024]{3,2,1,0:T(8,128)(2,1)S(1)}, u32[]{:S(2)}, u32[]{:S(2)}) collective-permute-start(bf16[1,1,256,1024]{3,2,1,0:T(8,128)(2,1)} %param.9), channel_id=1, source_target_pairs={{0,8},{4,12},{8,16},{12,20},{16,24},{20,28},{24,0},{28,4},{1,9},{5... | collective-permute-start | bytes 1572872 | tf_op jit(solution)/shard_map/ppermute | solution.py:103
  13.2 7.2 %collective-permute-start.4 = (bf16[2,304,128]{2,1,0:T(8,128)(2,1)S(1)}, bf16[2,304,128]{2,1,0:T(8,128)(2,1)S(1)}, u32[]{:S(2)}, u32[]{:S(2)}) collective-permute-start(bf16[2,304,128]{2,1,0:T(8,128)(2,1)S(1)} %get-tuple-element.29), channel_id=1, source_target_pairs={{0,4},{4,0},{1,5},{5,1},{2,6},{6,2},{3,7},{7,3},{8,12},{12,8},{9,1... | collective-permute-start | bytes 466952 | tf_op jit(solution)/shard_map/ppermute | solution.py:57
  17.8 5.5 %collective-permute-start.5 = (bf16[2,208,128]{2,1,0:T(8,128)(2,1)S(1)}, bf16[2,208,128]{2,1,0:T(8,128)(2,1)S(1)}, u32[]{:S(2)}, u32[]{:S(2)}) collective-permute-start(bf16[2,208,128]{2,1,0:T(8,128)(2,1)S(1)} %get-tuple-element.32), channel_id=1, source_target_pairs={{0,4},{4,0},{1,5},{5,1},{2,6},{6,2},{3,7},{7,3},{8,12},{12,8},{9,1... | collective-permute-start | bytes 319496 | tf_op jit(solution)/shard_map/ppermute | solution.py:57
  19.3 7.1 %copy-start.2 = (bf16[1,512,1024]{2,1,0:T(8,128)(2,1)S(1)}, bf16[1,512,1024]{2,1,0:T(8,128)(2,1)}, u32[]{:S(2)}) copy-start(bf16[1,512,1024]{2,1,0:T(8,128)(2,1)} %param.13) | copy-start | bytes 3145732
  19.3 7.1 %copy-start.7 = (s32[1,1,512]{2,1,0:T(1,128)S(1)}, s32[1,1,512]{2,1,0:T(1,128)}, u32[]{:S(2)}) copy-start(s32[1,1,512]{2,1,0:T(1,128)} %param.10) | copy-start | bytes 6148
  20.5 8.5 %collective-permute-start.6 = (bf16[1,304,128]{2,1,0:T(8,128)(2,1)S(1)}, bf16[1,304,128]{2,1,0:T(8,128)(2,1)S(1)}, u32[]{:S(2)}, u32[]{:S(2)}) collective-permute-start(bf16[1,304,128]{2,1,0:T(8,128)(2,1)S(1)} %get-tuple-element.37), channel_id=1, source_target_pairs={{0,2},{1,3},{2,0},{3,1},{4,6},{5,7},{6,4},{7,5},{8,10},{9,11},{10,... | collective-permute-start | bytes 233480 | tf_op jit(solution)/shard_map/ppermute | solution.py:57
  23.3 6.9 %collective-permute-start.7 = (bf16[1,208,128]{2,1,0:T(8,128)(2,1)S(1)}, bf16[1,208,128]{2,1,0:T(8,128)(2,1)S(1)}, u32[]{:S(2)}, u32[]{:S(2)}) collective-permute-start(bf16[1,208,128]{2,1,0:T(8,128)(2,1)S(1)} %get-tuple-element.39), channel_id=1, source_target_pairs={{0,2},{1,3},{2,0},{3,1},{4,6},{5,7},{6,4},{7,5},{8,10},{9,11},{10,... | collective-permute-start | bytes 159752 | tf_op jit(solution)/shard_map/ppermute | solution.py:57
  26.4 3.8 %copy-start.3 = (f32[1,65536]{1,0:T(1,128)S(1)}, f32[1,65536]{1,0:T(1,128)}, u32[]{:S(2)}) copy-start(f32[1,65536]{1,0:T(1,128)} %param.15) | copy-start | bytes 786436
  26.4 3.8 %copy-start.4 = (f32[1,65536]{1,0:T(1,128)S(1)}, f32[1,65536]{1,0:T(1,128)}, u32[]{:S(2)}) copy-start(f32[1,65536]{1,0:T(1,128)} %param.16) | copy-start | bytes 786436
  26.4 3.8 %copy-start.5 = (f32[1,65536]{1,0:T(1,128)S(1)}, f32[1,65536]{1,0:T(1,128)}, u32[]{:S(2)}) copy-start(f32[1,65536]{1,0:T(1,128)} %param.17) | copy-start | bytes 786436

commit v8 on v5

--- a/solution.py
+++ b/solution.py
@@ -187,7 +187,7 @@
         master_row = master_ref[span, :]
         new_moment = beta_one * moment_ref[span, :] + (1.0 - beta_one) * grad_sum
         new_second = beta_two * second_ref[span, :] + (1.0 - beta_two) * grad_sum * grad_sum
-        update = new_moment / fix_one / (jnp.sqrt(new_second / fix_two) + adam_eps) + decay * master_row
+        update = new_moment * (1.0 / fix_one) / (jnp.sqrt(new_second * (1.0 / fix_two)) + adam_eps) + decay * master_row
         new_master_ref[span, :] = master_row - rate * update
         new_moment_ref[span, :] = new_moment
         new_second_ref[span, :] = new_second

time: 31 us -> 31 us (level)
  no operation moved by 1% of the time
where the time goes in v8:
time: 31 us; the launch traced here: 30.9 us
  starting transfers between devices  15 us (48%)
  waiting for transfers between devices  8.72 us (28%)
  Pallas kernels  5.59 us (18%)
  local copies, waits for them, and re-layouts  0.86 us (3%)
  between operations  0.71 us (2%)
    ppermute x6, starting transfers between devices, flipped(): lax.ppermute(value, axis, [(i, i ^ 1 << bit) for i in range(lax.axis_size...  11.6 us
    ppermute x6, waiting for transfers between devices, flipped(): lax.ppermute(value, axis, [(i, i ^ 1 << bit) for i in range(lax.axis_size...  8.47 us
    ppermute x2, starting transfers between devices, relayed(): return lax.ppermute(section_held, ('pipe', 'ctx'), pairs)  3.41 us
    pallas_call x1, Pallas kernels, on_device(): pl.pallas_call(functools.partial(finish_kernel, ctxs, range(first_heads,...  2.51 us
    pallas_call x1, Pallas kernels, on_device(): pl.pallas_call(project_kernel, out_shape=jax.ShapeDtypeStruct((row_count,...  1.1 us
    pallas_call x1, Pallas kernels, on_device(): pl.pallas_call(functools.partial(adam_kernel, starts[:-1]), out_shape=[ja...  0.99 us
    pallas_call x1, Pallas kernels, on_device(): pl.pallas_call(functools.partial(others_kernel, ctxs), out_shape=jax.Shap...  0.83 us
    reshape x2, local copies, waits for them, and re-layouts, on_device(): sent.append(taken.astype(jnp.bfloat16).reshape(shards // 2, hi - lo, lane))  0.75 us
  transfers between devices with their start and end apart: 8, of which 5 were waited for; matrix products, arithmetic and copies ran while one was open for 3% of the time, Pallas kernels for 15%

profile of v8, /device:TPU:0, one launch (start us, length us, event | category | flops | bytes accessed | tf_op | source)
XLA Modules:
  0.0 30.9 jit_solution(17373006753374495269)
XLA Ops:
  0.6 0.0 copy-start
  0.6 2.5 %collective-permute-start.1 = (bf16[1,1,256,1024]{3,2,1,0:T(8,128)(2,1)}, bf16[1,1,256,1024]{3,2,1,0:T(8,128)(2,1)S(1)}, u32[]{:S(2)}, u32[]{:S(2)}) collective-permute-start(bf16[1,1,256,1024]{3,2,1,0:T(8,128)(2,1)} %param.9), channel_id=1, source_target_pairs={{0,12},{4,8},{8,20},{12,16},{16,28},{20,24},{24,4},{28,0},{1,13},{... | collective-permute-start | bytes 1572872 | tf_op jit(solution)/shard_map/ppermute | solution.py:103
  3.1 0.0 copy-done
  3.2 0.0 copy-start.6
  3.2 2.2 %collective-permute-start.2 = (bf16[4,320,128]{2,1,0:T(8,128)(2,1)S(1)}, bf16[4,320,128]{2,1,0:T(8,128)(2,1)S(1)}, u32[]{:S(2)}, u32[]{:S(2)}) collective-permute-start(bf16[4,320,128]{2,1,0:T(8,128)(2,1)S(1)} %fusion), channel_id=1, source_target_pairs={{0,1},{1,0},{2,3},{3,2},{4,5},{5,4},{6,7},{7,6},{8,9},{9,8},{10,11... | collective-permute-start | bytes 983048 | tf_op jit(solution)/shard_map/ppermute | solution.py:57
  5.4 0.7 %fusion.1 = bf16[4,192,128]{2,1,0:T(8,128)(2,1)} fusion(f32[4,2,512,128]{3,2,1,0:T(8,128)S(1)} %bitcast.27, s32[]{:T(128)S(6)} %select_n.10), kind=kLoop, calls=%fused_computation.4 | loop fusion | bytes 393220 | tf_op jit(solution)/shard_map/reshape | solution.py:214
  6.1 0.0 collective-permute-start.3
  6.1 0.0 copy-start.1
  6.1 0.1 dynamic-slice_bitcast_fusion.part_ref
  6.2 1.0 %collective-permute-start = (bf16[1,1,256,1024]{3,2,1,0:T(8,128)(2,1)}, bf16[1,1,256,1024]{3,2,1,0:T(8,128)(2,1)S(1)}, u32[]{:S(2)}, u32[]{:S(2)}) collective-permute-start(bf16[1,1,256,1024]{3,2,1,0:T(8,128)(2,1)} %param.9), channel_id=1, source_target_pairs={{0,8},{4,12},{8,16},{12,20},{16,24},{20,28},{24,0},{28,4},{1,9},{5... | collective-permute-start | bytes 1572872 | tf_op jit(solution)/shard_map/ppermute | solution.py:103
  7.1 6.4 %collective-permute-done.2.got_ref = bf16[4,320,128]{2,1,0:T(8,128)(2,1)S(1)} collective-permute-done((bf16[4,320,128]{2,1,0:T(8,128)(2,1)S(1)}, bf16[4,320,128]{2,1,0:T(8,128)(2,1)S(1)}, u32[]{:S(2)}, u32[]{:S(2)}) %collective-permute-start.2) | collective-permute-done | bytes 327712 | tf_op jit(solution)/shard_map/ppermute | solution.py:57
  13.5 0.1 join.4
  13.6 2.5 %collective-permute-start.4 = (bf16[2,320,128]{2,1,0:T(8,128)(2,1)S(1)}, bf16[2,320,128]{2,1,0:T(8,128)(2,1)S(1)}, u32[]{:S(2)}, u32[]{:S(2)}) collective-permute-start(bf16[2,320,128]{2,1,0:T(8,128)(2,1)S(1)} %get-tuple-element.29), channel_id=1, source_target_pairs={{0,4},{4,0},{1,5},{5,1},{2,6},{6,2},{3,7},{7,3},{8,12},{12,8},{9,1... | collective-permute-start | bytes 491528 | tf_op jit(solution)/shard_map/ppermute | solution.py:57
  16.0 0.3 collective-permute-done.1
  16.3 0.0 copy-done.6
  16.3 0.0 copy-done.1
  16.3 0.8 %others.1.others_ref = bf16[256,1024]{1,0:T(8,128)(2,1)S(1)} custom-call(f32[1,1024]{1,0:T(1,128)S(1)} %copy-done.6, bf16[1024,1536]{1,0:T(8,128)(2,1)S(1)} %bitcast.30, bf16[256,1024]{1,0:T(8,128)(2,1)S(1)} %bitcast.33), custom_call_target="tpu_custom_call" | custom-call | flops 5750000128 | bytes 18450000 | tf_op jit(solution)/shard_map/others/pallas_call | solution.py:237
  17.1 0.6 %collective-permute-done.3.got_ref = bf16[4,192,128]{2,1,0:T(8,128)(2,1)S(1)} collective-permute-done((bf16[4,192,128]{2,1,0:T(8,128)(2,1)}, bf16[4,192,128]{2,1,0:T(8,128)(2,1)S(1)}, u32[]{:S(2)}, u32[]{:S(2)}) %collective-permute-start.3) | collective-permute-done | bytes 196640 | tf_op jit(solution)/shard_map/ppermute | solution.py:57
  17.8 1.5 %collective-permute-start.5 = (bf16[2,192,128]{2,1,0:T(8,128)(2,1)S(1)}, bf16[2,192,128]{2,1,0:T(8,128)(2,1)S(1)}, u32[]{:S(2)}, u32[]{:S(2)}) collective-permute-start(bf16[2,192,128]{2,1,0:T(8,128)(2,1)S(1)} %get-tuple-element.32), channel_id=1, source_target_pairs={{0,4},{4,0},{1,5},{5,1},{2,6},{6,2},{3,7},{7,3},{8,12},{12,8},{9,1... | collective-permute-start | bytes 294920 | tf_op jit(solution)/shard_map/ppermute | solution.py:57
  19.3 0.0 collective-permute-done
  19.3 0.0 copy-start.2
  19.3 0.0 copy-start.7
  19.3 1.1 %project.1.qkv_ref = bf16[256,1536]{1,0:T(8,128)(2,1)S(1)} custom-call(f32[1,1024]{1,0:T(1,128)S(1)} %copy-done.6, bf16[1024,1536]{1,0:T(8,128)(2,1)S(1)} %bitcast.31, bf16[256,1024]{1,0:T(8,128)(2,1)S(1)} %bitcast.34), custom_call_target="tpu_custom_call" | custom-call | flops 1264999936 | bytes 4059000 | tf_op jit(solution)/shard_map/project/pallas_call | solution.py:251
  20.4 0.3 %collective-permute-done.4.got_ref = bf16[2,320,128]{2,1,0:T(8,128)(2,1)S(1)} collective-permute-done((bf16[2,320,128]{2,1,0:T(8,128)(2,1)S(1)}, bf16[2,320,128]{2,1,0:T(8,128)(2,1)S(1)}, u32[]{:S(2)}, u32[]{:S(2)}) %collective-permute-start.4) | collective-permute-done | bytes 163872 | tf_op jit(solution)/shard_map/ppermute | solution.py:57
  20.8 2.7 %collective-permute-start.6 = (bf16[1,320,128]{2,1,0:T(8,128)(2,1)S(1)}, bf16[1,320,128]{2,1,0:T(8,128)(2,1)S(1)}, u32[]{:S(2)}, u32[]{:S(2)}) collective-permute-start(bf16[1,320,128]{2,1,0:T(8,128)(2,1)S(1)} %get-tuple-element.37), channel_id=1, source_target_pairs={{0,2},{1,3},{2,0},{3,1},{4,6},{5,7},{6,4},{7,5},{8,10},{9,11},{10,... | collective-permute-start | bytes 245768 | tf_op jit(solution)/shard_map/ppermute | solution.py:57
  23.5 0.0 collective-permute-done.5.got_ref
  23.5 2.7 %collective-permute-start.7 = (bf16[1,192,128]{2,1,0:T(8,128)(2,1)S(1)}, bf16[1,192,128]{2,1,0:T(8,128)(2,1)S(1)}, u32[]{:S(2)}, u32[]{:S(2)}) collective-permute-start(bf16[1,192,128]{2,1,0:T(8,128)(2,1)S(1)} %get-tuple-element.39), channel_id=1, source_target_pairs={{0,2},{1,3},{2,0},{3,1},{4,6},{5,7},{6,4},{7,5},{8,10},{9,11},{10,... | collective-permute-start | bytes 147464 | tf_op jit(solution)/shard_map/ppermute | solution.py:57
  26.2 0.0 copy-done.2
  26.2 0.0 copy-done.7
  26.2 0.0 copy-start.3
  26.2 0.0 copy-start.4
  26.2 0.0 copy-start.5
  26.2 2.5 %finish.1 = bf16[256,1024]{1,0:T(8,128)(2,1)} custom-call(bf16[256,1536]{1,0:T(8,128)(2,1)S(1)} %project.1.qkv_ref, s32[1,512]{1,0:T(1,128)S(1)} %bitcast.39, bf16[256,1024]{1,0:T(8,128)(2,1)S(1)} %others.1.others_ref, bf16[512,1024]{1,0:T(8,128)(2,1)S(1)} %bitcast.32, bf16[256,1024]{1,0:T(8,128)(2,1)S(1)} %bitcast.35), custom_call_target="tpu_custom_call" | custom-call | flops 3449999872 | bytes 11070000 | tf_op jit(solution)/shard_map/finish/pallas_call | solution.py:269
  28.7 0.0 collective-permute-done.6.refs_1_
  28.8 1.1 %collective-permute-done.7.refs_3_ = bf16[1,192,128]{2,1,0:T(8,128)(2,1)S(1)} collective-permute-done((bf16[1,192,128]{2,1,0:T(8,128)(2,1)S(1)}, bf16[1,192,128]{2,1,0:T(8,128)(2,1)S(1)}, u32[]{:S(2)}, u32[]{:S(2)}) %collective-permute-start.7) | collective-permute-done | bytes 49184 | tf_op jit(solution)/shard_map/ppermute | solution.py:57
  29.9 0.0 copy-done.3
  29.9 0.0 copy-done.4
  29.9 0.0 copy-done.5
  29.9 1.0 %adam.1 = (f32[512,128]{1,0:T(8,128)}, f32[512,128]{1,0:T(8,128)}, f32[512,128]{1,0:T(8,128)}) custom-call(f32[1,320,128]{2,1,0:T(8,128)S(1)} %get-tuple-element.41.refs_0_, bf16[1,320,128]{2,1,0:T(8,128)(2,1)S(1)} %collective-permute-done.6.refs_1_, f32[1,192,128]{2,1,0:T(8,128)S(1)} %get-tuple-element.43.refs_2_, ...), custom_call_target="tpu_custom_call" | custom-call | flops 1150000000 | bytes 3690000 | tf_op jit(solution)/shard_map/adam/pallas_call | solution.py:281
  (4 shorter events, 0.1 us)
Async XLA Ops:
  0.6 2.5 %copy-start = (f32[1,1,1,524288]{3,2,1,0:T(1,128)S(1)}, f32[1,1,1,524288]{3,2,1,0:T(1,128)}, u32[]{:S(2)}) copy-start(f32[1,1,1,524288]{3,2,1,0:T(1,128)} %param.14) | copy-start | bytes 6291460
  0.6 15.6 %collective-permute-start.1 = (bf16[1,1,256,1024]{3,2,1,0:T(8,128)(2,1)}, bf16[1,1,256,1024]{3,2,1,0:T(8,128)(2,1)S(1)}, u32[]{:S(2)}, u32[]{:S(2)}) collective-permute-start(bf16[1,1,256,1024]{3,2,1,0:T(8,128)(2,1)} %param.9), channel_id=1, source_target_pairs={{0,12},{4,8},{8,20},{12,16},{16,28},{20,24},{24,4},{28,0},{1,13},{... | collective-permute-start | bytes 1572872 | tf_op jit(solution)/shard_map/ppermute | solution.py:103
  3.2 13.1 %copy-start.6 = (f32[1,1024]{1,0:T(1,128)S(1)}, f32[1,1024]{1,0:T(1,128)}, u32[]{:S(2)}) copy-start(f32[1,1024]{1,0:T(1,128)} %gain_ref.3) | copy-start | bytes 12292
  3.2 10.3 %collective-permute-start.2 = (bf16[4,320,128]{2,1,0:T(8,128)(2,1)S(1)}, bf16[4,320,128]{2,1,0:T(8,128)(2,1)S(1)}, u32[]{:S(2)}, u32[]{:S(2)}) collective-permute-start(bf16[4,320,128]{2,1,0:T(8,128)(2,1)S(1)} %fusion), channel_id=1, source_target_pairs={{0,1},{1,0},{2,3},{3,2},{4,5},{5,4},{6,7},{7,6},{8,9},{9,8},{10,11... | collective-permute-start | bytes 983048 | tf_op jit(solution)/shard_map/ppermute | solution.py:57
  6.1 11.7 %collective-permute-start.3 = (bf16[4,192,128]{2,1,0:T(8,128)(2,1)}, bf16[4,192,128]{2,1,0:T(8,128)(2,1)S(1)}, u32[]{:S(2)}, u32[]{:S(2)}) collective-permute-start(bf16[4,192,128]{2,1,0:T(8,128)(2,1)} %fusion.1), channel_id=1, source_target_pairs={{0,1},{1,0},{2,3},{3,2},{4,5},{5,4},{6,7},{7,6},{8,9},{9,8},{10,11... | collective-permute-start | bytes 589832 | tf_op jit(solution)/shard_map/ppermute | solution.py:57
  6.1 10.2 %copy-start.1 = (bf16[1,1024,1536]{2,1,0:T(8,128)(2,1)S(1)}, bf16[1,1024,1536]{2,1,0:T(8,128)(2,1)}, u32[]{:S(2)}) copy-start(bf16[1,1024,1536]{2,1,0:T(8,128)(2,1)} %param.12) | copy-start | bytes 9437188
  6.2 13.1 %collective-permute-start = (bf16[1,1,256,1024]{3,2,1,0:T(8,128)(2,1)}, bf16[1,1,256,1024]{3,2,1,0:T(8,128)(2,1)S(1)}, u32[]{:S(2)}, u32[]{:S(2)}) collective-permute-start(bf16[1,1,256,1024]{3,2,1,0:T(8,128)(2,1)} %param.9), channel_id=1, source_target_pairs={{0,8},{4,12},{8,16},{12,20},{16,24},{20,28},{24,0},{28,4},{1,9},{5... | collective-permute-start | bytes 1572872 | tf_op jit(solution)/shard_map/ppermute | solution.py:103
  13.6 7.2 %collective-permute-start.4 = (bf16[2,320,128]{2,1,0:T(8,128)(2,1)S(1)}, bf16[2,320,128]{2,1,0:T(8,128)(2,1)S(1)}, u32[]{:S(2)}, u32[]{:S(2)}) collective-permute-start(bf16[2,320,128]{2,1,0:T(8,128)(2,1)S(1)} %get-tuple-element.29), channel_id=1, source_target_pairs={{0,4},{4,0},{1,5},{5,1},{2,6},{6,2},{3,7},{7,3},{8,12},{12,8},{9,1... | collective-permute-start | bytes 491528 | tf_op jit(solution)/shard_map/ppermute | solution.py:57
  17.8 5.7 %collective-permute-start.5 = (bf16[2,192,128]{2,1,0:T(8,128)(2,1)S(1)}, bf16[2,192,128]{2,1,0:T(8,128)(2,1)S(1)}, u32[]{:S(2)}, u32[]{:S(2)}) collective-permute-start(bf16[2,192,128]{2,1,0:T(8,128)(2,1)S(1)} %get-tuple-element.32), channel_id=1, source_target_pairs={{0,4},{4,0},{1,5},{5,1},{2,6},{6,2},{3,7},{7,3},{8,12},{12,8},{9,1... | collective-permute-start | bytes 294920 | tf_op jit(solution)/shard_map/ppermute | solution.py:57
  19.3 6.9 %copy-start.2 = (bf16[1,512,1024]{2,1,0:T(8,128)(2,1)S(1)}, bf16[1,512,1024]{2,1,0:T(8,128)(2,1)}, u32[]{:S(2)}) copy-start(bf16[1,512,1024]{2,1,0:T(8,128)(2,1)} %param.13) | copy-start | bytes 3145732
  19.3 6.9 %copy-start.7 = (s32[1,1,512]{2,1,0:T(1,128)S(1)}, s32[1,1,512]{2,1,0:T(1,128)}, u32[]{:S(2)}) copy-start(s32[1,1,512]{2,1,0:T(1,128)} %param.10) | copy-start | bytes 6148
  20.8 8.0 %collective-permute-start.6 = (bf16[1,320,128]{2,1,0:T(8,128)(2,1)S(1)}, bf16[1,320,128]{2,1,0:T(8,128)(2,1)S(1)}, u32[]{:S(2)}, u32[]{:S(2)}) collective-permute-start(bf16[1,320,128]{2,1,0:T(8,128)(2,1)S(1)} %get-tuple-element.37), channel_id=1, source_target_pairs={{0,2},{1,3},{2,0},{3,1},{4,6},{5,7},{6,4},{7,5},{8,10},{9,11},{10,... | collective-permute-start | bytes 245768 | tf_op jit(solution)/shard_map/ppermute | solution.py:57
  23.5 6.4 %collective-permute-start.7 = (bf16[1,192,128]{2,1,0:T(8,128)(2,1)S(1)}, bf16[1,192,128]{2,1,0:T(8,128)(2,1)S(1)}, u32[]{:S(2)}, u32[]{:S(2)}) collective-permute-start(bf16[1,192,128]{2,1,0:T(8,128)(2,1)S(1)} %get-tuple-element.39), channel_id=1, source_target_pairs={{0,2},{1,3},{2,0},{3,1},{4,6},{5,7},{6,4},{7,5},{8,10},{9,11},{10,... | collective-permute-start | bytes 147464 | tf_op jit(solution)/shard_map/ppermute | solution.py:57
  26.2 3.7 %copy-start.3 = (f32[1,65536]{1,0:T(1,128)S(1)}, f32[1,65536]{1,0:T(1,128)}, u32[]{:S(2)}) copy-start(f32[1,65536]{1,0:T(1,128)} %param.15) | copy-start | bytes 786436
  26.2 3.7 %copy-start.4 = (f32[1,65536]{1,0:T(1,128)S(1)}, f32[1,65536]{1,0:T(1,128)}, u32[]{:S(2)}) copy-start(f32[1,65536]{1,0:T(1,128)} %param.16) | copy-start | bytes 786436
  26.2 3.7 %copy-start.5 = (f32[1,65536]{1,0:T(1,128)S(1)}, f32[1,65536]{1,0:T(1,128)}, u32[]{:S(2)}) copy-start(f32[1,65536]{1,0:T(1,128)} %param.17) | copy-start | bytes 786436
